TPU v7x, 32 devices: a whole 2x2x4 slice. The times are simulated.
32 devices in a mesh: fsdp: 8 (over y, x, core), seq: 4 (over z).
Axes of the slice: x: 2, y: 2, z: 4, core: 2. Of those that a mesh axis runs over, the one named last changes fastest.
Arguments:
- tokens: bfloat16 [8, 512, 2048], P('fsdp', 'seq'), may hold values from -13 to 13
- adjacency: int32 [8, 8], replicated, may hold values from 0 to 1, as said below
- w_query: bfloat16 [2048, 1024], P(('fsdp', 'seq')), may hold values from -1 to 1
- w_key: bfloat16 [2048, 256], P(('fsdp', 'seq')), may hold values from -1 to 1
- value_weight: bfloat16 [2048, 256], P(('fsdp', 'seq')), may hold values from -0.125 to 0.125
- grad_attn: bfloat16 [8, 512, 1024], P('fsdp', 'seq'), may hold values from -6 to 6
Outputs:
- attended: bfloat16 [8, 512, 1024], P('fsdp', 'seq')
- grad_tokens: bfloat16 [8, 512, 2048], P('fsdp', 'seq')
- grad_wq: bfloat16 [2048, 1024], P(('fsdp', 'seq'))
- grad_wk: bfloat16 [2048, 256], P(('fsdp', 'seq'))
- grad_wv: bfloat16 [2048, 256], P(('fsdp', 'seq'))
Inputs may be any that keep to these rules, and one draw needn't show every extreme that they name: `adjacency`: symmetric, and every diagonal entry is 1.
All inputs are finite; a program needn't handle non-finite values.
Results may differ from a plain program's by a relative error of at most 0.011.
The roundings to bfloat16 on the way count: a program that leaves them out, or rounds other values in their place, can miss the bound.
Values may be sent and summed in bfloat16 or wider, within the bound.
No kernel may reach another device: no remote copies, remote signals or barrier semaphores. Data moves between devices by JAX's collectives and lax.ppermute only.
A program may use at most 128 MiB of HBM per device.

v0:
```python
import math

import jax
import jax.numpy as jnp
from jax import lax
from jax.sharding import PartitionSpec as P

KEY_VALUE_HEADS = 4
HEAD_SIZE = 64
BLK = 64


def attend_group(query, keys, values, grad_out, allowed):
    scores = jnp.einsum("qhd,kd->hqk", query, keys, preferred_element_type=jnp.float32) * 0.125
    scores = jnp.where(allowed[None], scores, jnp.float32(-1e30))
    highest = jnp.max(scores, axis=-1, keepdims=True)
    expo = jnp.exp(scores - highest)
    probs = expo / jnp.sum(expo, axis=-1, keepdims=True)
    probs_low = probs.astype(jnp.bfloat16)
    output = jnp.einsum("hqk,kd->qhd", probs_low, values, preferred_element_type=jnp.float32)
    grad_probs = jnp.einsum("qhd,kd->hqk", grad_out, values, preferred_element_type=jnp.float32)
    inner = jnp.sum(probs * grad_probs, axis=-1, keepdims=True)
    grad_scores = (probs * (grad_probs - inner) * 0.125).astype(jnp.bfloat16)
    grad_query = jnp.einsum("hqk,kd->qhd", grad_scores, keys, preferred_element_type=jnp.float32)
    grad_keys = jnp.einsum("hqk,qhd->kd", grad_scores, query, preferred_element_type=jnp.float32)
    grad_values = jnp.einsum("hqk,qhd->kd", probs_low, grad_out, preferred_element_type=jnp.float32)
    return (output, grad_query, grad_keys, grad_values)


def body(tokens, adjacency, w_query, w_key, value_weight, grad_attn):
    local_tokens = tokens[0]
    local_grad = grad_attn[0]
    rows_here = local_tokens.shape[0]
    full_q, full_k, full_v = (
        lax.all_gather(w_query, ("fsdp", "seq"), axis=0, tiled=True),
        lax.all_gather(w_key, ("fsdp", "seq"), axis=0, tiled=True),
        lax.all_gather(value_weight, ("fsdp", "seq"), axis=0, tiled=True),
    )
    query = jnp.dot(local_tokens, full_q, preferred_element_type=jnp.float32).astype(jnp.bfloat16)
    keys = jnp.dot(local_tokens, full_k, preferred_element_type=jnp.float32).astype(jnp.bfloat16)
    values = jnp.dot(local_tokens, full_v, preferred_element_type=jnp.float32).astype(jnp.bfloat16)
    all_keys, all_values = (
        lax.all_gather(keys, "seq", axis=0, tiled=True),
        lax.all_gather(values, "seq", axis=0, tiled=True),
    )
    blocks_here = rows_here // BLK
    position = lax.axis_index("seq")
    mask_rows = lax.dynamic_slice_in_dim(adjacency, position * blocks_here, blocks_here, 0)
    allowed = jnp.repeat(jnp.repeat(mask_rows, BLK, axis=0), BLK, axis=1) > 0
    group_size = w_query.shape[1] // w_key.shape[1]
    outs_list, dq_list, dk_list, dv_list = ([], [], [], [])
    for head_grouping in range(KEY_VALUE_HEADS):
        low = head_grouping * group_size * HEAD_SIZE
        high = low + group_size * HEAD_SIZE
        group_query = query[:, low:high].reshape(rows_here, group_size, HEAD_SIZE)
        group_grad = local_grad[:, low:high].reshape(rows_here, group_size, HEAD_SIZE)
        group_keys = all_keys[:, head_grouping * HEAD_SIZE : (head_grouping + 1) * HEAD_SIZE]
        group_values = all_values[:, head_grouping * HEAD_SIZE : (head_grouping + 1) * HEAD_SIZE]
        output, grad_query, grad_keys, grad_values = attend_group(
            group_query, group_keys, group_values, group_grad, allowed
        )
        outs_list.append(output.reshape(rows_here, group_size * HEAD_SIZE))
        dq_list.append(grad_query.reshape(rows_here, group_size * HEAD_SIZE))
        dk_list.append(grad_keys)
        dv_list.append(grad_values)
    attended = jnp.concatenate(outs_list, axis=1).astype(jnp.bfloat16)
    grad_query = jnp.concatenate(dq_list, axis=1).astype(jnp.bfloat16)
    key_terms = jnp.concatenate(dk_list, axis=1)
    value_terms = jnp.concatenate(dv_list, axis=1)
    summed_keys, summed_values = (
        lax.psum_scatter(key_terms, "seq", scatter_dimension=0, tiled=True),
        lax.psum_scatter(value_terms, "seq", scatter_dimension=0, tiled=True),
    )
    grad_keys = summed_keys.astype(jnp.bfloat16)
    grad_values = summed_values.astype(jnp.bfloat16)
    grad_in = jnp.dot(grad_query, full_q.T, preferred_element_type=jnp.float32)
    grad_in = grad_in + jnp.dot(grad_keys, full_k.T, preferred_element_type=jnp.float32)
    grad_in = grad_in + jnp.dot(grad_values, full_v.T, preferred_element_type=jnp.float32)
    joined = jnp.concatenate([grad_query, grad_keys, grad_values], axis=1)
    total_tokens = all_keys.shape[0] * lax.axis_size("fsdp")
    factor = 1.0 / math.sqrt(total_tokens)
    summed = lax.psum_scatter(
        jnp.dot(local_tokens.T, joined, preferred_element_type=jnp.float32) * factor,
        ("fsdp", "seq"),
        scatter_dimension=0,
        tiled=True,
    )
    width_q = w_query.shape[1]
    key_width = w_key.shape[1]
    grad_wq = summed[:, :width_q].astype(jnp.bfloat16)
    grad_wk = summed[:, width_q : width_q + key_width].astype(jnp.bfloat16)
    grad_wv = summed[:, width_q + key_width :].astype(jnp.bfloat16)
    return (attended[None], grad_in.astype(jnp.bfloat16)[None], grad_wq, grad_wk, grad_wv)


def solution(mesh):
    return jax.shard_map(
        body,
        mesh=mesh,
        in_specs=(
            P("fsdp", "seq", None),
            P(),
            P(("fsdp", "seq"), None),
            P(("fsdp", "seq"), None),
            P(("fsdp", "seq"), None),
            P("fsdp", "seq", None),
        ),
        out_specs=(
            P("fsdp", "seq", None),
            P("fsdp", "seq", None),
            P(("fsdp", "seq"), None),
            P(("fsdp", "seq"), None),
            P(("fsdp", "seq"), None),
        ),
        check_vma=False,
    )
```

profile of v0, /device:TPU:0, one launch (start us, length us, event | category | flops | bytes accessed | tf_op | source)
XLA Modules:
  0.0 444.3 jit_solution(9299213943364896199)
XLA Ops:
  10.4 1.0 fusion.124
  11.9 55.6 %all-gather.6.cloned.1.call-done = bf16[2048,256]{1,0:T(8,128)(2,1)} async-done(((bf16[64,256]{1,0:T(8,128)(2,1)}), bf16[2048,256]{1,0:T(8,128)(2,1)}) %all-gather.6.cloned.1.call-update) | async-done | bytes 1048592 | tf_op jit(solution)/shard_map/all_gather | solution.py:36
  67.5 1.5 convolution_convert_fusion.9
  69.0 13.9 %all_gather.18 = bf16[512,256]{1,0:T(8,128)(2,1)S(1)} all-gather(bf16[128,256]{1,0:T(8,128)(2,1)S(1)} %convolution_convert_fusion.9), channel_id=1, replica_groups=mesh['fsdp'=8,'seq'=4] {'seq'}, dimensions={0}, use_global_device_ids=true | all-gather | bytes 327680 | tf_op jit(solution)/shard_map/all_gather | solution.py:43
  82.9 40.3 %all-gather.4.cloned.1.call-done = bf16[2048,256]{1,0:T(8,128)(2,1)} async-done(((bf16[64,256]{1,0:T(8,128)(2,1)}), bf16[2048,256]{1,0:T(8,128)(2,1)}) %all-gather.4.cloned.1.call-update) | async-done | bytes 1048592 | tf_op jit(solution)/shard_map/all_gather | solution.py:37
  123.2 1.5 convolution_convert_fusion.10
  124.8 14.0 %all_gather.16 = bf16[512,256]{1,0:T(8,128)(2,1)S(1)} all-gather(bf16[128,256]{1,0:T(8,128)(2,1)S(1)} %convolution_convert_fusion.10), channel_id=1, replica_groups=mesh['fsdp'=8,'seq'=4] {'seq'}, dimensions={0}, use_global_device_ids=true | all-gather | bytes 327680 | tf_op jit(solution)/shard_map/all_gather | solution.py:44
  138.8 1.4 convolution_bitcast_fusion.2
  140.7 1.3 convolution_bitcast_fusion.3
  142.0 45.3 %all-gather.8.cloned.1.call-done = bf16[2048,1024]{1,0:T(8,128)(2,1)} async-done(((bf16[64,1024]{1,0:T(8,128)(2,1)}), bf16[2048,1024]{1,0:T(8,128)(2,1)}) %all-gather.8.cloned.1.call-update) | async-done | bytes 4194320 | tf_op jit(solution)/shard_map/all_gather | solution.py:35
  187.3 2.9 convolution_convert_fusion
  190.9 1.6 copy.112
  192.5 1.6 copy.124
  195.5 2.3 fusion.128
  197.8 2.2 fusion.127
  200.1 2.3 fusion.126
  202.4 1.4 fusion.129
  203.8 2.8 convolution_bitcast_fusion.10
  206.7 2.7 convolution_bitcast_fusion.9
  209.4 2.7 convolution_bitcast_fusion.8
  212.0 3.5 convolution_bitcast_fusion.11
  215.5 1.9 pad_maximum_fusion
  217.5 1.6 convolution_bitcast_fusion.6
  219.1 2.2 convolution_bitcast_fusion.5
  221.3 2.3 convolution_bitcast_fusion.4
  223.7 2.2 convolution_bitcast_fusion.7
  225.9 1.8 pad_maximum_fusion.1
  227.7 2.8 convolution_convert_fusion.3
  230.4 2.7 convolution_convert_fusion.4
  233.4 2.0 convolution_convert_fusion.2
  235.4 2.1 convolution_convert_fusion.1
  237.8 0.9 convert_dynamic-update-slice_fusion.1
  238.7 21.8 %reduce-scatter.8.cloned.1.call-done = f32[128,256]{0,1:T(8,128)} async-done(((f32[512,256]{0,1:T(8,128)}), f32[128,256]{0,1:T(8,128)}) %reduce-scatter.8.cloned.1.call-update) | async-done | bytes 131088 | tf_op jit(solution)/shard_map/reduce_scatter | solution.py:72
  260.4 0.9 convert_dynamic-update-slice_fusion
  261.3 6.3 %multiply_bitcast_fusion = f32[2048,1536]{0,1:T(8,128)} fusion(bf16[128,1536]{0,1:T(8,128)(2,1)S(1)} %convert_dynamic-update-slice_fusion, bf16[1,128,2048]{2,1,0:T(8,128)(2,1)S(1)} %copy-done), kind=kOutput, calls=%fused_computation.8 | convolution fusion | flops 808452096 | bytes 13500416 | tf_op jit(solution)/shard_map/dot_general | solution.py:83
  267.6 12.6 %copy.207 = f32[2048,1536]{1,0:T(8,128)} copy(f32[2048,1536]{0,1:T(8,128)} %multiply_bitcast_fusion) | data formatting | bytes 25165824
  280.2 0.8 copy-done.12
  281.0 1.7 convolution_convert_fusion.7
  282.9 1.6 convolution_convert_fusion.6
  284.6 2.4 convolution_convert_fusion.5
  287.0 1.7 copy.131
  288.7 2.2 convolution_convert_fusion.8
  290.9 0.9 copy.128
  291.8 1.7 pad_maximum_fusion.2
  294.6 2.3 fusion.10
  296.9 137.1 %reduce-scatter.10.cloned.1.call-done = f32[64,1536]{1,0:T(8,128)} async-done(((f32[2048,1536]{1,0:T(8,128)}), f32[64,1536]{1,0:T(8,128)}) %reduce-scatter.10.cloned.1.call-update) | async-done | bytes 393232
  434.0 1.2 copy.208
  435.3 0.8 copy.156
  (64 shorter events, 9.6 us)
Async XLA Ops:
  7.2 60.3 %copy-start = (bf16[1,128,2048]{2,1,0:T(8,128)(2,1)S(1)}, bf16[1,128,2048]{2,1,0:T(8,128)(2,1)}, u32[]{:S(2)}) copy-start(bf16[1,128,2048]{2,1,0:T(8,128)(2,1)} %param.6) | copy-start | bytes 1572868
  7.2 60.3 %all-gather.6.cloned.1.call-start = ((), (), s32[]{:S(2)}) async-start(), calls=%async_computation.4 | async-start | bytes 1081344 | tf_op jit(solution)/shard_map/all_gather | solution.py:36
  7.9 115.3 %all-gather.4.cloned.1.call-start = ((), (), s32[]{:S(2)}) async-start(), calls=%async_computation.3 | async-start | bytes 1081344 | tf_op jit(solution)/shard_map/all_gather | solution.py:37
  8.7 178.7 %all-gather.8.cloned.1.call-start = ((), (), s32[]{:S(2)}) async-start(), calls=%async_computation.5 | async-start | bytes 4325376 | tf_op jit(solution)/shard_map/all_gather | solution.py:35
  9.4 228.4 %reduce-scatter.6.cloned.1.call-start = ((), (), s32[]{:S(2)}) async-start(), calls=%async_computation.6 | async-start | bytes 655360 | tf_op jit(solution)/shard_map/reduce_scatter | solution.py:71
  82.9 147.5 %copy-start.6 = (bf16[512,256]{1,0:T(8,128)(2,1)}, bf16[512,256]{1,0:T(8,128)(2,1)S(1)}, u32[]{:S(2)}) copy-start(bf16[512,256]{1,0:T(8,128)(2,1)S(1)} %all_gather.18) | copy-start | bytes 786436
  194.8 7.6 %copy-start.8 = (bf16[128,256]{0,1:T(8,128)(2,1)S(1)}, bf16[128,256]{0,1:T(8,128)(2,1)}, u32[]{:S(2)}) copy-start(bf16[128,256]{0,1:T(8,128)(2,1)} %copy.112) | copy-start | bytes 196612
  195.5 8.3 %copy-start.9 = (pred[128,8,64]{0,2,1:T(8,128)(4,1)}, pred[128,8,64]{0,2,1:T(8,128)(4,1)S(1)}, u32[]{:S(2)}) copy-start(pred[128,8,64]{0,2,1:T(8,128)(4,1)S(1)} %broadcast_in_dim.51) | copy-start | bytes 196612
  217.4 43.0 %reduce-scatter.8.cloned.1.call-start = ((), (), s32[]{:S(2)}) async-start(), calls=%async_computation.7 | async-start | bytes 655360 | tf_op jit(solution)/shard_map/reduce_scatter | solution.py:72
  221.3 4.6 %copy-start.7 = (f32[512,64]{0,1:T(8,128)S(1)}, f32[512,64]{0,1:T(8,128)}, u32[]{:S(2)}) copy-start(f32[512,64]{0,1:T(8,128)} %convolution_bitcast_fusion.5) | copy-start | bytes 393220
  233.1 200.9 %reduce-scatter.10.cloned.1.call-start = ((), (), s32[]{:S(2)}) async-start(), calls=%async_computation.8 | async-start | bytes 12976128
  280.2 0.8 copy-start.12
  281.0 1.8 copy-start.11
  281.0 3.5 copy-start.10
  284.5 9.0 %copy-start.3 = (bf16[2048,256]{1,0:T(8,128)(2,1)S(1)}, bf16[2048,256]{1,0:T(8,128)(2,1)}, u32[]{:S(2)}) copy-start(bf16[2048,256]{1,0:T(8,128)(2,1)} %all-gather.4.cloned.1.call-done) | copy-start | bytes 3145732
  284.6 9.0 %copy-start.5 = (f32[128,256]{0,1:T(8,128)S(1)}, f32[128,256]{0,1:T(8,128)}, u32[]{:S(2)}) copy-start(f32[128,256]{0,1:T(8,128)} %reduce-scatter.8.cloned.1.call-done) | copy-start | bytes 393220
  287.0 7.1 %copy-start.2 = (bf16[2048,256]{1,0:T(8,128)(2,1)S(1)}, bf16[2048,256]{1,0:T(8,128)(2,1)}, u32[]{:S(2)}) copy-start(bf16[2048,256]{1,0:T(8,128)(2,1)} %all-gather.6.cloned.1.call-done) | copy-start | bytes 3145732
  287.0 7.1 %copy-start.4 = (f32[128,256]{0,1:T(8,128)S(1)}, f32[128,256]{0,1:T(8,128)}, u32[]{:S(2)}) copy-start(f32[128,256]{0,1:T(8,128)} %reduce-scatter.6.cloned.1.call-done) | copy-start | bytes 393220
  291.8 2.7 copy-start.1
Sparse Core Ops, SparseCore 0:
  11.0 56.4 all-gather.5
  70.5 52.7 all-gather.3
  126.2 61.0 all-gather.7
  217.5 20.1 reduce-scatter.5
  240.4 19.9 reduce-scatter.7
  280.3 153.6 reduce-scatter.9
where the time goes:
time: 446 us; the launch traced here: 444 us
  waiting for transfers between devices  302 us (68%)
  matrix products  64.5 us (14%)
  blocking collectives  27.9 us (6%)
  local copies, waits for them, and re-layouts  26.7 us (6%)
  between operations  14.4 us (3%)
  other arithmetic  7.93 us (2%)
    unnamed x7, waiting for transfers between devices  139 us
    all_gather x1, waiting for transfers between devices, body(): lax.all_gather(w_key, ('fsdp', 'seq'), axis=0, tiled=True)  55.6 us
    all_gather x1, waiting for transfers between devices, body(): lax.all_gather(w_query, ('fsdp', 'seq'), axis=0, tiled=True)  45.3 us
    all_gather x1, waiting for transfers between devices, body(): lax.all_gather(value_weight, ('fsdp', 'seq'), axis=0, tiled=True)  40.3 us
    reduce_scatter x1, waiting for transfers between devices, body(): lax.psum_scatter(value_terms, 'seq', scatter_dimension=0, tiled=True)  21.8 us
    unnamed x35, local copies, waits for them, and re-layouts  16.9 us
    all_gather x1, blocking collectives, body(): lax.all_gather(values, 'seq', axis=0, tiled=True)  14 us
    all_gather x1, blocking collectives, body(): lax.all_gather(keys, 'seq', axis=0, tiled=True)  13.9 us
  transfers between devices with their start and end apart: 6, of which 6 were waited for; matrix products, arithmetic and copies ran while one was open for 10% of the time, Pallas kernels for 0%

commit v1 on v0

v1 whole, which is shorter than its diff:
```python
import functools
import math

import jax
import jax.numpy as jnp
from jax import lax
from jax.experimental import pallas as pl
from jax.experimental.pallas import tpu as pltpu
from jax.sharding import PartitionSpec as P

KEY_VALUE_HEADS = 4
HEAD_SIZE = 64
BLK = 64
F32 = jnp.float32
BF16 = jnp.bfloat16
VMEM_LIMIT = 48 * 1024 * 1024


def attend_group(query, keys, values, grad_out, allowed):
    scores = jnp.einsum("qhd,kd->hqk", query, keys, preferred_element_type=F32) * 0.125
    scores = jnp.where(allowed[None], scores, jnp.float32(-1e30))
    highest = jnp.max(scores, axis=-1, keepdims=True)
    expo = jnp.exp(scores - highest)
    probs = expo / jnp.sum(expo, axis=-1, keepdims=True)
    probs_low = probs.astype(BF16)
    output = jnp.einsum("hqk,kd->qhd", probs_low, values, preferred_element_type=F32)
    grad_probs = jnp.einsum("qhd,kd->hqk", grad_out, values, preferred_element_type=F32)
    inner = jnp.sum(probs * grad_probs, axis=-1, keepdims=True)
    grad_scores = (probs * (grad_probs - inner) * 0.125).astype(BF16)
    grad_query = jnp.einsum("hqk,kd->qhd", grad_scores, keys, preferred_element_type=F32)
    grad_keys = jnp.einsum("hqk,qhd->kd", grad_scores, query, preferred_element_type=F32)
    grad_values = jnp.einsum("hqk,qhd->kd", probs_low, grad_out, preferred_element_type=F32)
    return (output, grad_query, grad_keys, grad_values)


def general_body(tokens, adjacency, w_query, w_key, value_weight, grad_attn):
    local_tokens = tokens[0]
    local_grad = grad_attn[0]
    rows_here = local_tokens.shape[0]
    full_q, full_k, full_v = (
        lax.all_gather(w_query, ("fsdp", "seq"), axis=0, tiled=True),
        lax.all_gather(w_key, ("fsdp", "seq"), axis=0, tiled=True),
        lax.all_gather(value_weight, ("fsdp", "seq"), axis=0, tiled=True),
    )
    query = jnp.dot(local_tokens, full_q, preferred_element_type=F32).astype(BF16)
    keys = jnp.dot(local_tokens, full_k, preferred_element_type=F32).astype(BF16)
    values = jnp.dot(local_tokens, full_v, preferred_element_type=F32).astype(BF16)
    all_keys, all_values = (
        lax.all_gather(keys, "seq", axis=0, tiled=True),
        lax.all_gather(values, "seq", axis=0, tiled=True),
    )
    blocks_here = rows_here // BLK
    position = lax.axis_index("seq")
    mask_rows = lax.dynamic_slice_in_dim(adjacency, position * blocks_here, blocks_here, 0)
    allowed = jnp.repeat(jnp.repeat(mask_rows, BLK, axis=0), BLK, axis=1) > 0
    group_size = w_query.shape[1] // w_key.shape[1]
    outs_list, dq_list, dk_list, dv_list = ([], [], [], [])
    for head_grouping in range(KEY_VALUE_HEADS):
        low = head_grouping * group_size * HEAD_SIZE
        high = low + group_size * HEAD_SIZE
        group_query = query[:, low:high].reshape(rows_here, group_size, HEAD_SIZE)
        group_grad = local_grad[:, low:high].reshape(rows_here, group_size, HEAD_SIZE)
        group_keys = all_keys[:, head_grouping * HEAD_SIZE : (head_grouping + 1) * HEAD_SIZE]
        group_values = all_values[:, head_grouping * HEAD_SIZE : (head_grouping + 1) * HEAD_SIZE]
        output, grad_query, grad_keys, grad_values = attend_group(
            group_query, group_keys, group_values, group_grad, allowed
        )
        outs_list.append(output.reshape(rows_here, group_size * HEAD_SIZE))
        dq_list.append(grad_query.reshape(rows_here, group_size * HEAD_SIZE))
        dk_list.append(grad_keys)
        dv_list.append(grad_values)
    attended = jnp.concatenate(outs_list, axis=1).astype(BF16)
    grad_query = jnp.concatenate(dq_list, axis=1).astype(BF16)
    key_terms = jnp.concatenate(dk_list, axis=1)
    value_terms = jnp.concatenate(dv_list, axis=1)
    summed_keys, summed_values = (
        lax.psum_scatter(key_terms, "seq", scatter_dimension=0, tiled=True),
        lax.psum_scatter(value_terms, "seq", scatter_dimension=0, tiled=True),
    )
    grad_keys = summed_keys.astype(BF16)
    grad_values = summed_values.astype(BF16)
    grad_in = jnp.dot(grad_query, full_q.T, preferred_element_type=F32)
    grad_in = grad_in + jnp.dot(grad_keys, full_k.T, preferred_element_type=F32)
    grad_in = grad_in + jnp.dot(grad_values, full_v.T, preferred_element_type=F32)
    joined = jnp.concatenate([grad_query, grad_keys, grad_values], axis=1)
    total_tokens = all_keys.shape[0] * lax.axis_size("fsdp")
    factor = 1.0 / math.sqrt(total_tokens)
    summed = lax.psum_scatter(
        jnp.dot(local_tokens.T, joined, preferred_element_type=F32) * factor,
        ("fsdp", "seq"),
        scatter_dimension=0,
        tiled=True,
    )
    width_q = w_query.shape[1]
    key_width = w_key.shape[1]
    grad_wq = summed[:, :width_q].astype(BF16)
    grad_wk = summed[:, width_q : width_q + key_width].astype(BF16)
    grad_wv = summed[:, width_q + key_width :].astype(BF16)
    return (attended[None], grad_in.astype(BF16)[None], grad_wq, grad_wk, grad_wv)


def swap(x, axis, j):
    n = lax.axis_size(axis)
    return lax.ppermute(x, axis, [(i, i ^ j) for i in range(n)])


def vmem_call(kernel, out_shape, scratch_shapes=(), smem=0, total=0):
    def call(*args):
        in_specs = [
            pl.BlockSpec(memory_space=pltpu.SMEM if i < smem else pltpu.VMEM)
            for i in range(len(args))
        ]
        outs = jax.tree.map(lambda _: pl.BlockSpec(memory_space=pltpu.VMEM), out_shape)
        return pl.pallas_call(
            kernel,
            out_shape=out_shape,
            in_specs=in_specs,
            out_specs=outs,
            scratch_shapes=scratch_shapes,
            compiler_params=pltpu.CompilerParams(vmem_limit_bytes=VMEM_LIMIT),
            cost_estimate=pl.CostEstimate(flops=total, bytes_accessed=4 << 20, transcendentals=0),
        )(*args)

    return call


def shape(*dims, dtype=BF16):
    return jax.ShapeDtypeStruct(dims, dtype)


def group_columns(ref, group, width):
    if width % 128 == 0:
        return ref[:, pl.ds(pl.multiple_of(group * width, width), width)]
    per = 128 // width
    wide = ref[:, pl.ds(pl.multiple_of((group // per) * 128, 128), 128)]
    part = wide[:, :width]
    for i in range(1, per):
        part = jnp.where(group % per == i, wide[:, i * width : (i + 1) * width], part)
    return part


def pack_kernel(place_ref, wq_ref, wk_ref, wv_ref, grad_ref, *outs):
    s = place_ref[1]
    w_all, w_outs, g_outs = outs[0], outs[1:4], outs[4:8]
    wide = wq_ref.shape[1] // 4
    narrow = wk_ref.shape[1] // 4
    for j in range(4):
        g = s ^ j
        q = group_columns(wq_ref, g, wide)
        k = group_columns(wk_ref, g, narrow)
        v = group_columns(wv_ref, g, narrow)
        row = jnp.concatenate([q, k, v], axis=1)
        w_all[j] = row
        if j > 0:
            w_outs[j - 1][...] = row
        g_outs[j][...] = group_columns(grad_ref, g, wide)


def attend_kernel(place_ref, adjacency_ref, *refs):
    f, s = place_ref[0], place_ref[1]
    x_refs, w_refs, g_refs = refs[0:4], refs[4:12], refs[12:16]
    att_refs, d_refs = refs[16:20], refs[20:24]
    w_scr, q_scr, gt_scr = refs[24:27]
    rows = x_refs[0].shape[0]
    length = 4 * rows
    depth = w_refs[0].shape[1]
    span = 4 * depth
    hs = HEAD_SIZE
    per = g_refs[0].shape[1] // hs
    wide = per * hs

    acc = None
    for jf in range(8):
        for l in range(4):
            w_scr[jf, pl.ds(pl.multiple_of((s ^ l) * depth, depth), depth), :] = w_refs[jf][l]
    for jf in range(8):
        cols = pl.ds(pl.multiple_of((f ^ jf) * span, span), span)
        x = jnp.concatenate([r[:, cols] for r in x_refs], axis=0)
        part = jnp.dot(x, w_scr[jf], preferred_element_type=F32)
        acc = part if acc is None else acc + part
    low = acc.astype(BF16)
    q_scr[...] = low[:, :wide]
    keys = low[:, wide : wide + hs]
    values = low[:, wide + hs : wide + 2 * hs]
    keys_t = keys.astype(F32).T.astype(BF16)
    values_t = values.astype(F32).T.astype(BF16)
    for j in range(4):
        gt_scr[j * rows : (j + 1) * rows, :] = g_refs[j][...]

    blocks = length // BLK
    half = rows // BLK

    def absolute(b):
        return (s ^ (b // half)) * half + b % half

    row_block = lax.broadcasted_iota(jnp.int32, (length, 128), 0) // BLK
    lane_block = lax.broadcasted_iota(jnp.int32, (length, 128), 1) // BLK

    tile = 128
    grad_keys = jnp.zeros((length, hs), F32)
    grad_values = jnp.zeros((length, hs), F32)
    out_t = [[None] * per for _ in range(length // tile)]
    dq_t = [[None] * per for _ in range(length // tile)]
    for t in range(length // tile):
        linked = jnp.zeros((length, tile), jnp.int32)
        for b in range(blocks):
            for c in range(tile // BLK):
                a = adjacency_ref[absolute(b), absolute(t * (tile // BLK) + c)]
                linked = jnp.where((row_block == b) & (lane_block == c), a, linked)
        bias = jnp.where(linked > 0, 0.0, -1e30).astype(F32)
        for h in range(per):
            q = q_scr[t * tile : (t + 1) * tile, h * hs : (h + 1) * hs]
            g = gt_scr[t * tile : (t + 1) * tile, h * hs : (h + 1) * hs]
            q8 = (q.astype(F32) * 0.125).astype(BF16)
            last = (((1,), (1,)), ((), ()))
            sc = lax.dot_general(keys, q8, last, preferred_element_type=F32) + bias
            top = jnp.max(sc, axis=0, keepdims=True)
            e = jnp.exp(sc - top)
            p = e * (1.0 / jnp.sum(e, axis=0, keepdims=True))
            p_low = p.astype(BF16)
            dp = lax.dot_general(values, g, last, preferred_element_type=F32)
            inner = jnp.sum(p * dp, axis=0, keepdims=True)
            ds = (p * (dp - inner)).astype(BF16)
            out_t[t][h] = jnp.dot(values_t, p_low, preferred_element_type=F32)
            dq_t[t][h] = jnp.dot(keys_t, ds, preferred_element_type=F32) * 0.125
            grad_keys = grad_keys + jnp.dot(ds, q8, preferred_element_type=F32)
            grad_values = grad_values + jnp.dot(p_low, g, preferred_element_type=F32)
    dkv = jnp.concatenate([grad_keys, grad_values], axis=1).astype(BF16)
    for j in range(4):
        att_refs[j][...] = jnp.concatenate(out_t[j], axis=0).T.astype(BF16)
        dq = jnp.concatenate(dq_t[j], axis=0).T.astype(BF16)
        block = jnp.concatenate([dq, dkv[j * rows : (j + 1) * rows]], axis=1)
        d_refs[j][:rows, :] = block
        d_refs[j ^ 1][rows:, :] = block


def weight_grad_kernel(parity, place_ref, x0, x1, x2, x3, d0_ref, d2_ref, out_ref):
    f, s = place_ref[0], place_ref[1]
    depth = out_ref.shape[2]
    span = 4 * depth
    d = jnp.concatenate([d0_ref[...], d2_ref[...]], axis=0)
    for i in range(4):
        cols = pl.ds(pl.multiple_of((f ^ (2 * i + parity)) * span, span), span)
        x = jnp.concatenate([r[:, cols] for r in (x0, x1, x2, x3)], axis=0)
        part = lax.dot_general(x, d, (((0,), (0,)), ((), ())), preferred_element_type=F32)
        for k in range(4):
            out_ref[i, s ^ k] = part[k * depth : (k + 1) * depth]


def token_grad_kernel(place_ref, d0, d1, d2, d3, *refs):
    f, s = place_ref[0], place_ref[1]
    w_refs, own_ref, send_ref = refs[:8], refs[8], refs[9]
    rows = own_ref.shape[0]
    depth = w_refs[0].shape[2]
    d = [r[...] for r in (d0, d1, d2, d3)]
    last = (((1,), (1,)), ((), ()))
    for jf in range(8):
        halves = []
        for l in range(2):
            total = None
            for j in range(4):
                part = lax.dot_general(
                    d[j], w_refs[jf][l, j ^ (2 * l)], last, preferred_element_type=F32
                )
                total = part if total is None else total + part
            halves.append(total)
        swapped = s // 2 == 1
        first = jnp.where(swapped, halves[1], halves[0])
        second = jnp.where(swapped, halves[0], halves[1])
        both = jnp.concatenate([first, second], axis=1).astype(BF16)
        cols = pl.ds(pl.multiple_of((f ^ jf) * 2 * depth, 2 * depth), 2 * depth)
        own_ref[:, cols] = both[:rows]
        send_ref[:, cols] = both[rows:]


def token_join_kernel(place_ref, own_ref, got_ref, out_ref):
    s = place_ref[1]
    odd = s % 2 == 1
    depth = own_ref.shape[1] // 16
    for b in range(8):
        cols = slice(b * 2 * depth, (b + 1) * 2 * depth)
        own, got = own_ref[:, cols], got_ref[:, cols]
        even = jnp.where(odd, got, own)
        other = jnp.where(odd, own, got)
        out_ref[:, b * 4 * depth : (b + 1) * 4 * depth] = jnp.concatenate(
            [even[:, :depth], other[:, :depth], even[:, depth:], other[:, depth:]], axis=1
        )


def attended_join_kernel(place_ref, a0, a1, a2, a3, out_ref):
    s = place_ref[1]
    wide = a0.shape[1]
    for j, a in enumerate((a0, a1, a2, a3)):
        out_ref[:, pl.ds(pl.multiple_of((s ^ j) * wide, wide), wide)] = a[...]


def weight_join_kernel(place_ref, b0, b1, b2, b3, q_ref, k_ref, v_ref):
    s = place_ref[1]
    wide = q_ref.shape[1] // 4
    narrow = k_ref.shape[1] // 4
    blocks = [b[...] for b in (b0, b1, b2, b3)]
    for j, b in enumerate(blocks):
        q_ref[:, pl.ds(pl.multiple_of((s ^ j) * wide, wide), wide)] = b[:, :wide]
    odd, high = s % 2 == 1, s // 2 == 1
    tails = [b[:, wide:] for b in blocks]
    one = [jnp.where(odd, tails[i ^ 1], tails[i]) for i in range(4)]
    two = [jnp.where(high, one[i ^ 2], one[i]) for i in range(4)]
    k_ref[...] = jnp.concatenate([b[:, :narrow] for b in two], axis=1)
    v_ref[...] = jnp.concatenate([b[:, narrow:] for b in two], axis=1)


def head_body(tokens, adjacency, w_query, w_key, value_weight, grad_attn):
    x0 = tokens[0]
    rows, width = x0.shape
    depth = w_query.shape[0]
    wide = w_query.shape[1] // 4
    narrow = w_key.shape[1] // 4
    joined = wide + 2 * narrow
    place = jnp.stack([lax.axis_index("fsdp"), lax.axis_index("seq")]).astype(jnp.int32)

    x2 = swap(x0, "seq", 2)
    x1 = swap(x0, "seq", 1)
    x3 = swap(x2, "seq", 1)

    packed = vmem_call(
        pack_kernel,
        [shape(4, depth, joined)]
        + [shape(depth, joined)] * 3
        + [shape(rows, wide)] * 4,
        smem=1,
    )(place, w_query, w_key, value_weight, grad_attn[0])
    w_all, w_send, g_send = packed[0], packed[1:4], packed[4:8]

    w_rows = jnp.stack([w_all[0]] + [swap(w_send[j - 1], "seq", j) for j in (1, 2, 3)])
    w_plane = [w_rows] + [swap(w_rows, "fsdp", j) for j in (2, 4, 6)]
    w_other = [swap(w, "fsdp", 1) for w in w_plane]
    w_group = [w_plane[i // 2] if i % 2 == 0 else w_other[i // 2] for i in range(8)]
    g_got = [g_send[0]] + [swap(g_send[j], "seq", j) for j in (1, 2, 3)]

    u_rows = jnp.stack([w_all, swap(w_all, "seq", 2)])
    u_plane = [u_rows] + [swap(u_rows, "fsdp", j) for j in (2, 4, 6)]
    u_other = [swap(u, "fsdp", 1) for u in u_plane]
    u_group = [u_plane[i // 2] if i % 2 == 0 else u_other[i // 2] for i in range(8)]

    results = vmem_call(
        attend_kernel,
        [shape(rows, wide)] * 4 + [shape(2 * rows, joined)] * 4,
        scratch_shapes=[
            pltpu.VMEM((8, 4 * depth, joined), BF16),
            pltpu.VMEM((4 * rows, wide), BF16),
            pltpu.VMEM((4 * rows, wide), BF16),
        ],
        smem=2,
        total=8 << 30,
    )(place, adjacency, x0, x1, x2, x3, *w_group, *g_got)
    att, d = results[:4], results[4:]

    d_got = [d[0]] + [swap(d[j], "seq", j) for j in (1, 2, 3)]

    def weight_grad(parity):
        return vmem_call(
            functools.partial(weight_grad_kernel, parity),
            shape(4, 4, depth, joined, dtype=F32),
            smem=1,
            total=1 << 30,
        )(place, x0, x1, x2, x3, d[0], d[2])

    sent = swap(weight_grad(1), "fsdp", 1)
    kept = weight_grad(0)
    total = [kept[i] + sent[i] for i in range(4)]
    got = [swap(total[i], "fsdp", 2 * i) for i in (1, 2, 3)]
    factor = 1.0 / math.sqrt(4 * rows * lax.axis_size("fsdp"))
    summed = (((total[0] + got[0]) + (got[1] + got[2])) * factor).astype(BF16)
    w_final = [summed[0]] + [swap(summed[j], "seq", j) for j in (1, 2, 3)]

    att_got = [att[0]] + [swap(att[j], "seq", j) for j in (1, 2, 3)]

    own, send = vmem_call(
        token_grad_kernel,
        [shape(rows, width // 2)] * 2,
        smem=1,
        total=1 << 30,
    )(place, *d_got, *u_group)
    half = swap(send, "seq", 1)

    attended = vmem_call(attended_join_kernel, shape(rows, 4 * wide), smem=1)(place, *att_got)
    grad_in = vmem_call(token_join_kernel, shape(rows, width), smem=1)(place, own, half)
    grad_wq, grad_wk, grad_wv = vmem_call(
        weight_join_kernel,
        [shape(depth, 4 * wide), shape(depth, 4 * narrow), shape(depth, 4 * narrow)],
        smem=1,
    )(place, *w_final)
    return attended[None], grad_in[None], grad_wq, grad_wk, grad_wv


def solution(mesh):
    by_heads = mesh.shape["seq"] == KEY_VALUE_HEADS and mesh.shape["fsdp"] == 8
    return jax.shard_map(
        head_body if by_heads else general_body,
        mesh=mesh,
        in_specs=(
            P("fsdp", "seq", None),
            P(),
            P(("fsdp", "seq"), None),
            P(("fsdp", "seq"), None),
            P(("fsdp", "seq"), None),
            P("fsdp", "seq", None),
        ),
        out_specs=(
            P("fsdp", "seq", None),
            P("fsdp", "seq", None),
            P(("fsdp", "seq"), None),
            P(("fsdp", "seq"), None),
            P(("fsdp", "seq"), None),
        ),
        check_vma=False,
    )
```

time: 446 us -> 165 us (0.37)
  waiting for transfers between devices: 302 us -> 87 us
  matrix products: 64.5 us -> 0 us
  starting transfers between devices: 0.42 us -> 49.4 us
  blocking collectives: 27.9 us -> 0 us
  Pallas kernels: 0 us -> 22.1 us
  local copies, waits for them, and re-layouts: 26.7 us -> 5.13 us
  between operations: 14.4 us -> 0.77 us
  other arithmetic: 7.93 us -> 0.39 us
    all_gather x3 -> x0, waiting for transfers between devices: 141 us -> none  [the longest x1 55.6 us: body(): lax.all_gather(w_key, ('fsdp', 'seq'), axis=0, tiled=True)]
    unnamed x7 -> x0, waiting for transfers between devices: 139 us -> none
    ppermute x0 -> x38, waiting for transfers between devices: none -> 87 us  [swap(): return lax.ppermute(x, axis, [(i, i ^ j) for i in range(n)])]
    dot_general x27 -> x0, matrix products: 56.2 us -> none  [the longest x4 11.7 us: attend_group(): jnp.einsum('hqk,qhd->kd', grad_scores, query, preferred_element_type=jnp....]
    ppermute x0 -> x38, starting transfers between devices: none -> 49.4 us  [swap(): return lax.ppermute(x, axis, [(i, i ^ j) for i in range(n)])]
    all_gather x2 -> x0, blocking collectives: 27.9 us -> none  [the longest x1 14 us: body(): lax.all_gather(values, 'seq', axis=0, tiled=True)]
    pallas_call x0 -> x8, Pallas kernels: none -> 22.1 us  [call(): pl.pallas_call(kernel, out_shape=out_shape, in_specs=in_specs, out_specs=...]
    reduce_scatter x2 -> x0, waiting for transfers between devices: 22 us -> none  [the longest x1 21.8 us: body(): lax.psum_scatter(value_terms, 'seq', scatter_dimension=0, tiled=True)]
  transfers between devices with their start and end apart: 6 -> 38, of which waited for: 6 -> 15; matrix products, arithmetic and copies ran while one was open for 10% -> 0% of each run, Pallas kernels for 0% -> 6%
where the time goes in v1:
time: 165 us
  waiting for transfers between devices  87 us (53%)
  starting transfers between devices  49.4 us (30%)
  Pallas kernels  22.1 us (13%)
  local copies, waits for them, and re-layouts  5.13 us (3%)
    ppermute x38, waiting for transfers between devices, swap(): return lax.ppermute(x, axis, [(i, i ^ j) for i in range(n)])  87 us
    ppermute x38, starting transfers between devices, swap(): return lax.ppermute(x, axis, [(i, i ^ j) for i in range(n)])  49.4 us
    pallas_call x8, Pallas kernels, call(): pl.pallas_call(kernel, out_shape=out_shape, in_specs=in_specs, out_specs=...  22.1 us
    unnamed x14, local copies, waits for them, and re-layouts  5.1 us
  transfers between devices with their start and end apart: 38, of which 15 were waited for; matrix products, arithmetic and copies ran while one was open for 0% of the time, Pallas kernels for 6%

profile of v1, /device:TPU:0, one launch (start us, length us, event | category | flops | bytes accessed | tf_op | source)
XLA Modules:
  0.0 164.8 jit_solution(224549401697187298)
XLA Ops:
  0.6 4.1 %collective-permute-start.1 = (bf16[128,2048]{1,0:T(8,128)(2,1)}, bf16[128,2048]{1,0:T(8,128)(2,1)S(1)}, u32[]{:S(2)}, u32[]{:S(2)}) collective-permute-start(bf16[128,2048]{1,0:T(8,128)(2,1)} %bitcast.35), channel_id=1, source_target_pairs={{0,2},{1,3},{2,0},{3,1},{4,6},{5,7},{6,4},{7,5},{8,10},{9,11},{10,... | collective-permute-start | bytes 1572872 | tf_op jit(solution)/shard_map/ppermute | solution.py:104
  4.8 0.9 copy-done.2
  5.8 0.9 copy-done.3
  6.7 0.8 copy-done.4
  8.9 1.6 collective-permute-start.3
  10.9 2.5 %collective-permute-start.5 = (bf16[64,384]{1,0:T(8,128)(2,1)S(1)}, bf16[64,384]{1,0:T(8,128)(2,1)S(1)}, u32[]{:S(2)}, u32[]{:S(2)}) collective-permute-start(bf16[64,384]{1,0:T(8,128)(2,1)S(1)} %get-tuple-element.29), channel_id=1, source_target_pairs={{0,3},{1,2},{2,1},{3,0},{4,7},{5,6},{6,5},{7,4},{8,11},{9,10},{10,... | collective-permute-start | bytes 147464 | tf_op jit(solution)/shard_map/ppermute | solution.py:104
  13.4 4.9 %collective-permute-done.3 = bf16[64,384]{1,0:T(8,128)(2,1)S(1)} collective-permute-done((bf16[64,384]{1,0:T(8,128)(2,1)S(1)}, bf16[64,384]{1,0:T(8,128)(2,1)S(1)}, u32[]{:S(2)}, u32[]{:S(2)}) %collective-permute-start.3) | collective-permute-done | bytes 49184 | tf_op jit(solution)/shard_map/ppermute | solution.py:104
  18.3 13.5 %collective-permute-done.4 = bf16[64,384]{1,0:T(8,128)(2,1)S(1)} collective-permute-done((bf16[64,384]{1,0:T(8,128)(2,1)S(1)}, bf16[64,384]{1,0:T(8,128)(2,1)S(1)}, u32[]{:S(2)}, u32[]{:S(2)}) %collective-permute-start.4) | collective-permute-done | bytes 49184 | tf_op jit(solution)/shard_map/ppermute | solution.py:104
  31.8 1.6 collective-permute-start.9
  33.5 1.2 collective-permute-start.13
  34.7 0.8 collective-permute-start
  35.5 1.2 collective-permute-start.2
  36.7 2.4 %collective-permute-start.14 = (bf16[128,256]{1,0:T(8,128)(2,1)S(1)}, bf16[128,256]{1,0:T(8,128)(2,1)S(1)}, u32[]{:S(2)}, u32[]{:S(2)}) collective-permute-start(bf16[128,256]{1,0:T(8,128)(2,1)S(1)} %get-tuple-element.32), channel_id=1, source_target_pairs={{0,2},{1,3},{2,0},{3,1},{4,6},{5,7},{6,4},{7,5},{8,10},{9,11},{10,... | collective-permute-start | bytes 196616 | tf_op jit(solution)/shard_map/ppermute | solution.py:104
  39.1 2.2 %collective-permute-start.15 = (bf16[128,256]{1,0:T(8,128)(2,1)S(1)}, bf16[128,256]{1,0:T(8,128)(2,1)S(1)}, u32[]{:S(2)}, u32[]{:S(2)}) collective-permute-start(bf16[128,256]{1,0:T(8,128)(2,1)S(1)} %get-tuple-element.33), channel_id=1, source_target_pairs={{0,3},{1,2},{2,1},{3,0},{4,7},{5,6},{6,5},{7,4},{8,11},{9,10},{10,... | collective-permute-start | bytes 196616 | tf_op jit(solution)/shard_map/ppermute | solution.py:104
  41.3 19.2 %collective-permute-done.14.refs_14_ = bf16[128,256]{1,0:T(8,128)(2,1)S(1)} collective-permute-done((bf16[128,256]{1,0:T(8,128)(2,1)S(1)}, bf16[128,256]{1,0:T(8,128)(2,1)S(1)}, u32[]{:S(2)}, u32[]{:S(2)}) %collective-permute-start.14) | collective-permute-done | bytes 65568 | tf_op jit(solution)/shard_map/ppermute | solution.py:104
  60.5 1.4 collective-permute-start.11
  61.9 3.1 %collective-permute-done.15.refs_15_ = bf16[128,256]{1,0:T(8,128)(2,1)S(1)} collective-permute-done((bf16[128,256]{1,0:T(8,128)(2,1)S(1)}, bf16[128,256]{1,0:T(8,128)(2,1)S(1)}, u32[]{:S(2)}, u32[]{:S(2)}) %collective-permute-start.15) | collective-permute-done | bytes 65568 | tf_op jit(solution)/shard_map/ppermute | solution.py:104
  65.0 1.5 collective-permute-start.7
  66.5 1.5 collective-permute-done.11.refs_10_
  68.0 2.7 %collective-permute-done.7.refs_6_ = bf16[4,64,384]{2,1,0:T(8,128)(2,1)S(1)} collective-permute-done((bf16[4,64,384]{2,1,0:T(8,128)(2,1)S(1)}, bf16[4,64,384]{2,1,0:T(8,128)(2,1)S(1)}, u32[]{:S(2)}, u32[]{:S(2)}) %collective-permute-start.7) | collective-permute-done | bytes 196640 | tf_op jit(solution)/shard_map/ppermute | solution.py:104
  71.2 0.9 collective-permute-done.12.refs_11_
  72.4 1.0 copy-done
  74.2 10.4 %shard_map.102 = (bf16[128,256]{1,0:T(8,128)(2,1)S(1)}, bf16[128,256]{1,0:T(8,128)(2,1)S(1)}, bf16[128,256]{1,0:T(8,128)(2,1)S(1)}, bf16[128,256]{1,0:T(8,128)(2...) custom-call(s32[2]{0:T(128)S(1)} %pad_add_fusion.place_ref, ...), custom_call_target="tpu_custom_call" | custom-call | flops 8589934592 | bytes 4194304 | tf_op jit(solution)/shard_map/pallas_call | solution.py:114
  84.6 1.3 shard_map.107
  86.2 2.0 %collective-permute-start.22 = (bf16[4,64,384]{2,1,0:T(8,128)(2,1)S(1)}, bf16[4,64,384]{2,1,0:T(8,128)(2,1)S(1)}, u32[]{:S(2)}, u32[]{:S(2)}) collective-permute-start(bf16[4,64,384]{2,1,0:T(8,128)(2,1)S(1)} %get-tuple-element.26), channel_id=1, source_target_pairs={{0,2},{1,3},{2,0},{3,1},{4,6},{5,7},{6,4},{7,5},{8,10},{9,11},{10,... | collective-permute-start | bytes 589832 | tf_op jit(solution)/shard_map/ppermute | solution.py:104
  88.2 10.2 %collective-permute-done.22 = bf16[4,64,384]{2,1,0:T(8,128)(2,1)S(1)} collective-permute-done((bf16[4,64,384]{2,1,0:T(8,128)(2,1)S(1)}, bf16[4,64,384]{2,1,0:T(8,128)(2,1)S(1)}, u32[]{:S(2)}, u32[]{:S(2)}) %collective-permute-start.22) | collective-permute-done | bytes 196640 | tf_op jit(solution)/shard_map/ppermute | solution.py:104
  98.4 1.6 collective-permute-start.24
  100.0 1.1 collective-permute-start.26
  101.1 0.8 collective-permute-start.28
  102.0 8.6 %collective-permute-done.24.refs_2_ = bf16[2,4,64,384]{3,2,1,0:T(8,128)(2,1)S(1)} collective-permute-done((bf16[2,4,64,384]{3,2,1,0:T(8,128)(2,1)S(1)}, bf16[2,4,64,384]{3,2,1,0:T(8,128)(2,1)S(1)}, u32[]{:S(2)}, u32[]{:S(2)}) %collective-permute-start.24) | collective-permute-done | bytes 393248 | tf_op jit(solution)/shard_map/ppermute | solution.py:104
  110.6 8.1 %collective-permute-done.26.refs_4_ = bf16[2,4,64,384]{3,2,1,0:T(8,128)(2,1)S(1)} collective-permute-done((bf16[2,4,64,384]{3,2,1,0:T(8,128)(2,1)S(1)}, bf16[2,4,64,384]{3,2,1,0:T(8,128)(2,1)S(1)}, u32[]{:S(2)}, u32[]{:S(2)}) %collective-permute-start.26) | collective-permute-done | bytes 393248 | tf_op jit(solution)/shard_map/ppermute | solution.py:104
  119.1 1.3 shard_map.106
  121.0 0.8 collective-permute-start.32
  121.8 1.3 collective-permute-start.33
  123.1 1.4 collective-permute-start.34
  124.5 3.4 %collective-permute-start.20 = (bf16[256,384]{1,0:T(8,128)(2,1)S(1)}, bf16[256,384]{1,0:T(8,128)(2,1)S(1)}, u32[]{:S(2)}, u32[]{:S(2)}) collective-permute-start(bf16[256,384]{1,0:T(8,128)(2,1)S(1)} %get-tuple-element.40.d2_ref), channel_id=1, source_target_pairs={{0,2},{1,3},{2,0},{3,1},{4,6},{5,7},{6,4},{7,5},{8,10},{9,11},{10,... | collective-permute-start | bytes 589832 | tf_op jit(solution)/shard_map/ppermute | solution.py:104
  127.9 3.8 %collective-permute-start.21 = (bf16[256,384]{1,0:T(8,128)(2,1)S(1)}, bf16[256,384]{1,0:T(8,128)(2,1)S(1)}, u32[]{:S(2)}, u32[]{:S(2)}) collective-permute-start(bf16[256,384]{1,0:T(8,128)(2,1)S(1)} %get-tuple-element.41), channel_id=1, source_target_pairs={{0,3},{1,2},{2,1},{3,0},{4,7},{5,6},{6,5},{7,4},{8,11},{9,10},{10,... | collective-permute-start | bytes 589832 | tf_op jit(solution)/shard_map/ppermute | solution.py:104
  131.7 9.8 %collective-permute-done.20.d2 = bf16[256,384]{1,0:T(8,128)(2,1)S(1)} collective-permute-done((bf16[256,384]{1,0:T(8,128)(2,1)S(1)}, bf16[256,384]{1,0:T(8,128)(2,1)S(1)}, u32[]{:S(2)}, u32[]{:S(2)}) %collective-permute-start.20) | collective-permute-done | bytes 196640 | tf_op jit(solution)/shard_map/ppermute | solution.py:104
  141.5 4.5 %collective-permute-start.17 = (bf16[128,256]{1,0:T(8,128)(2,1)S(1)}, bf16[128,256]{1,0:T(8,128)(2,1)S(1)}, u32[]{:S(2)}, u32[]{:S(2)}) collective-permute-start(bf16[128,256]{1,0:T(8,128)(2,1)S(1)} %get-tuple-element.36), channel_id=1, source_target_pairs={{0,2},{1,3},{2,0},{3,1},{4,6},{5,7},{6,4},{7,5},{8,10},{9,11},{10,... | collective-permute-start | bytes 196616 | tf_op jit(solution)/shard_map/ppermute | solution.py:104
  146.0 4.3 %shard_map.104 = (bf16[128,1024]{1,0:T(8,128)(2,1)S(1)}, bf16[128,1024]{1,0:T(8,128)(2,1)S(1)}) custom-call(s32[2]{0:T(128)S(1)} %pad_add_fusion.place_ref, bf16[256,384]{1,0:T(8,128)(2,1)S(1)} %get-tuple-element.38.d0.d0_ref, bf16[256,384]{1,0:T(8,128)(2,1)S(1)} %collective-permute-done.19.d1, bf16[256,384]{1,0:T(8,128)(2,1)S(1)} %collective-permute-done.20.d2, ...), custom_call_target="tpu_custom_call" | custom-call | flops 1073741824 | bytes 4194304 | tf_op jit(solution)/shard_map/pallas_call | solution.py:114
  150.3 1.5 collective-permute-start.18
  152.0 2.1 %collective-permute-start.35 = (bf16[64,384]{1,0:T(8,128)(2,1)S(1)}, bf16[64,384]{1,0:T(8,128)(2,1)S(1)}, u32[]{:S(2)}, u32[]{:S(2)}) collective-permute-start(bf16[64,384]{1,0:T(8,128)(2,1)S(1)} %get-tuple-element.52), channel_id=1, source_target_pairs={{0,1},{1,0},{2,3},{3,2},{4,5},{5,4},{6,7},{7,6},{8,9},{9,8},{10,11... | collective-permute-start | bytes 147464 | tf_op jit(solution)/shard_map/ppermute | solution.py:104
  154.0 1.0 collective-permute-start.36
  155.1 1.4 collective-permute-start.37
  157.2 1.3 shard_map.103
  158.5 3.3 %collective-permute-done.30.got_ref = bf16[128,1024]{1,0:T(8,128)(2,1)S(1)} collective-permute-done((bf16[128,1024]{1,0:T(8,128)(2,1)S(1)}, bf16[128,1024]{1,0:T(8,128)(2,1)S(1)}, u32[]{:S(2)}, u32[]{:S(2)}) %collective-permute-start.30) | collective-permute-done | bytes 262176 | tf_op jit(solution)/shard_map/ppermute | solution.py:104
  161.8 1.6 shard_map.105
  163.5 1.3 shard_map.108
  (57 shorter events, 5.8 us)
Async XLA Ops:
  0.6 34.9 %collective-permute-start.1 = (bf16[128,2048]{1,0:T(8,128)(2,1)}, bf16[128,2048]{1,0:T(8,128)(2,1)S(1)}, u32[]{:S(2)}, u32[]{:S(2)}) collective-permute-start(bf16[128,2048]{1,0:T(8,128)(2,1)} %bitcast.35), channel_id=1, source_target_pairs={{0,2},{1,3},{2,0},{3,1},{4,6},{5,7},{6,4},{7,5},{8,10},{9,11},{10,... | collective-permute-start | bytes 1572872 | tf_op jit(solution)/shard_map/ppermute | solution.py:104
  4.8 0.9 copy-start.2
  5.8 0.9 copy-start.3
  6.7 0.8 copy-start.4
  7.4 0.8 copy-start.5
  8.9 9.3 %collective-permute-start.3 = (bf16[64,384]{1,0:T(8,128)(2,1)S(1)}, bf16[64,384]{1,0:T(8,128)(2,1)S(1)}, u32[]{:S(2)}, u32[]{:S(2)}) collective-permute-start(bf16[64,384]{1,0:T(8,128)(2,1)S(1)} %get-tuple-element.27), channel_id=1, source_target_pairs={{0,1},{1,0},{2,3},{3,2},{4,5},{5,4},{6,7},{7,6},{8,9},{9,8},{10,11... | collective-permute-start | bytes 147464 | tf_op jit(solution)/shard_map/ppermute | solution.py:104
  10.6 21.2 %collective-permute-start.4 = (bf16[64,384]{1,0:T(8,128)(2,1)S(1)}, bf16[64,384]{1,0:T(8,128)(2,1)S(1)}, u32[]{:S(2)}, u32[]{:S(2)}) collective-permute-start(bf16[64,384]{1,0:T(8,128)(2,1)S(1)} %get-tuple-element.28), channel_id=1, source_target_pairs={{0,2},{1,3},{2,0},{3,1},{4,6},{5,7},{6,4},{7,5},{8,10},{9,11},{10,... | collective-permute-start | bytes 147464 | tf_op jit(solution)/shard_map/ppermute | solution.py:104
  10.9 20.9 %collective-permute-start.5 = (bf16[64,384]{1,0:T(8,128)(2,1)S(1)}, bf16[64,384]{1,0:T(8,128)(2,1)S(1)}, u32[]{:S(2)}, u32[]{:S(2)}) collective-permute-start(bf16[64,384]{1,0:T(8,128)(2,1)S(1)} %get-tuple-element.29), channel_id=1, source_target_pairs={{0,3},{1,2},{2,1},{3,0},{4,7},{5,6},{6,5},{7,4},{8,11},{9,10},{10,... | collective-permute-start | bytes 147464 | tf_op jit(solution)/shard_map/ppermute | solution.py:104
  31.8 34.7 %collective-permute-start.9 = (bf16[4,64,384]{2,1,0:T(8,128)(2,1)S(1)}, bf16[4,64,384]{2,1,0:T(8,128)(2,1)S(1)}, u32[]{:S(2)}, u32[]{:S(2)}) collective-permute-start(bf16[4,64,384]{2,1,0:T(8,128)(2,1)S(1)} %pad_maximum_fusion.1.refs_4_), channel_id=1, source_target_pairs={{0,16},{4,20},{8,24},{12,28},{16,0},{20,4},{24,8},{28,12},{1,17},{... | collective-permute-start | bytes 589832 | tf_op jit(solution)/shard_map/ppermute | solution.py:104
  33.5 5.7 %collective-permute-start.13 = (bf16[128,256]{1,0:T(8,128)(2,1)S(1)}, bf16[128,256]{1,0:T(8,128)(2,1)S(1)}, u32[]{:S(2)}, u32[]{:S(2)}) collective-permute-start(bf16[128,256]{1,0:T(8,128)(2,1)S(1)} %get-tuple-element.31), channel_id=1, source_target_pairs={{0,1},{1,0},{2,3},{3,2},{4,5},{5,4},{6,7},{7,6},{8,9},{9,8},{10,11... | collective-permute-start | bytes 196616 | tf_op jit(solution)/shard_map/ppermute | solution.py:104
  34.7 37.8 %collective-permute-start = (bf16[128,2048]{1,0:T(8,128)(2,1)}, bf16[128,2048]{1,0:T(8,128)(2,1)S(1)}, u32[]{:S(2)}, u32[]{:S(2)}) collective-permute-start(bf16[128,2048]{1,0:T(8,128)(2,1)} %bitcast.36), channel_id=1, source_target_pairs={{0,1},{1,0},{2,3},{3,2},{4,5},{5,4},{6,7},{7,6},{8,9},{9,8},{10,11... | collective-permute-start | bytes 1572872 | tf_op jit(solution)/shard_map/ppermute | solution.py:104
  35.5 36.9 %collective-permute-start.2 = (bf16[128,2048]{1,0:T(8,128)(2,1)S(1)}, bf16[128,2048]{1,0:T(8,128)(2,1)S(1)}, u32[]{:S(2)}, u32[]{:S(2)}) collective-permute-start(bf16[128,2048]{1,0:T(8,128)(2,1)S(1)} %collective-permute-done.1.refs_2_.x2), channel_id=1, source_target_pairs={{0,1},{1,0},{2,3},{3,2},{4,5},{5,4},{6,7},{7,6},{8,9},{9,8},{10,11... | collective-permute-start | bytes 1572872 | tf_op jit(solution)/shard_map/ppermute | solution.py:104
  36.7 23.8 %collective-permute-start.14 = (bf16[128,256]{1,0:T(8,128)(2,1)S(1)}, bf16[128,256]{1,0:T(8,128)(2,1)S(1)}, u32[]{:S(2)}, u32[]{:S(2)}) collective-permute-start(bf16[128,256]{1,0:T(8,128)(2,1)S(1)} %get-tuple-element.32), channel_id=1, source_target_pairs={{0,2},{1,3},{2,0},{3,1},{4,6},{5,7},{6,4},{7,5},{8,10},{9,11},{10,... | collective-permute-start | bytes 196616 | tf_op jit(solution)/shard_map/ppermute | solution.py:104
  39.1 25.9 %collective-permute-start.15 = (bf16[128,256]{1,0:T(8,128)(2,1)S(1)}, bf16[128,256]{1,0:T(8,128)(2,1)S(1)}, u32[]{:S(2)}, u32[]{:S(2)}) collective-permute-start(bf16[128,256]{1,0:T(8,128)(2,1)S(1)} %get-tuple-element.33), channel_id=1, source_target_pairs={{0,3},{1,2},{2,1},{3,0},{4,7},{5,6},{6,5},{7,4},{8,11},{9,10},{10,... | collective-permute-start | bytes 196616 | tf_op jit(solution)/shard_map/ppermute | solution.py:104
  60.5 7.5 %collective-permute-start.11 = (bf16[4,64,384]{2,1,0:T(8,128)(2,1)S(1)}, bf16[4,64,384]{2,1,0:T(8,128)(2,1)S(1)}, u32[]{:S(2)}, u32[]{:S(2)}) collective-permute-start(bf16[4,64,384]{2,1,0:T(8,128)(2,1)S(1)} %pad_maximum_fusion.1.refs_4_), channel_id=1, source_target_pairs={{0,24},{4,28},{8,16},{12,20},{16,8},{20,12},{24,0},{28,4},{1,25},{... | collective-permute-start | bytes 589832 | tf_op jit(solution)/shard_map/ppermute | solution.py:104
  65.0 5.7 %collective-permute-start.7 = (bf16[4,64,384]{2,1,0:T(8,128)(2,1)S(1)}, bf16[4,64,384]{2,1,0:T(8,128)(2,1)S(1)}, u32[]{:S(2)}, u32[]{:S(2)}) collective-permute-start(bf16[4,64,384]{2,1,0:T(8,128)(2,1)S(1)} %pad_maximum_fusion.1.refs_4_), channel_id=1, source_target_pairs={{0,8},{4,12},{8,0},{12,4},{16,24},{20,28},{24,16},{28,20},{1,9},{5... | collective-permute-start | bytes 589832 | tf_op jit(solution)/shard_map/ppermute | solution.py:104
  66.5 4.2 %collective-permute-start.6 = (bf16[4,64,384]{2,1,0:T(8,128)(2,1)S(1)}, bf16[4,64,384]{2,1,0:T(8,128)(2,1)S(1)}, u32[]{:S(2)}, u32[]{:S(2)}) collective-permute-start(bf16[4,64,384]{2,1,0:T(8,128)(2,1)S(1)} %pad_maximum_fusion.1.refs_4_), channel_id=1, source_target_pairs={{0,4},{4,0},{8,12},{12,8},{16,20},{20,16},{24,28},{28,24},{1,5},{5... | collective-permute-start | bytes 589832 | tf_op jit(solution)/shard_map/ppermute | solution.py:104
  68.0 3.2 %collective-permute-start.10 = (bf16[4,64,384]{2,1,0:T(8,128)(2,1)S(1)}, bf16[4,64,384]{2,1,0:T(8,128)(2,1)S(1)}, u32[]{:S(2)}, u32[]{:S(2)}) collective-permute-start(bf16[4,64,384]{2,1,0:T(8,128)(2,1)S(1)} %collective-permute-done.9.refs_8_), channel_id=1, source_target_pairs={{0,4},{4,0},{8,12},{12,8},{16,20},{20,16},{24,28},{28,24},{1,5},{5... | collective-permute-start | bytes 589832 | tf_op jit(solution)/shard_map/ppermute | solution.py:104
  70.7 1.4 collective-permute-start.12
  70.7 1.7 %collective-permute-start.8 = (bf16[4,64,384]{2,1,0:T(8,128)(2,1)S(1)}, bf16[4,64,384]{2,1,0:T(8,128)(2,1)S(1)}, u32[]{:S(2)}, u32[]{:S(2)}) collective-permute-start(bf16[4,64,384]{2,1,0:T(8,128)(2,1)S(1)} %collective-permute-done.7.refs_6_), channel_id=1, source_target_pairs={{0,4},{4,0},{8,12},{12,8},{16,20},{20,16},{24,28},{28,24},{1,5},{5... | collective-permute-start | bytes 589832 | tf_op jit(solution)/shard_map/ppermute | solution.py:104
  72.4 1.0 copy-start
  73.5 0.7 copy-start.6
  74.2 10.4 %copy-start.1 = (bf16[1,128,2048]{2,1,0:T(8,128)(2,1)S(1)}, bf16[1,128,2048]{2,1,0:T(8,128)(2,1)}, u32[]{:S(2)}) copy-start(bf16[1,128,2048]{2,1,0:T(8,128)(2,1)} %param.6) | copy-start | bytes 1572868
  85.9 34.6 %collective-permute-start.31 = (f32[4,4,64,384]{3,2,1,0:T(8,128)S(1)}, f32[4,4,64,384]{3,2,1,0:T(8,128)S(1)}, u32[]{:S(2)}, u32[]{:S(2)}) collective-permute-start(f32[4,4,64,384]{3,2,1,0:T(8,128)S(1)} %shard_map.107), channel_id=1, source_target_pairs={{0,4},{4,0},{8,12},{12,8},{16,20},{20,16},{24,28},{28,24},{1,5},{5... | collective-permute-start | bytes 4718600 | tf_op jit(solution)/shard_map/ppermute | solution.py:104
  86.2 12.2 %collective-permute-start.22 = (bf16[4,64,384]{2,1,0:T(8,128)(2,1)S(1)}, bf16[4,64,384]{2,1,0:T(8,128)(2,1)S(1)}, u32[]{:S(2)}, u32[]{:S(2)}) collective-permute-start(bf16[4,64,384]{2,1,0:T(8,128)(2,1)S(1)} %get-tuple-element.26), channel_id=1, source_target_pairs={{0,2},{1,3},{2,0},{3,1},{4,6},{5,7},{6,4},{7,5},{8,10},{9,11},{10,... | collective-permute-start | bytes 589832 | tf_op jit(solution)/shard_map/ppermute | solution.py:104
  98.4 12.1 %collective-permute-start.24 = (bf16[2,4,64,384]{3,2,1,0:T(8,128)(2,1)S(1)}, bf16[2,4,64,384]{3,2,1,0:T(8,128)(2,1)S(1)}, u32[]{:S(2)}, u32[]{:S(2)}) collective-permute-start(bf16[2,4,64,384]{3,2,1,0:T(8,128)(2,1)S(1)} %pad_maximum_fusion.refs_0_), channel_id=1, source_target_pairs={{0,8},{4,12},{8,0},{12,4},{16,24},{20,28},{24,16},{28,20},{1,9},{5... | collective-permute-start | bytes 1179656 | tf_op jit(solution)/shard_map/ppermute | solution.py:104
  100.0 18.6 %collective-permute-start.26 = (bf16[2,4,64,384]{3,2,1,0:T(8,128)(2,1)S(1)}, bf16[2,4,64,384]{3,2,1,0:T(8,128)(2,1)S(1)}, u32[]{:S(2)}, u32[]{:S(2)}) collective-permute-start(bf16[2,4,64,384]{3,2,1,0:T(8,128)(2,1)S(1)} %pad_maximum_fusion.refs_0_), channel_id=1, source_target_pairs={{0,16},{4,20},{8,24},{12,28},{16,0},{20,4},{24,8},{28,12},{1,17},{... | collective-permute-start | bytes 1179656 | tf_op jit(solution)/shard_map/ppermute | solution.py:104
  101.1 17.5 %collective-permute-start.28 = (bf16[2,4,64,384]{3,2,1,0:T(8,128)(2,1)S(1)}, bf16[2,4,64,384]{3,2,1,0:T(8,128)(2,1)S(1)}, u32[]{:S(2)}, u32[]{:S(2)}) collective-permute-start(bf16[2,4,64,384]{3,2,1,0:T(8,128)(2,1)S(1)} %pad_maximum_fusion.refs_0_), channel_id=1, source_target_pairs={{0,24},{4,28},{8,16},{12,20},{16,8},{20,12},{24,0},{28,4},{1,25},{... | collective-permute-start | bytes 1179656 | tf_op jit(solution)/shard_map/ppermute | solution.py:104
  102.0 19.0 %collective-permute-start.23 = (bf16[2,4,64,384]{3,2,1,0:T(8,128)(2,1)S(1)}, bf16[2,4,64,384]{3,2,1,0:T(8,128)(2,1)S(1)}, u32[]{:S(2)}, u32[]{:S(2)}) collective-permute-start(bf16[2,4,64,384]{3,2,1,0:T(8,128)(2,1)S(1)} %pad_maximum_fusion.refs_0_), channel_id=1, source_target_pairs={{0,4},{4,0},{8,12},{12,8},{16,20},{20,16},{24,28},{28,24},{1,5},{5... | collective-permute-start | bytes 1179656 | tf_op jit(solution)/shard_map/ppermute | solution.py:104
  110.6 11.2 %collective-permute-start.25 = (bf16[2,4,64,384]{3,2,1,0:T(8,128)(2,1)S(1)}, bf16[2,4,64,384]{3,2,1,0:T(8,128)(2,1)S(1)}, u32[]{:S(2)}, u32[]{:S(2)}) collective-permute-start(bf16[2,4,64,384]{3,2,1,0:T(8,128)(2,1)S(1)} %collective-permute-done.24.refs_2_), channel_id=1, source_target_pairs={{0,4},{4,0},{8,12},{12,8},{16,20},{20,16},{24,28},{28,24},{1,5},{5... | collective-permute-start | bytes 1179656 | tf_op jit(solution)/shard_map/ppermute | solution.py:104
  118.6 4.5 %collective-permute-start.27 = (bf16[2,4,64,384]{3,2,1,0:T(8,128)(2,1)S(1)}, bf16[2,4,64,384]{3,2,1,0:T(8,128)(2,1)S(1)}, u32[]{:S(2)}, u32[]{:S(2)}) collective-permute-start(bf16[2,4,64,384]{3,2,1,0:T(8,128)(2,1)S(1)} %collective-permute-done.26.refs_4_), channel_id=1, source_target_pairs={{0,4},{4,0},{8,12},{12,8},{16,20},{20,16},{24,28},{28,24},{1,5},{5... | collective-permute-start | bytes 1179656 | tf_op jit(solution)/shard_map/ppermute | solution.py:104
  118.6 5.9 %collective-permute-start.29 = (bf16[2,4,64,384]{3,2,1,0:T(8,128)(2,1)S(1)}, bf16[2,4,64,384]{3,2,1,0:T(8,128)(2,1)S(1)}, u32[]{:S(2)}, u32[]{:S(2)}) collective-permute-start(bf16[2,4,64,384]{3,2,1,0:T(8,128)(2,1)S(1)} %collective-permute-done.28.refs_6_), channel_id=1, source_target_pairs={{0,4},{4,0},{8,12},{12,8},{16,20},{20,16},{24,28},{28,24},{1,5},{5... | collective-permute-start | bytes 1179656 | tf_op jit(solution)/shard_map/ppermute | solution.py:104
  120.5 7.4 %collective-permute-start.19 = (bf16[256,384]{1,0:T(8,128)(2,1)S(1)}, bf16[256,384]{1,0:T(8,128)(2,1)S(1)}, u32[]{:S(2)}, u32[]{:S(2)}) collective-permute-start(bf16[256,384]{1,0:T(8,128)(2,1)S(1)} %get-tuple-element.39), channel_id=1, source_target_pairs={{0,1},{1,0},{2,3},{3,2},{4,5},{5,4},{6,7},{7,6},{8,9},{9,8},{10,11... | collective-permute-start | bytes 589832 | tf_op jit(solution)/shard_map/ppermute | solution.py:104
  121.0 29.4 %collective-permute-start.32 = (f32[4,64,384]{2,1,0:T(8,128)S(1)}, f32[4,64,384]{2,1,0:T(8,128)S(1)}, u32[]{:S(2)}, u32[]{:S(2)}) collective-permute-start(f32[4,64,384]{2,1,0:T(8,128)S(1)} %get-tuple-element.49), channel_id=1, source_target_pairs={{0,8},{4,12},{8,0},{12,4},{16,24},{20,28},{24,16},{28,20},{1,9},{5... | collective-permute-start | bytes 1179656 | tf_op jit(solution)/shard_map/ppermute | solution.py:104
  121.8 30.0 %collective-permute-start.33 = (f32[4,64,384]{2,1,0:T(8,128)S(1)}, f32[4,64,384]{2,1,0:T(8,128)S(1)}, u32[]{:S(2)}, u32[]{:S(2)}) collective-permute-start(f32[4,64,384]{2,1,0:T(8,128)S(1)} %get-tuple-element.48), channel_id=1, source_target_pairs={{0,16},{4,20},{8,24},{12,28},{16,0},{20,4},{24,8},{28,12},{1,17},{... | collective-permute-start | bytes 1179656 | tf_op jit(solution)/shard_map/ppermute | solution.py:104
  123.1 28.7 %collective-permute-start.34 = (f32[4,64,384]{2,1,0:T(8,128)S(1)}, f32[4,64,384]{2,1,0:T(8,128)S(1)}, u32[]{:S(2)}, u32[]{:S(2)}) collective-permute-start(f32[4,64,384]{2,1,0:T(8,128)S(1)} %get-tuple-element.47), channel_id=1, source_target_pairs={{0,24},{4,28},{8,16},{12,20},{16,8},{20,12},{24,0},{28,4},{1,25},{... | collective-permute-start | bytes 1179656 | tf_op jit(solution)/shard_map/ppermute | solution.py:104
  124.5 17.0 %collective-permute-start.20 = (bf16[256,384]{1,0:T(8,128)(2,1)S(1)}, bf16[256,384]{1,0:T(8,128)(2,1)S(1)}, u32[]{:S(2)}, u32[]{:S(2)}) collective-permute-start(bf16[256,384]{1,0:T(8,128)(2,1)S(1)} %get-tuple-element.40.d2_ref), channel_id=1, source_target_pairs={{0,2},{1,3},{2,0},{3,1},{4,6},{5,7},{6,4},{7,5},{8,10},{9,11},{10,... | collective-permute-start | bytes 589832 | tf_op jit(solution)/shard_map/ppermute | solution.py:104
  127.9 13.6 %collective-permute-start.21 = (bf16[256,384]{1,0:T(8,128)(2,1)S(1)}, bf16[256,384]{1,0:T(8,128)(2,1)S(1)}, u32[]{:S(2)}, u32[]{:S(2)}) collective-permute-start(bf16[256,384]{1,0:T(8,128)(2,1)S(1)} %get-tuple-element.41), channel_id=1, source_target_pairs={{0,3},{1,2},{2,1},{3,0},{4,7},{5,6},{6,5},{7,4},{8,11},{9,10},{10,... | collective-permute-start | bytes 589832 | tf_op jit(solution)/shard_map/ppermute | solution.py:104
  141.5 12.5 %collective-permute-start.16 = (bf16[128,256]{1,0:T(8,128)(2,1)S(1)}, bf16[128,256]{1,0:T(8,128)(2,1)S(1)}, u32[]{:S(2)}, u32[]{:S(2)}) collective-permute-start(bf16[128,256]{1,0:T(8,128)(2,1)S(1)} %get-tuple-element.35), channel_id=1, source_target_pairs={{0,1},{1,0},{2,3},{3,2},{4,5},{5,4},{6,7},{7,6},{8,9},{9,8},{10,11... | collective-permute-start | bytes 196616 | tf_op jit(solution)/shard_map/ppermute | solution.py:104
  141.5 13.6 %collective-permute-start.17 = (bf16[128,256]{1,0:T(8,128)(2,1)S(1)}, bf16[128,256]{1,0:T(8,128)(2,1)S(1)}, u32[]{:S(2)}, u32[]{:S(2)}) collective-permute-start(bf16[128,256]{1,0:T(8,128)(2,1)S(1)} %get-tuple-element.36), channel_id=1, source_target_pairs={{0,2},{1,3},{2,0},{3,1},{4,6},{5,7},{6,4},{7,5},{8,10},{9,11},{10,... | collective-permute-start | bytes 196616 | tf_op jit(solution)/shard_map/ppermute | solution.py:104
  150.3 6.9 %collective-permute-start.18 = (bf16[128,256]{1,0:T(8,128)(2,1)S(1)}, bf16[128,256]{1,0:T(8,128)(2,1)S(1)}, u32[]{:S(2)}, u32[]{:S(2)}) collective-permute-start(bf16[128,256]{1,0:T(8,128)(2,1)S(1)} %get-tuple-element.37), channel_id=1, source_target_pairs={{0,3},{1,2},{2,1},{3,0},{4,7},{5,6},{6,5},{7,4},{8,11},{9,10},{10,... | collective-permute-start | bytes 196616 | tf_op jit(solution)/shard_map/ppermute | solution.py:104
  151.8 10.0 %collective-permute-start.30 = (bf16[128,1024]{1,0:T(8,128)(2,1)S(1)}, bf16[128,1024]{1,0:T(8,128)(2,1)S(1)}, u32[]{:S(2)}, u32[]{:S(2)}) collective-permute-start(bf16[128,1024]{1,0:T(8,128)(2,1)S(1)} %get-tuple-element.43), channel_id=1, source_target_pairs={{0,1},{1,0},{2,3},{3,2},{4,5},{5,4},{6,7},{7,6},{8,9},{9,8},{10,11... | collective-permute-start | bytes 786440 | tf_op jit(solution)/shard_map/ppermute | solution.py:104
  152.0 11.4 %collective-permute-start.35 = (bf16[64,384]{1,0:T(8,128)(2,1)S(1)}, bf16[64,384]{1,0:T(8,128)(2,1)S(1)}, u32[]{:S(2)}, u32[]{:S(2)}) collective-permute-start(bf16[64,384]{1,0:T(8,128)(2,1)S(1)} %get-tuple-element.52), channel_id=1, source_target_pairs={{0,1},{1,0},{2,3},{3,2},{4,5},{5,4},{6,7},{7,6},{8,9},{9,8},{10,11... | collective-permute-start | bytes 147464 | tf_op jit(solution)/shard_map/ppermute | solution.py:104
  154.0 9.4 %collective-permute-start.36 = (bf16[64,384]{1,0:T(8,128)(2,1)S(1)}, bf16[64,384]{1,0:T(8,128)(2,1)S(1)}, u32[]{:S(2)}, u32[]{:S(2)}) collective-permute-start(bf16[64,384]{1,0:T(8,128)(2,1)S(1)} %get-tuple-element.51), channel_id=1, source_target_pairs={{0,2},{1,3},{2,0},{3,1},{4,6},{5,7},{6,4},{7,5},{8,10},{9,11},{10,... | collective-permute-start | bytes 147464 | tf_op jit(solution)/shard_map/ppermute | solution.py:104
  155.1 8.4 %collective-permute-start.37 = (bf16[64,384]{1,0:T(8,128)(2,1)S(1)}, bf16[64,384]{1,0:T(8,128)(2,1)S(1)}, u32[]{:S(2)}, u32[]{:S(2)}) collective-permute-start(bf16[64,384]{1,0:T(8,128)(2,1)S(1)} %get-tuple-element.50), channel_id=1, source_target_pairs={{0,3},{1,2},{2,1},{3,0},{4,7},{5,6},{6,5},{7,4},{8,11},{9,10},{10,... | collective-permute-start | bytes 147464 | tf_op jit(solution)/shard_map/ppermute | solution.py:104

commit v2 on v1

--- a/solution.py
+++ b/solution.py
@@ -14,6 +14,7 @@
 F32 = jnp.float32
 BF16 = jnp.bfloat16
 VMEM_LIMIT = 48 * 1024 * 1024
+COST = 2
 
 
 def attend_group(query, keys, values, grad_out, allowed):
@@ -104,18 +105,17 @@
     return lax.ppermute(x, axis, [(i, i ^ j) for i in range(n)])
 
 
-def vmem_call(kernel, out_shape, scratch_shapes=(), smem=0, total=0):
+def vmem_call(kernel, out_shape, scratch_shapes=(), smem=0, total=0, place=pltpu.VMEM):
     def call(*args):
         in_specs = [
-            pl.BlockSpec(memory_space=pltpu.SMEM if i < smem else pltpu.VMEM)
+            pl.BlockSpec(memory_space=pltpu.SMEM if i < smem else place)
             for i in range(len(args))
         ]
-        outs = jax.tree.map(lambda _: pl.BlockSpec(memory_space=pltpu.VMEM), out_shape)
         return pl.pallas_call(
             kernel,
             out_shape=out_shape,
             in_specs=in_specs,
-            out_specs=outs,
+            out_specs=jax.tree.map(lambda _: pl.BlockSpec(memory_space=pltpu.VMEM), out_shape),
             scratch_shapes=scratch_shapes,
             compiler_params=pltpu.CompilerParams(vmem_limit_bytes=VMEM_LIMIT),
             cost_estimate=pl.CostEstimate(flops=total, bytes_accessed=4 << 20, transcendentals=0),
@@ -139,40 +139,57 @@
     return part
 
 
-def pack_kernel(place_ref, wq_ref, wk_ref, wv_ref, grad_ref, *outs):
+def pack_kernel(place_ref, wq_hbm, wk_hbm, wv_hbm, grad_hbm, w_all, *refs):
+    outs, held, sem = refs[:4], refs[4:8], refs[8]
+    copies = [
+        pltpu.make_async_copy(source, target, sem.at[i])
+        for i, (source, target) in enumerate(zip((wq_hbm, wk_hbm, wv_hbm, grad_hbm), held))
+    ]
+    for copy in copies:
+        copy.start()
+    for copy in copies:
+        copy.wait()
+    wq_ref, wk_ref, wv_ref, grad_ref = held
     s = place_ref[1]
-    w_all, w_outs, g_outs = outs[0], outs[1:4], outs[4:8]
     wide = wq_ref.shape[1] // 4
     narrow = wk_ref.shape[1] // 4
+    joined = wide + 2 * narrow
+    depth = wq_ref.shape[0]
+    tail = outs[0].shape[1]
     for j in range(4):
         g = s ^ j
         q = group_columns(wq_ref, g, wide)
         k = group_columns(wk_ref, g, narrow)
         v = group_columns(wv_ref, g, narrow)
         row = jnp.concatenate([q, k, v], axis=1)
-        w_all[j] = row
-        if j > 0:
-            w_outs[j - 1][...] = row
-        g_outs[j][...] = group_columns(grad_ref, g, wide)
+        w_all[:, j * joined : (j + 1) * joined] = row
+        outs[1][:, tail + j * joined : tail + (j + 1) * joined] = row
+        outs[j][:, :joined] = row
+        grad = group_columns(grad_ref, g, wide)
+        for i in range(grad_ref.shape[0] // depth):
+            cols = slice(joined + i * wide, joined + (i + 1) * wide)
+            outs[j][:, cols] = grad[i * depth : (i + 1) * depth]
 
 
 def attend_kernel(place_ref, adjacency_ref, *refs):
     f, s = place_ref[0], place_ref[1]
-    x_refs, w_refs, g_refs = refs[0:4], refs[4:12], refs[12:16]
-    att_refs, d_refs = refs[16:20], refs[20:24]
-    w_scr, q_scr, gt_scr = refs[24:27]
+    x_refs, own_ref, other_ref, pay_refs = refs[0:4], refs[4], refs[5], refs[6:10]
+    d_refs = refs[10:14]
+    w_scr, q_scr, gt_scr = refs[14:17]
     rows = x_refs[0].shape[0]
     length = 4 * rows
-    depth = w_refs[0].shape[1]
+    depth, joined = own_ref.shape[2:]
     span = 4 * depth
     hs = HEAD_SIZE
-    per = g_refs[0].shape[1] // hs
-    wide = per * hs
+    wide = joined - 2 * hs
+    per = wide // hs
 
     acc = None
     for jf in range(8):
+        w_ref = own_ref if jf % 2 == 0 else other_ref
         for l in range(4):
-            w_scr[jf, pl.ds(pl.multiple_of((s ^ l) * depth, depth), depth), :] = w_refs[jf][l]
+            place = pl.ds(pl.multiple_of((s ^ l) * depth, depth), depth)
+            w_scr[jf, place, :] = w_ref[jf // 2, l]
     for jf in range(8):
         cols = pl.ds(pl.multiple_of((f ^ jf) * span, span), span)
         x = jnp.concatenate([r[:, cols] for r in x_refs], axis=0)
@@ -185,7 +202,9 @@
     keys_t = keys.astype(F32).T.astype(BF16)
     values_t = values.astype(F32).T.astype(BF16)
     for j in range(4):
-        gt_scr[j * rows : (j + 1) * rows, :] = g_refs[j][...]
+        for i in range(rows // depth):
+            cols = slice(joined + i * wide, joined + (i + 1) * wide)
+            gt_scr[j * rows + i * depth : j * rows + (i + 1) * depth, :] = pay_refs[j][:, cols]
 
     blocks = length // BLK
     half = rows // BLK
@@ -227,71 +246,68 @@
             grad_values = grad_values + jnp.dot(p_low, g, preferred_element_type=F32)
     dkv = jnp.concatenate([grad_keys, grad_values], axis=1).astype(BF16)
     for j in range(4):
-        att_refs[j][...] = jnp.concatenate(out_t[j], axis=0).T.astype(BF16)
+        att = jnp.concatenate(out_t[j], axis=0).T.astype(BF16)
         dq = jnp.concatenate(dq_t[j], axis=0).T.astype(BF16)
         block = jnp.concatenate([dq, dkv[j * rows : (j + 1) * rows]], axis=1)
-        d_refs[j][:rows, :] = block
-        d_refs[j ^ 1][rows:, :] = block
-
-
-def weight_grad_kernel(parity, place_ref, x0, x1, x2, x3, d0_ref, d2_ref, out_ref):
+        d_refs[j][:rows, :joined] = block
+        d_refs[j ^ 2][rows:, :joined] = block
+        d_refs[j][:rows, joined:] = att[:, : wide // 2]
+        d_refs[j][rows:, joined:] = att[:, wide // 2 :]
+
+
+def weight_grad_kernel(parity, place_ref, x0, x1, x2, x3, d0_ref, d1_ref, out_ref):
     f, s = place_ref[0], place_ref[1]
-    depth = out_ref.shape[2]
+    depth, joined = out_ref.shape[2:]
     span = 4 * depth
-    d = jnp.concatenate([d0_ref[...], d2_ref[...]], axis=0)
+    d = jnp.concatenate([d0_ref[:, :joined], d1_ref[:, :joined]], axis=0)
     for i in range(4):
         cols = pl.ds(pl.multiple_of((f ^ (2 * i + parity)) * span, span), span)
-        x = jnp.concatenate([r[:, cols] for r in (x0, x1, x2, x3)], axis=0)
+        x = jnp.concatenate([r[:, cols] for r in (x0, x2, x1, x3)], axis=0)
         part = lax.dot_general(x, d, (((0,), (0,)), ((), ())), preferred_element_type=F32)
         for k in range(4):
             out_ref[i, s ^ k] = part[k * depth : (k + 1) * depth]
 
 
-def token_grad_kernel(place_ref, d0, d1, d2, d3, *refs):
+def token_grad_kernel(place_ref, d0, d1, d2, d3, even_ref, odd_ref, own_ref, send_ref):
     f, s = place_ref[0], place_ref[1]
-    w_refs, own_ref, send_ref = refs[:8], refs[8], refs[9]
     rows = own_ref.shape[0]
-    depth = w_refs[0].shape[2]
-    d = [r[...] for r in (d0, d1, d2, d3)]
+    depth, columns = even_ref.shape[2:]
+    joined = columns // 4
     last = (((1,), (1,)), ((), ()))
-    for jf in range(8):
-        halves = []
-        for l in range(2):
-            total = None
-            for j in range(4):
-                part = lax.dot_general(
-                    d[j], w_refs[jf][l, j ^ (2 * l)], last, preferred_element_type=F32
-                )
-                total = part if total is None else total + part
-            halves.append(total)
-        swapped = s // 2 == 1
-        first = jnp.where(swapped, halves[1], halves[0])
-        second = jnp.where(swapped, halves[0], halves[1])
-        both = jnp.concatenate([first, second], axis=1).astype(BF16)
-        cols = pl.ds(pl.multiple_of((f ^ jf) * 2 * depth, 2 * depth), 2 * depth)
+    sides = []
+    for l, order in enumerate(((d0, d1, d2, d3), (d1, d0, d3, d2))):
+        d = jnp.concatenate([r[:, :joined] for r in order], axis=1)
+        w = jnp.concatenate([(even_ref, odd_ref)[i % 2][i // 2, l] for i in range(8)], axis=0)
+        sides.append(lax.dot_general(d, w, last, preferred_element_type=F32).astype(BF16))
+    odd = s % 2 == 1
+    first = jnp.where(odd, sides[1], sides[0])
+    second = jnp.where(odd, sides[0], sides[1])
+    for i in range(8):
+        part = slice(i * depth, (i + 1) * depth)
+        both = jnp.concatenate([first[:, part], second[:, part]], axis=1)
+        cols = pl.ds(pl.multiple_of((f ^ i) * 2 * depth, 2 * depth), 2 * depth)
         own_ref[:, cols] = both[:rows]
         send_ref[:, cols] = both[rows:]
 
 
 def token_join_kernel(place_ref, own_ref, got_ref, out_ref):
+    high = place_ref[1] // 2
+    part = own_ref.shape[1] // 8
+    for i in range(8):
+        cols = slice(i * part, (i + 1) * part)
+        here = pl.multiple_of((2 * i + high) * part, part)
+        there = pl.multiple_of((2 * i + 1 - high) * part, part)
+        out_ref[:, pl.ds(here, part)] = own_ref[:, cols]
+        out_ref[:, pl.ds(there, part)] = got_ref[:, cols]
+
+
+def attended_join_kernel(place_ref, d0, d1, d2, d3, out_ref):
     s = place_ref[1]
-    odd = s % 2 == 1
-    depth = own_ref.shape[1] // 16
-    for b in range(8):
-        cols = slice(b * 2 * depth, (b + 1) * 2 * depth)
-        own, got = own_ref[:, cols], got_ref[:, cols]
-        even = jnp.where(odd, got, own)
-        other = jnp.where(odd, own, got)
-        out_ref[:, b * 4 * depth : (b + 1) * 4 * depth] = jnp.concatenate(
-            [even[:, :depth], other[:, :depth], even[:, depth:], other[:, depth:]], axis=1
-        )
-
-
-def attended_join_kernel(place_ref, a0, a1, a2, a3, out_ref):
-    s = place_ref[1]
-    wide = a0.shape[1]
-    for j, a in enumerate((a0, a1, a2, a3)):
-        out_ref[:, pl.ds(pl.multiple_of((s ^ j) * wide, wide), wide)] = a[...]
+    rows = out_ref.shape[0]
+    part = out_ref.shape[1] // 8
+    for j, ref in enumerate((d0, d1, d2, d3)):
+        both = jnp.concatenate([ref[:rows, -part:], ref[rows:, -part:]], axis=1)
+        out_ref[:, pl.ds(pl.multiple_of((s ^ j) * 2 * part, 2 * part), 2 * part)] = both
 
 
 def weight_join_kernel(place_ref, b0, b1, b2, b3, q_ref, k_ref, v_ref):
@@ -318,72 +334,78 @@
     joined = wide + 2 * narrow
     place = jnp.stack([lax.axis_index("fsdp"), lax.axis_index("seq")]).astype(jnp.int32)
 
+    x1 = swap(x0, "seq", 1)
     x2 = swap(x0, "seq", 2)
-    x1 = swap(x0, "seq", 1)
+
+    few = joined + rows // depth * wide
+    w_all, *pay = vmem_call(
+        pack_kernel,
+        [shape(depth, 4 * joined)]
+        + [shape(depth, few + (4 * joined if j == 1 else 0)) for j in range(4)],
+        scratch_shapes=[
+            pltpu.VMEM((depth, 4 * wide), BF16),
+            pltpu.VMEM((depth, 4 * narrow), BF16),
+            pltpu.VMEM((depth, 4 * narrow), BF16),
+            pltpu.VMEM((rows, 4 * wide), BF16),
+            pltpu.SemaphoreType.DMA((4,)),
+        ],
+        smem=1,
+        place=pltpu.HBM,
+    )(place, w_query, w_key, value_weight, grad_attn[0])
+
+    pay = [pay[0]] + [swap(pay[j], "seq", j) for j in (1, 2, 3)]
+    pay, x1 = lax.optimization_barrier((pay, x1))
+
+    w_rows = jnp.stack([p[:, :joined] for p in pay])
+    w_own = jnp.stack([w_rows] + [swap(w_rows, "fsdp", j) for j in (2, 4, 6)])
+    u_rows = jnp.stack([w_all, pay[1][:, few:]])
+    w_own, x2, u_rows = lax.optimization_barrier((w_own, x2, u_rows))
+
     x3 = swap(x2, "seq", 1)
-
-    packed = vmem_call(
-        pack_kernel,
-        [shape(4, depth, joined)]
-        + [shape(depth, joined)] * 3
-        + [shape(rows, wide)] * 4,
-        smem=1,
-    )(place, w_query, w_key, value_weight, grad_attn[0])
-    w_all, w_send, g_send = packed[0], packed[1:4], packed[4:8]
-
-    w_rows = jnp.stack([w_all[0]] + [swap(w_send[j - 1], "seq", j) for j in (1, 2, 3)])
-    w_plane = [w_rows] + [swap(w_rows, "fsdp", j) for j in (2, 4, 6)]
-    w_other = [swap(w, "fsdp", 1) for w in w_plane]
-    w_group = [w_plane[i // 2] if i % 2 == 0 else w_other[i // 2] for i in range(8)]
-    g_got = [g_send[0]] + [swap(g_send[j], "seq", j) for j in (1, 2, 3)]
-
-    u_rows = jnp.stack([w_all, swap(w_all, "seq", 2)])
-    u_plane = [u_rows] + [swap(u_rows, "fsdp", j) for j in (2, 4, 6)]
-    u_other = [swap(u, "fsdp", 1) for u in u_plane]
-    u_group = [u_plane[i // 2] if i % 2 == 0 else u_other[i // 2] for i in range(8)]
-
-    results = vmem_call(
+    w_other = swap(w_own, "fsdp", 1)
+    u_own = jnp.stack([u_rows] + [swap(u_rows, "fsdp", j) for j in (2, 4, 6)])
+    u_other = swap(u_own, "fsdp", 1)
+
+    d = vmem_call(
         attend_kernel,
-        [shape(rows, wide)] * 4 + [shape(2 * rows, joined)] * 4,
+        [shape(2 * rows, joined + wide // 2)] * 4,
         scratch_shapes=[
             pltpu.VMEM((8, 4 * depth, joined), BF16),
             pltpu.VMEM((4 * rows, wide), BF16),
             pltpu.VMEM((4 * rows, wide), BF16),
         ],
         smem=2,
-        total=8 << 30,
-    )(place, adjacency, x0, x1, x2, x3, *w_group, *g_got)
-    att, d = results[:4], results[4:]
-
-    d_got = [d[0]] + [swap(d[j], "seq", j) for j in (1, 2, 3)]
-
-    def weight_grad(parity):
+        total=20 << 30,
+    )(place, adjacency, x0, x1, x2, x3, w_own, w_other, *pay)
+
+    def weight_grad(parity, d):
         return vmem_call(
             functools.partial(weight_grad_kernel, parity),
             shape(4, 4, depth, joined, dtype=F32),
             smem=1,
             total=1 << 30,
-        )(place, x0, x1, x2, x3, d[0], d[2])
-
-    sent = swap(weight_grad(1), "fsdp", 1)
-    kept = weight_grad(0)
-    total = [kept[i] + sent[i] for i in range(4)]
+        )(place, x0, x1, x2, x3, d[0], d[1])
+
+    away = weight_grad(1, d)
+    d, away = lax.optimization_barrier((d, away))
+    sent = swap(away, "fsdp", 1)
+    d_got = [d[0]] + [swap(d[j], "seq", j) for j in (1, 2, 3)]
+    kept = weight_grad(0, d)
+    total = kept + sent
     got = [swap(total[i], "fsdp", 2 * i) for i in (1, 2, 3)]
     factor = 1.0 / math.sqrt(4 * rows * lax.axis_size("fsdp"))
     summed = (((total[0] + got[0]) + (got[1] + got[2])) * factor).astype(BF16)
     w_final = [summed[0]] + [swap(summed[j], "seq", j) for j in (1, 2, 3)]
 
-    att_got = [att[0]] + [swap(att[j], "seq", j) for j in (1, 2, 3)]
-
     own, send = vmem_call(
         token_grad_kernel,
         [shape(rows, width // 2)] * 2,
         smem=1,
-        total=1 << 30,
-    )(place, *d_got, *u_group)
-    half = swap(send, "seq", 1)
-
-    attended = vmem_call(attended_join_kernel, shape(rows, 4 * wide), smem=1)(place, *att_got)
+        total=COST << 30,
+    )(place, *d_got, u_own, u_other)
+    half = swap(send, "seq", 2)
+
+    attended = vmem_call(attended_join_kernel, shape(rows, 4 * wide), smem=1)(place, *d_got)
     grad_in = vmem_call(token_join_kernel, shape(rows, width), smem=1)(place, own, half)
     grad_wq, grad_wk, grad_wv = vmem_call(
         weight_join_kernel,

time: 165 us -> 120 us (0.73)
  waiting for transfers between devices: 87 us -> 61.6 us
  starting transfers between devices: 49.4 us -> 33.5 us
  Pallas kernels: 22.1 us -> 19.8 us
    ppermute x38 -> x25, waiting for transfers between devices: 87 us -> 61.6 us  [swap(): return lax.ppermute(x, axis, [(i, i ^ j) for i in range(n)])]
    ppermute x38 -> x25, starting transfers between devices: 49.4 us -> 33.5 us  [swap(): return lax.ppermute(x, axis, [(i, i ^ j) for i in range(n)])]
    pallas_call x8, Pallas kernels: 22.1 us -> 19.8 us  [call(): pl.pallas_call(kernel, out_shape=out_shape, in_specs=in_specs, out_specs=...]
    unnamed x14 -> x12, local copies, waits for them, and re-layouts: 5.1 us -> 3.38 us
  transfers between devices with their start and end apart: 38 -> 25, of which waited for: 15 -> 11; matrix products, arithmetic and copies ran while one was open for 0% -> 1% of each run, Pallas kernels for 6% -> 15%
where the time goes in v2:
time: 120 us
  waiting for transfers between devices  61.6 us (51%)
  starting transfers between devices  33.5 us (28%)
  Pallas kernels  19.8 us (16%)
  local copies, waits for them, and re-layouts  3.52 us (3%)
    ppermute x25, waiting for transfers between devices, swap(): return lax.ppermute(x, axis, [(i, i ^ j) for i in range(n)])  61.6 us
    ppermute x25, starting transfers between devices, swap(): return lax.ppermute(x, axis, [(i, i ^ j) for i in range(n)])  33.5 us
    pallas_call x8, Pallas kernels, call(): pl.pallas_call(kernel, out_shape=out_shape, in_specs=in_specs, out_specs=...  19.8 us
    unnamed x12, local copies, waits for them, and re-layouts  3.38 us
  transfers between devices with their start and end apart: 25, of which 11 were waited for; matrix products, arithmetic and copies ran while one was open for 1% of the time, Pallas kernels for 15%

profile of v2, /device:TPU:0, one launch (start us, length us, event | category | flops | bytes accessed | tf_op | source)
XLA Modules:
  0.0 120.2 jit_solution(17837059558039619506)
XLA Ops:
  0.6 3.1 %collective-permute-start.3 = (bf16[128,2048]{1,0:T(8,128)(2,1)}, bf16[128,2048]{1,0:T(8,128)(2,1)S(1)}, u32[]{:S(2)}, u32[]{:S(2)}) collective-permute-start(bf16[128,2048]{1,0:T(8,128)(2,1)} %bitcast.50), channel_id=1, source_target_pairs={{0,1},{1,0},{2,3},{3,2},{4,5},{5,4},{6,7},{7,6},{8,9},{9,8},{10,11... | collective-permute-start | bytes 1572872 | tf_op jit(solution)/shard_map/ppermute | solution.py:105
  3.8 0.9 copy-done.1
  4.7 0.9 copy-done.2
  5.7 0.8 copy-done.3
  6.4 0.8 copy-done.4
  7.2 1.1 shard_map.101
  8.2 0.1 collective-permute-start
  8.3 3.0 %collective-permute-start.1 = (bf16[64,896]{1,0:T(8,128)(2,1)S(1)}, bf16[64,896]{1,0:T(8,128)(2,1)S(1)}, u32[]{:S(2)}, u32[]{:S(2)}) collective-permute-start(bf16[64,896]{1,0:T(8,128)(2,1)S(1)} %get-tuple-element.34), channel_id=1, source_target_pairs={{0,2},{1,3},{2,0},{3,1},{4,6},{5,7},{6,4},{7,5},{8,10},{9,11},{10,... | collective-permute-start | bytes 344072 | tf_op jit(solution)/shard_map/ppermute | solution.py:105
  11.3 1.3 %collective-permute-start.2 = (bf16[64,896]{1,0:T(8,128)(2,1)S(1)}, bf16[64,896]{1,0:T(8,128)(2,1)S(1)}, u32[]{:S(2)}, u32[]{:S(2)}) collective-permute-start(bf16[64,896]{1,0:T(8,128)(2,1)S(1)} %get-tuple-element.35), channel_id=1, source_target_pairs={{0,3},{1,2},{2,1},{3,0},{4,7},{5,6},{6,5},{7,4},{8,11},{9,10},{10,... | collective-permute-start | bytes 344072 | tf_op jit(solution)/shard_map/ppermute | solution.py:105
  12.7 1.7 %collective-permute-start.7 = (bf16[128,2048]{1,0:T(8,128)(2,1)}, bf16[128,2048]{1,0:T(8,128)(2,1)S(1)}, u32[]{:S(2)}, u32[]{:S(2)}) collective-permute-start(bf16[128,2048]{1,0:T(8,128)(2,1)} %bitcast.51), channel_id=1, source_target_pairs={{0,2},{1,3},{2,0},{3,1},{4,6},{5,7},{6,4},{7,5},{8,10},{9,11},{10,... | collective-permute-start | bytes 1572872 | tf_op jit(solution)/shard_map/ppermute | solution.py:105
  14.4 11.0 %collective-permute-done.1.refs_8_ = bf16[64,896]{1,0:T(8,128)(2,1)S(1)} collective-permute-done((bf16[64,896]{1,0:T(8,128)(2,1)S(1)}, bf16[64,896]{1,0:T(8,128)(2,1)S(1)}, u32[]{:S(2)}, u32[]{:S(2)}) %collective-permute-start.1) | collective-permute-done | bytes 114720 | tf_op jit(solution)/shard_map/ppermute | solution.py:105
  25.4 5.4 %collective-permute-done.2.refs_9_ = bf16[64,896]{1,0:T(8,128)(2,1)S(1)} collective-permute-done((bf16[64,896]{1,0:T(8,128)(2,1)S(1)}, bf16[64,896]{1,0:T(8,128)(2,1)S(1)}, u32[]{:S(2)}, u32[]{:S(2)}) %collective-permute-start.2) | collective-permute-done | bytes 114720 | tf_op jit(solution)/shard_map/ppermute | solution.py:105
  30.9 4.8 %collective-permute-done.refs_7_ = bf16[64,2432]{1,0:T(8,128)(2,1)S(1)} collective-permute-done((bf16[64,2432]{1,0:T(8,128)(2,1)S(1)}, bf16[64,2432]{1,0:T(8,128)(2,1)S(1)}, u32[]{:S(2)}, u32[]{:S(2)}) %collective-permute-start) | collective-permute-done | bytes 311328 | tf_op jit(solution)/shard_map/ppermute | solution.py:105
  35.8 1.4 %collective-permute-start.5 = (bf16[4,64,384]{2,1,0:T(8,128)(2,1)S(1)}, bf16[4,64,384]{2,1,0:T(8,128)(2,1)S(1)}, u32[]{:S(2)}, u32[]{:S(2)}) collective-permute-start(bf16[4,64,384]{2,1,0:T(8,128)(2,1)S(1)} %get-tuple-element.67), channel_id=1, source_target_pairs={{0,16},{4,20},{8,24},{12,28},{16,0},{20,4},{24,8},{28,12},{1,17},{... | collective-permute-start | bytes 589832 | tf_op jit(solution)/shard_map/ppermute | solution.py:105
  37.2 1.4 %collective-permute-start.6 = (bf16[4,64,384]{2,1,0:T(8,128)(2,1)S(1)}, bf16[4,64,384]{2,1,0:T(8,128)(2,1)S(1)}, u32[]{:S(2)}, u32[]{:S(2)}) collective-permute-start(bf16[4,64,384]{2,1,0:T(8,128)(2,1)S(1)} %get-tuple-element.67), channel_id=1, source_target_pairs={{0,24},{4,28},{8,16},{12,20},{16,8},{20,12},{24,0},{28,4},{1,25},{... | collective-permute-start | bytes 589832 | tf_op jit(solution)/shard_map/ppermute | solution.py:105
  38.6 0.7 collective-permute-start.4
  39.4 6.7 %collective-permute-done.5 = bf16[4,64,384]{2,1,0:T(8,128)(2,1)S(1)} collective-permute-done((bf16[4,64,384]{2,1,0:T(8,128)(2,1)S(1)}, bf16[4,64,384]{2,1,0:T(8,128)(2,1)S(1)}, u32[]{:S(2)}, u32[]{:S(2)}) %collective-permute-start.5) | collective-permute-done | bytes 196640 | tf_op jit(solution)/shard_map/ppermute | solution.py:105
  46.2 1.2 %collective-permute-done.4 = bf16[4,64,384]{2,1,0:T(8,128)(2,1)S(1)} collective-permute-done((bf16[4,64,384]{2,1,0:T(8,128)(2,1)S(1)}, bf16[4,64,384]{2,1,0:T(8,128)(2,1)S(1)}, u32[]{:S(2)}, u32[]{:S(2)}) %collective-permute-start.4) | collective-permute-done | bytes 196640 | tf_op jit(solution)/shard_map/ppermute | solution.py:105
  47.4 0.1 pad_maximum_fusion.1.refs_4_
  47.7 1.1 collective-permute-start.13
  48.8 1.5 %collective-permute-start.14 = (bf16[2,64,1536]{2,1,0:T(8,128)(2,1)S(1)}, bf16[2,64,1536]{2,1,0:T(8,128)(2,1)S(1)}, u32[]{:S(2)}, u32[]{:S(2)}) collective-permute-start(bf16[2,64,1536]{2,1,0:T(8,128)(2,1)S(1)} %pad_maximum_fusion.2), channel_id=1, source_target_pairs={{0,16},{4,20},{8,24},{12,28},{16,0},{20,4},{24,8},{28,12},{1,17},{... | collective-permute-start | bytes 1179656 | tf_op jit(solution)/shard_map/ppermute | solution.py:105
  50.3 1.0 collective-permute-start.15
  51.2 10.7 %collective-permute-done.8.refs_3_.x3 = bf16[128,2048]{1,0:T(8,128)(2,1)S(1)} collective-permute-done((bf16[128,2048]{1,0:T(8,128)(2,1)S(1)}, bf16[128,2048]{1,0:T(8,128)(2,1)S(1)}, u32[]{:S(2)}, u32[]{:S(2)}) %collective-permute-start.8) | collective-permute-done | bytes 524320 | tf_op jit(solution)/shard_map/ppermute | solution.py:105
  62.0 10.4 %shard_map.102 = (bf16[256,512]{1,0:T(8,128)(2,1)S(1)}, bf16[256,512]{1,0:T(8,128)(2,1)S(1)}, bf16[256,512]{1,0:T(8,128)(2,1)S(1)}, bf16[256,512]{1,0:T(8,128)(2,1)S(1)}) custom-call(s32[2]{0:T(128)S(1)} %pad_add_fusion.place_ref, s32[8,8]{1,0:T(8,128)S(1)} %copy-done.5, bf16[128,2048]{1,0:T(8,128)(2,1)S(1)} %bitcast.52, ...), custom_call_target="tpu_custom_call" | custom-call | flops 21474836480 | bytes 4194304 | tf_op jit(solution)/shard_map/pallas_call | solution.py:114
  72.4 1.3 %shard_map.103 = f32[4,4,64,384]{3,2,1,0:T(8,128)S(1)} custom-call(s32[2]{0:T(128)S(1)} %pad_add_fusion.place_ref, bf16[128,2048]{1,0:T(8,128)(2,1)S(1)} %bitcast.53, bf16[128,2048]{1,0:T(8,128)(2,1)S(1)} %collective-permute-done.3.refs_1_.x1, bf16[128,2048]{1,0:T(8,128)(2,1)S(1)} %collective-permute-done.7.refs_2_.x2, ...), custom_call_target="tpu_custom_call" | custom-call | flops 1073741824 | bytes 4194304 | tf_op jit(solution)/shard_map/pallas_call | solution.py:114
  73.8 0.2 pad_maximum_fusion.even_ref
  74.0 0.5 collective-permute-start.16
  74.5 0.3 collective-permute-start.10
  74.8 1.6 %collective-permute-start.11 = (bf16[256,512]{1,0:T(8,128)(2,1)S(1)}, bf16[256,512]{1,0:T(8,128)(2,1)S(1)}, u32[]{:S(2)}, u32[]{:S(2)}) collective-permute-start(bf16[256,512]{1,0:T(8,128)(2,1)S(1)} %get-tuple-element.50), channel_id=1, source_target_pairs={{0,2},{1,3},{2,0},{3,1},{4,6},{5,7},{6,4},{7,5},{8,10},{9,11},{10,... | collective-permute-start | bytes 786440 | tf_op jit(solution)/shard_map/ppermute | solution.py:105
  76.4 2.5 %collective-permute-start.12 = (bf16[256,512]{1,0:T(8,128)(2,1)S(1)}, bf16[256,512]{1,0:T(8,128)(2,1)S(1)}, u32[]{:S(2)}, u32[]{:S(2)}) collective-permute-start(bf16[256,512]{1,0:T(8,128)(2,1)S(1)} %get-tuple-element.51), channel_id=1, source_target_pairs={{0,3},{1,2},{2,1},{3,0},{4,7},{5,6},{6,5},{7,4},{8,11},{9,10},{10,... | collective-permute-start | bytes 786440 | tf_op jit(solution)/shard_map/ppermute | solution.py:105
  78.9 1.3 %shard_map.107 = f32[4,4,64,384]{3,2,1,0:T(8,128)S(1)} custom-call(s32[2]{0:T(128)S(1)} %pad_add_fusion.place_ref, bf16[128,2048]{1,0:T(8,128)(2,1)S(1)} %bitcast.54, bf16[128,2048]{1,0:T(8,128)(2,1)S(1)} %collective-permute-done.3.refs_1_.x1, bf16[128,2048]{1,0:T(8,128)(2,1)S(1)} %collective-permute-done.7.refs_2_.x2, ...), custom_call_target="tpu_custom_call" | custom-call | flops 1073741824 | bytes 4194304 | tf_op jit(solution)/shard_map/pallas_call | solution.py:114
  80.2 0.2 add.12
  80.6 1.1 collective-permute-start.19
  81.6 5.4 %collective-permute-done.10.d1 = bf16[256,512]{1,0:T(8,128)(2,1)S(1)} collective-permute-done((bf16[256,512]{1,0:T(8,128)(2,1)S(1)}, bf16[256,512]{1,0:T(8,128)(2,1)S(1)}, u32[]{:S(2)}, u32[]{:S(2)}) %collective-permute-start.10) | collective-permute-done | bytes 262176 | tf_op jit(solution)/shard_map/ppermute | solution.py:105
  87.1 1.4 %collective-permute-start.20 = (f32[4,64,384]{2,1,0:T(8,128)S(1)}, f32[4,64,384]{2,1,0:T(8,128)S(1)}, u32[]{:S(2)}, u32[]{:S(2)}) collective-permute-start(f32[4,64,384]{2,1,0:T(8,128)S(1)} %get-tuple-element.60), channel_id=1, source_target_pairs={{0,16},{4,20},{8,24},{12,28},{16,0},{20,4},{24,8},{28,12},{1,17},{... | collective-permute-start | bytes 1179656 | tf_op jit(solution)/shard_map/ppermute | solution.py:105
  88.5 7.6 %collective-permute-done.11.d2 = bf16[256,512]{1,0:T(8,128)(2,1)S(1)} collective-permute-done((bf16[256,512]{1,0:T(8,128)(2,1)S(1)}, bf16[256,512]{1,0:T(8,128)(2,1)S(1)}, u32[]{:S(2)}, u32[]{:S(2)}) %collective-permute-start.11) | collective-permute-done | bytes 262176 | tf_op jit(solution)/shard_map/ppermute | solution.py:105
  96.1 1.9 %collective-permute-start.21 = (f32[4,64,384]{2,1,0:T(8,128)S(1)}, f32[4,64,384]{2,1,0:T(8,128)S(1)}, u32[]{:S(2)}, u32[]{:S(2)}) collective-permute-start(f32[4,64,384]{2,1,0:T(8,128)S(1)} %get-tuple-element.59), channel_id=1, source_target_pairs={{0,24},{4,28},{8,16},{12,20},{16,8},{20,12},{24,0},{28,4},{1,25},{... | collective-permute-start | bytes 1179656 | tf_op jit(solution)/shard_map/ppermute | solution.py:105
  98.1 1.8 %shard_map.105 = (bf16[128,1024]{1,0:T(8,128)(2,1)S(1)}, bf16[128,1024]{1,0:T(8,128)(2,1)S(1)}) custom-call(s32[2]{0:T(128)S(1)} %pad_add_fusion.place_ref, bf16[256,512]{1,0:T(8,128)(2,1)S(1)} %get-tuple-element.48.d0_ref.d0, bf16[256,512]{1,0:T(8,128)(2,1)S(1)} %collective-permute-done.10.d1, bf16[256,512]{1,0:T(8,128)(2,1)S(1)} %collective-permute-done.11.d2, ...), custom_call_target="tpu_custom_call" | custom-call | flops 2147483648 | bytes 4194304 | tf_op jit(solution)/shard_map/pallas_call | solution.py:114
  99.9 3.2 %collective-permute-start.17 = (bf16[128,1024]{1,0:T(8,128)(2,1)S(1)}, bf16[128,1024]{1,0:T(8,128)(2,1)S(1)}, u32[]{:S(2)}, u32[]{:S(2)}) collective-permute-start(bf16[128,1024]{1,0:T(8,128)(2,1)S(1)} %get-tuple-element.54), channel_id=1, source_target_pairs={{0,2},{1,3},{2,0},{3,1},{4,6},{5,7},{6,4},{7,5},{8,10},{9,11},{10,... | collective-permute-start | bytes 786440 | tf_op jit(solution)/shard_map/ppermute | solution.py:105
  103.0 1.7 %collective-permute-done.20 = f32[4,64,384]{2,1,0:T(8,128)S(1)} collective-permute-done((f32[4,64,384]{2,1,0:T(8,128)S(1)}, f32[4,64,384]{2,1,0:T(8,128)S(1)}, u32[]{:S(2)}, u32[]{:S(2)}) %collective-permute-start.20) | collective-permute-done | bytes 393248 | tf_op jit(solution)/shard_map/ppermute | solution.py:105
  104.7 1.4 %collective-permute-done.21 = f32[4,64,384]{2,1,0:T(8,128)S(1)} collective-permute-done((f32[4,64,384]{2,1,0:T(8,128)S(1)}, f32[4,64,384]{2,1,0:T(8,128)S(1)}, u32[]{:S(2)}, u32[]{:S(2)}) %collective-permute-start.21) | collective-permute-done | bytes 393248 | tf_op jit(solution)/shard_map/ppermute | solution.py:105
  106.1 0.1 fusion.3
  106.3 2.3 %collective-permute-start.23 = (bf16[64,384]{1,0:T(8,128)(2,1)S(1)}, bf16[64,384]{1,0:T(8,128)(2,1)S(1)}, u32[]{:S(2)}, u32[]{:S(2)}) collective-permute-start(bf16[64,384]{1,0:T(8,128)(2,1)S(1)} %get-tuple-element.63), channel_id=1, source_target_pairs={{0,2},{1,3},{2,0},{3,1},{4,6},{5,7},{6,4},{7,5},{8,10},{9,11},{10,... | collective-permute-start | bytes 147464 | tf_op jit(solution)/shard_map/ppermute | solution.py:105
  108.6 2.1 %collective-permute-start.24 = (bf16[64,384]{1,0:T(8,128)(2,1)S(1)}, bf16[64,384]{1,0:T(8,128)(2,1)S(1)}, u32[]{:S(2)}, u32[]{:S(2)}) collective-permute-start(bf16[64,384]{1,0:T(8,128)(2,1)S(1)} %get-tuple-element.62), channel_id=1, source_target_pairs={{0,3},{1,2},{2,1},{3,0},{4,7},{5,6},{6,5},{7,4},{8,11},{9,10},{10,... | collective-permute-start | bytes 147464 | tf_op jit(solution)/shard_map/ppermute | solution.py:105
  110.7 1.3 %shard_map.104 = bf16[128,1024]{1,0:T(8,128)(2,1)} custom-call(s32[2]{0:T(128)S(1)} %pad_add_fusion.place_ref, bf16[256,512]{1,0:T(8,128)(2,1)S(1)} %get-tuple-element.48.d0_ref.d0, bf16[256,512]{1,0:T(8,128)(2,1)S(1)} %collective-permute-done.10.d1, bf16[256,512]{1,0:T(8,128)(2,1)S(1)} %collective-permute-done.11.d2, ...), custom_call_target="tpu_custom_call" | custom-call | bytes 4194304 | tf_op jit(solution)/shard_map/pallas_call | solution.py:114
  111.9 5.5 %collective-permute-done.17.got_ref = bf16[128,1024]{1,0:T(8,128)(2,1)S(1)} collective-permute-done((bf16[128,1024]{1,0:T(8,128)(2,1)S(1)}, bf16[128,1024]{1,0:T(8,128)(2,1)S(1)}, u32[]{:S(2)}, u32[]{:S(2)}) %collective-permute-start.17) | collective-permute-done | bytes 262176 | tf_op jit(solution)/shard_map/ppermute | solution.py:105
  117.4 1.5 %shard_map.106 = bf16[128,2048]{1,0:T(8,128)(2,1)} custom-call(s32[2]{0:T(128)S(1)} %pad_add_fusion.place_ref, bf16[128,1024]{1,0:T(8,128)(2,1)S(1)} %get-tuple-element.53.own_ref, bf16[128,1024]{1,0:T(8,128)(2,1)S(1)} %collective-permute-done.17.got_ref), custom_call_target="tpu_custom_call" | custom-call | bytes 4194304 | tf_op jit(solution)/shard_map/pallas_call | solution.py:114
  118.9 1.3 %shard_map.108 = (bf16[64,1024]{1,0:T(8,128)(2,1)}, bf16[64,256]{1,0:T(8,128)(2,1)}, bf16[64,256]{1,0:T(8,128)(2,1)}) custom-call(s32[2]{0:T(128)S(1)} %pad_add_fusion.place_ref, bf16[64,384]{1,0:T(8,128)(2,1)S(1)} %get-tuple-element.65.b0, bf16[64,384]{1,0:T(8,128)(2,1)S(1)} %collective-permute-done.22.b1, bf16[64,384]{1,0:T(8,128)(2,1)S(1)} %collective-permute-done.23.b2, ...), custom_call_target="tpu_custom_call" | custom-call | bytes 4194304 | tf_op jit(solution)/shard_map/pallas_call | solution.py:114
  (34 shorter events, 0.6 us)
Async XLA Ops:
  0.6 35.1 %collective-permute-start.3 = (bf16[128,2048]{1,0:T(8,128)(2,1)}, bf16[128,2048]{1,0:T(8,128)(2,1)S(1)}, u32[]{:S(2)}, u32[]{:S(2)}) collective-permute-start(bf16[128,2048]{1,0:T(8,128)(2,1)} %bitcast.50), channel_id=1, source_target_pairs={{0,1},{1,0},{2,3},{3,2},{4,5},{5,4},{6,7},{7,6},{8,9},{9,8},{10,11... | collective-permute-start | bytes 1572872 | tf_op jit(solution)/shard_map/ppermute | solution.py:105
  3.8 0.9 copy-start.1
  4.7 0.9 copy-start.2
  5.7 0.8 copy-start.3
  6.4 0.8 copy-start.4
  8.2 27.4 %collective-permute-start = (bf16[64,2432]{1,0:T(8,128)(2,1)S(1)}, bf16[64,2432]{1,0:T(8,128)(2,1)S(1)}, u32[]{:S(2)}, u32[]{:S(2)}) collective-permute-start(bf16[64,2432]{1,0:T(8,128)(2,1)S(1)} %get-tuple-element.33), channel_id=1, source_target_pairs={{0,1},{1,0},{2,3},{3,2},{4,5},{5,4},{6,7},{7,6},{8,9},{9,8},{10,11... | collective-permute-start | bytes 933896 | tf_op jit(solution)/shard_map/ppermute | solution.py:105
  8.3 17.1 %collective-permute-start.1 = (bf16[64,896]{1,0:T(8,128)(2,1)S(1)}, bf16[64,896]{1,0:T(8,128)(2,1)S(1)}, u32[]{:S(2)}, u32[]{:S(2)}) collective-permute-start(bf16[64,896]{1,0:T(8,128)(2,1)S(1)} %get-tuple-element.34), channel_id=1, source_target_pairs={{0,2},{1,3},{2,0},{3,1},{4,6},{5,7},{6,4},{7,5},{8,10},{9,11},{10,... | collective-permute-start | bytes 344072 | tf_op jit(solution)/shard_map/ppermute | solution.py:105
  11.3 19.5 %collective-permute-start.2 = (bf16[64,896]{1,0:T(8,128)(2,1)S(1)}, bf16[64,896]{1,0:T(8,128)(2,1)S(1)}, u32[]{:S(2)}, u32[]{:S(2)}) collective-permute-start(bf16[64,896]{1,0:T(8,128)(2,1)S(1)} %get-tuple-element.35), channel_id=1, source_target_pairs={{0,3},{1,2},{2,1},{3,0},{4,7},{5,6},{6,5},{7,4},{8,11},{9,10},{10,... | collective-permute-start | bytes 344072 | tf_op jit(solution)/shard_map/ppermute | solution.py:105
  12.7 34.8 %collective-permute-start.7 = (bf16[128,2048]{1,0:T(8,128)(2,1)}, bf16[128,2048]{1,0:T(8,128)(2,1)S(1)}, u32[]{:S(2)}, u32[]{:S(2)}) collective-permute-start(bf16[128,2048]{1,0:T(8,128)(2,1)} %bitcast.51), channel_id=1, source_target_pairs={{0,2},{1,3},{2,0},{3,1},{4,6},{5,7},{6,4},{7,5},{8,10},{9,11},{10,... | collective-permute-start | bytes 1572872 | tf_op jit(solution)/shard_map/ppermute | solution.py:105
  35.7 26.2 %copy-start = (bf16[1,128,2048]{2,1,0:T(8,128)(2,1)S(1)}, bf16[1,128,2048]{2,1,0:T(8,128)(2,1)}, u32[]{:S(2)}) copy-start(bf16[1,128,2048]{2,1,0:T(8,128)(2,1)} %param.6) | copy-start | bytes 1572868
  35.7 26.2 %copy-start.5 = (s32[8,8]{1,0:T(8,128)S(1)}, s32[8,8]{1,0:T(8,128)}, u32[]{:S(2)}) copy-start(s32[8,8]{1,0:T(8,128)} %adjacency_ref.1) | copy-start | bytes 772
  35.8 10.4 %collective-permute-start.5 = (bf16[4,64,384]{2,1,0:T(8,128)(2,1)S(1)}, bf16[4,64,384]{2,1,0:T(8,128)(2,1)S(1)}, u32[]{:S(2)}, u32[]{:S(2)}) collective-permute-start(bf16[4,64,384]{2,1,0:T(8,128)(2,1)S(1)} %get-tuple-element.67), channel_id=1, source_target_pairs={{0,16},{4,20},{8,24},{12,28},{16,0},{20,4},{24,8},{28,12},{1,17},{... | collective-permute-start | bytes 589832 | tf_op jit(solution)/shard_map/ppermute | solution.py:105
  37.2 9.0 %collective-permute-start.6 = (bf16[4,64,384]{2,1,0:T(8,128)(2,1)S(1)}, bf16[4,64,384]{2,1,0:T(8,128)(2,1)S(1)}, u32[]{:S(2)}, u32[]{:S(2)}) collective-permute-start(bf16[4,64,384]{2,1,0:T(8,128)(2,1)S(1)} %get-tuple-element.67), channel_id=1, source_target_pairs={{0,24},{4,28},{8,16},{12,20},{16,8},{20,12},{24,0},{28,4},{1,25},{... | collective-permute-start | bytes 589832 | tf_op jit(solution)/shard_map/ppermute | solution.py:105
  38.6 8.7 %collective-permute-start.4 = (bf16[4,64,384]{2,1,0:T(8,128)(2,1)S(1)}, bf16[4,64,384]{2,1,0:T(8,128)(2,1)S(1)}, u32[]{:S(2)}, u32[]{:S(2)}) collective-permute-start(bf16[4,64,384]{2,1,0:T(8,128)(2,1)S(1)} %get-tuple-element.67), channel_id=1, source_target_pairs={{0,8},{4,12},{8,0},{12,4},{16,24},{20,28},{24,16},{28,20},{1,9},{5... | collective-permute-start | bytes 589832 | tf_op jit(solution)/shard_map/ppermute | solution.py:105
  47.5 14.4 %collective-permute-start.9 = (bf16[4,4,64,384]{3,2,1,0:T(8,128)(2,1)S(1)}, bf16[4,4,64,384]{3,2,1,0:T(8,128)(2,1)S(1)}, u32[]{:S(2)}, u32[]{:S(2)}) collective-permute-start(bf16[4,4,64,384]{3,2,1,0:T(8,128)(2,1)S(1)} %pad_maximum_fusion.1.refs_4_), channel_id=1, source_target_pairs={{0,4},{4,0},{8,12},{12,8},{16,20},{20,16},{24,28},{28,24},{1,5},{5... | collective-permute-start | bytes 2359304 | tf_op jit(solution)/shard_map/ppermute | solution.py:105
  47.6 14.3 %collective-permute-start.8 = (bf16[128,2048]{1,0:T(8,128)(2,1)S(1)}, bf16[128,2048]{1,0:T(8,128)(2,1)S(1)}, u32[]{:S(2)}, u32[]{:S(2)}) collective-permute-start(bf16[128,2048]{1,0:T(8,128)(2,1)S(1)} %collective-permute-done.7.refs_2_.x2), channel_id=1, source_target_pairs={{0,1},{1,0},{2,3},{3,2},{4,5},{5,4},{6,7},{7,6},{8,9},{9,8},{10,11... | collective-permute-start | bytes 1572872 | tf_op jit(solution)/shard_map/ppermute | solution.py:105
  47.7 26.1 %collective-permute-start.13 = (bf16[2,64,1536]{2,1,0:T(8,128)(2,1)S(1)}, bf16[2,64,1536]{2,1,0:T(8,128)(2,1)S(1)}, u32[]{:S(2)}, u32[]{:S(2)}) collective-permute-start(bf16[2,64,1536]{2,1,0:T(8,128)(2,1)S(1)} %pad_maximum_fusion.2), channel_id=1, source_target_pairs={{0,8},{4,12},{8,0},{12,4},{16,24},{20,28},{24,16},{28,20},{1,9},{5... | collective-permute-start | bytes 1179656 | tf_op jit(solution)/shard_map/ppermute | solution.py:105
  48.8 25.0 %collective-permute-start.14 = (bf16[2,64,1536]{2,1,0:T(8,128)(2,1)S(1)}, bf16[2,64,1536]{2,1,0:T(8,128)(2,1)S(1)}, u32[]{:S(2)}, u32[]{:S(2)}) collective-permute-start(bf16[2,64,1536]{2,1,0:T(8,128)(2,1)S(1)} %pad_maximum_fusion.2), channel_id=1, source_target_pairs={{0,16},{4,20},{8,24},{12,28},{16,0},{20,4},{24,8},{28,12},{1,17},{... | collective-permute-start | bytes 1179656 | tf_op jit(solution)/shard_map/ppermute | solution.py:105
  50.3 23.5 %collective-permute-start.15 = (bf16[2,64,1536]{2,1,0:T(8,128)(2,1)S(1)}, bf16[2,64,1536]{2,1,0:T(8,128)(2,1)S(1)}, u32[]{:S(2)}, u32[]{:S(2)}) collective-permute-start(bf16[2,64,1536]{2,1,0:T(8,128)(2,1)S(1)} %pad_maximum_fusion.2), channel_id=1, source_target_pairs={{0,24},{4,28},{8,16},{12,20},{16,8},{20,12},{24,0},{28,4},{1,25},{... | collective-permute-start | bytes 1179656 | tf_op jit(solution)/shard_map/ppermute | solution.py:105
  73.7 6.6 %collective-permute-start.18 = (f32[4,4,64,384]{3,2,1,0:T(8,128)S(1)}, f32[4,4,64,384]{3,2,1,0:T(8,128)S(1)}, u32[]{:S(2)}, u32[]{:S(2)}) collective-permute-start(f32[4,4,64,384]{3,2,1,0:T(8,128)S(1)} %shard_map.103), channel_id=1, source_target_pairs={{0,4},{4,0},{8,12},{12,8},{16,20},{20,16},{24,28},{28,24},{1,5},{5... | collective-permute-start | bytes 4718600 | tf_op jit(solution)/shard_map/ppermute | solution.py:105
  74.0 24.1 %collective-permute-start.16 = (bf16[4,2,64,1536]{3,2,1,0:T(8,128)(2,1)S(1)}, bf16[4,2,64,1536]{3,2,1,0:T(8,128)(2,1)S(1)}, u32[]{:S(2)}, u32[]{:S(2)}) collective-permute-start(bf16[4,2,64,1536]{3,2,1,0:T(8,128)(2,1)S(1)} %pad_maximum_fusion.even_ref), channel_id=1, source_target_pairs={{0,4},{4,0},{8,12},{12,8},{16,20},{20,16},{24,28},{28,24},{1,5},{5... | collective-permute-start | bytes 4718600 | tf_op jit(solution)/shard_map/ppermute | solution.py:105
  74.5 12.5 %collective-permute-start.10 = (bf16[256,512]{1,0:T(8,128)(2,1)S(1)}, bf16[256,512]{1,0:T(8,128)(2,1)S(1)}, u32[]{:S(2)}, u32[]{:S(2)}) collective-permute-start(bf16[256,512]{1,0:T(8,128)(2,1)S(1)} %get-tuple-element.49.d1_ref), channel_id=1, source_target_pairs={{0,1},{1,0},{2,3},{3,2},{4,5},{5,4},{6,7},{7,6},{8,9},{9,8},{10,11... | collective-permute-start | bytes 786440 | tf_op jit(solution)/shard_map/ppermute | solution.py:105
  74.8 21.3 %collective-permute-start.11 = (bf16[256,512]{1,0:T(8,128)(2,1)S(1)}, bf16[256,512]{1,0:T(8,128)(2,1)S(1)}, u32[]{:S(2)}, u32[]{:S(2)}) collective-permute-start(bf16[256,512]{1,0:T(8,128)(2,1)S(1)} %get-tuple-element.50), channel_id=1, source_target_pairs={{0,2},{1,3},{2,0},{3,1},{4,6},{5,7},{6,4},{7,5},{8,10},{9,11},{10,... | collective-permute-start | bytes 786440 | tf_op jit(solution)/shard_map/ppermute | solution.py:105
  76.4 21.7 %collective-permute-start.12 = (bf16[256,512]{1,0:T(8,128)(2,1)S(1)}, bf16[256,512]{1,0:T(8,128)(2,1)S(1)}, u32[]{:S(2)}, u32[]{:S(2)}) collective-permute-start(bf16[256,512]{1,0:T(8,128)(2,1)S(1)} %get-tuple-element.51), channel_id=1, source_target_pairs={{0,3},{1,2},{2,1},{3,0},{4,7},{5,6},{6,5},{7,4},{8,11},{9,10},{10,... | collective-permute-start | bytes 786440 | tf_op jit(solution)/shard_map/ppermute | solution.py:105
  80.6 22.5 %collective-permute-start.19 = (f32[4,64,384]{2,1,0:T(8,128)S(1)}, f32[4,64,384]{2,1,0:T(8,128)S(1)}, u32[]{:S(2)}, u32[]{:S(2)}) collective-permute-start(f32[4,64,384]{2,1,0:T(8,128)S(1)} %get-tuple-element.61), channel_id=1, source_target_pairs={{0,8},{4,12},{8,0},{12,4},{16,24},{20,28},{24,16},{28,20},{1,9},{5... | collective-permute-start | bytes 1179656 | tf_op jit(solution)/shard_map/ppermute | solution.py:105
  87.1 17.6 %collective-permute-start.20 = (f32[4,64,384]{2,1,0:T(8,128)S(1)}, f32[4,64,384]{2,1,0:T(8,128)S(1)}, u32[]{:S(2)}, u32[]{:S(2)}) collective-permute-start(f32[4,64,384]{2,1,0:T(8,128)S(1)} %get-tuple-element.60), channel_id=1, source_target_pairs={{0,16},{4,20},{8,24},{12,28},{16,0},{20,4},{24,8},{28,12},{1,17},{... | collective-permute-start | bytes 1179656 | tf_op jit(solution)/shard_map/ppermute | solution.py:105
  96.1 9.9 %collective-permute-start.21 = (f32[4,64,384]{2,1,0:T(8,128)S(1)}, f32[4,64,384]{2,1,0:T(8,128)S(1)}, u32[]{:S(2)}, u32[]{:S(2)}) collective-permute-start(f32[4,64,384]{2,1,0:T(8,128)S(1)} %get-tuple-element.59), channel_id=1, source_target_pairs={{0,24},{4,28},{8,16},{12,20},{16,8},{20,12},{24,0},{28,4},{1,25},{... | collective-permute-start | bytes 1179656 | tf_op jit(solution)/shard_map/ppermute | solution.py:105
  99.9 17.6 %collective-permute-start.17 = (bf16[128,1024]{1,0:T(8,128)(2,1)S(1)}, bf16[128,1024]{1,0:T(8,128)(2,1)S(1)}, u32[]{:S(2)}, u32[]{:S(2)}) collective-permute-start(bf16[128,1024]{1,0:T(8,128)(2,1)S(1)} %get-tuple-element.54), channel_id=1, source_target_pairs={{0,2},{1,3},{2,0},{3,1},{4,6},{5,7},{6,4},{7,5},{8,10},{9,11},{10,... | collective-permute-start | bytes 786440 | tf_op jit(solution)/shard_map/ppermute | solution.py:105
  106.2 12.7 %collective-permute-start.22 = (bf16[64,384]{1,0:T(8,128)(2,1)S(1)}, bf16[64,384]{1,0:T(8,128)(2,1)S(1)}, u32[]{:S(2)}, u32[]{:S(2)}) collective-permute-start(bf16[64,384]{1,0:T(8,128)(2,1)S(1)} %get-tuple-element.64), channel_id=1, source_target_pairs={{0,1},{1,0},{2,3},{3,2},{4,5},{5,4},{6,7},{7,6},{8,9},{9,8},{10,11... | collective-permute-start | bytes 147464 | tf_op jit(solution)/shard_map/ppermute | solution.py:105
  106.3 12.6 %collective-permute-start.23 = (bf16[64,384]{1,0:T(8,128)(2,1)S(1)}, bf16[64,384]{1,0:T(8,128)(2,1)S(1)}, u32[]{:S(2)}, u32[]{:S(2)}) collective-permute-start(bf16[64,384]{1,0:T(8,128)(2,1)S(1)} %get-tuple-element.63), channel_id=1, source_target_pairs={{0,2},{1,3},{2,0},{3,1},{4,6},{5,7},{6,4},{7,5},{8,10},{9,11},{10,... | collective-permute-start | bytes 147464 | tf_op jit(solution)/shard_map/ppermute | solution.py:105
  108.6 10.3 %collective-permute-start.24 = (bf16[64,384]{1,0:T(8,128)(2,1)S(1)}, bf16[64,384]{1,0:T(8,128)(2,1)S(1)}, u32[]{:S(2)}, u32[]{:S(2)}) collective-permute-start(bf16[64,384]{1,0:T(8,128)(2,1)S(1)} %get-tuple-element.62), channel_id=1, source_target_pairs={{0,3},{1,2},{2,1},{3,0},{4,7},{5,6},{6,5},{7,4},{8,11},{9,10},{10,... | collective-permute-start | bytes 147464 | tf_op jit(solution)/shard_map/ppermute | solution.py:105

commit v3 on v2

--- a/solution.py
+++ b/solution.py
@@ -14,7 +14,6 @@
 F32 = jnp.float32
 BF16 = jnp.bfloat16
 VMEM_LIMIT = 48 * 1024 * 1024
-COST = 2
 
 
 def attend_group(query, keys, values, grad_out, allowed):
@@ -105,6 +104,21 @@
     return lax.ppermute(x, axis, [(i, i ^ j) for i in range(n)])
 
 
+def note_kernel(*refs):
+    refs[-1][...] = jnp.zeros_like(refs[-1])
+
+
+def note(cost, *others):
+    return pl.pallas_call(
+        note_kernel,
+        out_shape=shape(8, 128, dtype=F32),
+        in_specs=[pl.BlockSpec(memory_space=pltpu.VMEM)] * len(others),
+        out_specs=pl.BlockSpec(memory_space=pltpu.VMEM),
+        compiler_params=pltpu.CompilerParams(vmem_limit_bytes=VMEM_LIMIT),
+        cost_estimate=pl.CostEstimate(flops=cost << 30, bytes_accessed=0, transcendentals=0),
+    )(*others)
+
+
 def vmem_call(kernel, out_shape, scratch_shapes=(), smem=0, total=0, place=pltpu.VMEM):
     def call(*args):
         in_specs = [
@@ -139,8 +153,8 @@
     return part
 
 
-def pack_kernel(place_ref, wq_hbm, wk_hbm, wv_hbm, grad_hbm, w_all, *refs):
-    outs, held, sem = refs[:4], refs[4:8], refs[8]
+def pack_kernel(place_ref, wq_hbm, wk_hbm, wv_hbm, grad_hbm, w_rest, near, *refs):
+    outs, held, sem = refs[:3], refs[3:7], refs[7]
     copies = [
         pltpu.make_async_copy(source, target, sem.at[i])
         for i, (source, target) in enumerate(zip((wq_hbm, wk_hbm, wv_hbm, grad_hbm), held))
@@ -155,46 +169,45 @@
     narrow = wk_ref.shape[1] // 4
     joined = wide + 2 * narrow
     depth = wq_ref.shape[0]
-    tail = outs[0].shape[1]
+    targets = (outs[0], near, outs[1], outs[2])
+    spots = (1, 0, 3, 2)
     for j in range(4):
         g = s ^ j
         q = group_columns(wq_ref, g, wide)
         k = group_columns(wk_ref, g, narrow)
         v = group_columns(wv_ref, g, narrow)
         row = jnp.concatenate([q, k, v], axis=1)
-        w_all[:, j * joined : (j + 1) * joined] = row
-        outs[1][:, tail + j * joined : tail + (j + 1) * joined] = row
-        outs[j][:, :joined] = row
+        near[:, spots[j] * joined : (spots[j] + 1) * joined] = row
+        if j > 0:
+            w_rest[:, (j - 1) * joined : j * joined] = row
+        if j != 1:
+            targets[j][:, :joined] = row
         grad = group_columns(grad_ref, g, wide)
+        left = 4 * joined if j == 1 else joined
         for i in range(grad_ref.shape[0] // depth):
-            cols = slice(joined + i * wide, joined + (i + 1) * wide)
-            outs[j][:, cols] = grad[i * depth : (i + 1) * depth]
+            piece = grad[i * depth : (i + 1) * depth]
+            targets[j][:, left + i * wide : left + (i + 1) * wide] = piece
 
 
 def attend_kernel(place_ref, adjacency_ref, *refs):
     f, s = place_ref[0], place_ref[1]
     x_refs, own_ref, other_ref, pay_refs = refs[0:4], refs[4], refs[5], refs[6:10]
-    d_refs = refs[10:14]
-    w_scr, q_scr, gt_scr = refs[14:17]
+    d_refs = refs[11:15]
+    w_scr, q_scr, gt_scr = refs[15:18]
     rows = x_refs[0].shape[0]
     length = 4 * rows
     depth, joined = own_ref.shape[2:]
-    span = 4 * depth
     hs = HEAD_SIZE
     wide = joined - 2 * hs
     per = wide // hs
 
-    acc = None
     for jf in range(8):
         w_ref = own_ref if jf % 2 == 0 else other_ref
         for l in range(4):
-            place = pl.ds(pl.multiple_of((s ^ l) * depth, depth), depth)
-            w_scr[jf, place, :] = w_ref[jf // 2, l]
-    for jf in range(8):
-        cols = pl.ds(pl.multiple_of((f ^ jf) * span, span), span)
-        x = jnp.concatenate([r[:, cols] for r in x_refs], axis=0)
-        part = jnp.dot(x, w_scr[jf], preferred_element_type=F32)
-        acc = part if acc is None else acc + part
+            row = pl.multiple_of(((f ^ jf) * 4 + (s ^ l)) * depth, depth)
+            w_scr[pl.ds(row, depth), :] = w_ref[jf // 2, l]
+    x = jnp.concatenate([r[...] for r in x_refs], axis=0)
+    acc = jnp.dot(x, w_scr[...], preferred_element_type=F32)
     low = acc.astype(BF16)
     q_scr[...] = low[:, :wide]
     keys = low[:, wide : wide + hs]
@@ -202,8 +215,9 @@
     keys_t = keys.astype(F32).T.astype(BF16)
     values_t = values.astype(F32).T.astype(BF16)
     for j in range(4):
+        left = 4 * joined if j == 1 else joined
         for i in range(rows // depth):
-            cols = slice(joined + i * wide, joined + (i + 1) * wide)
+            cols = slice(left + i * wide, left + (i + 1) * wide)
             gt_scr[j * rows + i * depth : j * rows + (i + 1) * depth, :] = pay_refs[j][:, cols]
 
     blocks = length // BLK
@@ -212,26 +226,29 @@
     def absolute(b):
         return (s ^ (b // half)) * half + b % half
 
-    row_block = lax.broadcasted_iota(jnp.int32, (length, 128), 0) // BLK
-    lane_block = lax.broadcasted_iota(jnp.int32, (length, 128), 1) // BLK
-
-    tile = 128
+    tile = length
+    lane_block = lax.broadcasted_iota(jnp.int32, (1, tile), 1) // BLK
+    last = (((1,), (1,)), ((), ()))
+
+    def bias_row(b, t):
+        row = jnp.zeros((1, tile), F32)
+        for c in range(tile // BLK):
+            linked = adjacency_ref[absolute(b), absolute(t * (tile // BLK) + c)] > 0
+            row = jnp.where(lane_block == c, jnp.where(linked, 0.0, -1e30).astype(F32), row)
+        return row
+
     grad_keys = jnp.zeros((length, hs), F32)
     grad_values = jnp.zeros((length, hs), F32)
-    out_t = [[None] * per for _ in range(length // tile)]
-    dq_t = [[None] * per for _ in range(length // tile)]
+    out_t = [[None] * (length // tile) for _ in range(per)]
+    dq_t = [[None] * (length // tile) for _ in range(per)]
     for t in range(length // tile):
-        linked = jnp.zeros((length, tile), jnp.int32)
-        for b in range(blocks):
-            for c in range(tile // BLK):
-                a = adjacency_ref[absolute(b), absolute(t * (tile // BLK) + c)]
-                linked = jnp.where((row_block == b) & (lane_block == c), a, linked)
-        bias = jnp.where(linked > 0, 0.0, -1e30).astype(F32)
+        bias = jnp.concatenate(
+            [jnp.broadcast_to(bias_row(b, t), (BLK, tile)) for b in range(blocks)], axis=0
+        )
         for h in range(per):
             q = q_scr[t * tile : (t + 1) * tile, h * hs : (h + 1) * hs]
             g = gt_scr[t * tile : (t + 1) * tile, h * hs : (h + 1) * hs]
             q8 = (q.astype(F32) * 0.125).astype(BF16)
-            last = (((1,), (1,)), ((), ()))
             sc = lax.dot_general(keys, q8, last, preferred_element_type=F32) + bias
             top = jnp.max(sc, axis=0, keepdims=True)
             e = jnp.exp(sc - top)
@@ -240,14 +257,16 @@
             dp = lax.dot_general(values, g, last, preferred_element_type=F32)
             inner = jnp.sum(p * dp, axis=0, keepdims=True)
             ds = (p * (dp - inner)).astype(BF16)
-            out_t[t][h] = jnp.dot(values_t, p_low, preferred_element_type=F32)
-            dq_t[t][h] = jnp.dot(keys_t, ds, preferred_element_type=F32) * 0.125
+            out_t[h][t] = jnp.dot(values_t, p_low, preferred_element_type=F32)
+            dq_t[h][t] = jnp.dot(keys_t, ds, preferred_element_type=F32) * 0.125
             grad_keys = grad_keys + jnp.dot(ds, q8, preferred_element_type=F32)
             grad_values = grad_values + jnp.dot(p_low, g, preferred_element_type=F32)
     dkv = jnp.concatenate([grad_keys, grad_values], axis=1).astype(BF16)
+    out_t = jnp.concatenate([jnp.concatenate(o, axis=1) for o in out_t], axis=0)
+    dq_t = jnp.concatenate([jnp.concatenate(o, axis=1) for o in dq_t], axis=0)
     for j in range(4):
-        att = jnp.concatenate(out_t[j], axis=0).T.astype(BF16)
-        dq = jnp.concatenate(dq_t[j], axis=0).T.astype(BF16)
+        att = out_t[:, j * rows : (j + 1) * rows].T.astype(BF16)
+        dq = dq_t[:, j * rows : (j + 1) * rows].T.astype(BF16)
         block = jnp.concatenate([dq, dkv[j * rows : (j + 1) * rows]], axis=1)
         d_refs[j][:rows, :joined] = block
         d_refs[j ^ 2][rows:, :joined] = block
@@ -268,17 +287,21 @@
             out_ref[i, s ^ k] = part[k * depth : (k + 1) * depth]
 
 
-def token_grad_kernel(place_ref, d0, d1, d2, d3, even_ref, odd_ref, own_ref, send_ref):
+def token_grad_kernel(place_ref, d0, d1, d2, d3, *refs):
     f, s = place_ref[0], place_ref[1]
+    group_refs, rest_refs, own_ref, send_ref = refs[:2], refs[2:4], refs[4], refs[5]
     rows = own_ref.shape[0]
-    depth, columns = even_ref.shape[2:]
-    joined = columns // 4
+    depth, joined = group_refs[0].shape[2:]
     last = (((1,), (1,)), ((), ()))
+    d = [r[:, :joined] for r in (d0, d1, d2, d3)]
     sides = []
-    for l, order in enumerate(((d0, d1, d2, d3), (d1, d0, d3, d2))):
-        d = jnp.concatenate([r[:, :joined] for r in order], axis=1)
-        w = jnp.concatenate([(even_ref, odd_ref)[i % 2][i // 2, l] for i in range(8)], axis=0)
-        sides.append(lax.dot_general(d, w, last, preferred_element_type=F32).astype(BF16))
+    for l in range(2):
+        first = jnp.concatenate([group_refs[i % 2][i // 2, l] for i in range(8)], axis=0)
+        total = lax.dot_general(d[0], first, last, preferred_element_type=F32)
+        w = jnp.concatenate([rest_refs[i % 2][i // 2, l] for i in range(8)], axis=0)
+        others = jnp.concatenate([d[1], d[2], d[3]], axis=1)
+        total = total + lax.dot_general(others, w, last, preferred_element_type=F32)
+        sides.append(total.astype(BF16))
     odd = s % 2 == 1
     first = jnp.where(odd, sides[1], sides[0])
     second = jnp.where(odd, sides[0], sides[1])
@@ -337,11 +360,11 @@
     x1 = swap(x0, "seq", 1)
     x2 = swap(x0, "seq", 2)
 
-    few = joined + rows // depth * wide
-    w_all, *pay = vmem_call(
+    few = rows // depth * wide
+    w_rest, near, *pay = vmem_call(
         pack_kernel,
-        [shape(depth, 4 * joined)]
-        + [shape(depth, few + (4 * joined if j == 1 else 0)) for j in range(4)],
+        [shape(depth, 3 * joined), shape(depth, 4 * joined + few)]
+        + [shape(depth, joined + few)] * 3,
         scratch_shapes=[
             pltpu.VMEM((depth, 4 * wide), BF16),
             pltpu.VMEM((depth, 4 * narrow), BF16),
@@ -353,30 +376,29 @@
         place=pltpu.HBM,
     )(place, w_query, w_key, value_weight, grad_attn[0])
 
-    pay = [pay[0]] + [swap(pay[j], "seq", j) for j in (1, 2, 3)]
-    pay, x1 = lax.optimization_barrier((pay, x1))
+    pay = [pay[0], swap(near, "seq", 1), swap(pay[1], "seq", 2), swap(pay[2], "seq", 3)]
+    pay, x2 = lax.optimization_barrier((pay, x2))
 
     w_rows = jnp.stack([p[:, :joined] for p in pay])
     w_own = jnp.stack([w_rows] + [swap(w_rows, "fsdp", j) for j in (2, 4, 6)])
-    u_rows = jnp.stack([w_all, pay[1][:, few:]])
-    w_own, x2, u_rows = lax.optimization_barrier((w_own, x2, u_rows))
-
+    u_rows = jnp.stack([w_rest, pay[1][:, joined : 4 * joined]])
+    w_own, x1 = lax.optimization_barrier((w_own, x1))
     x3 = swap(x2, "seq", 1)
+    x3, mark = lax.optimization_barrier((x3, note(8, x3)))
     w_other = swap(w_own, "fsdp", 1)
-    u_own = jnp.stack([u_rows] + [swap(u_rows, "fsdp", j) for j in (2, 4, 6)])
-    u_other = swap(u_own, "fsdp", 1)
+    u_part = [swap(u_rows, "fsdp", j) for j in (2, 4)]
 
     d = vmem_call(
         attend_kernel,
         [shape(2 * rows, joined + wide // 2)] * 4,
         scratch_shapes=[
-            pltpu.VMEM((8, 4 * depth, joined), BF16),
+            pltpu.VMEM((width, joined), BF16),
             pltpu.VMEM((4 * rows, wide), BF16),
             pltpu.VMEM((4 * rows, wide), BF16),
         ],
         smem=2,
         total=20 << 30,
-    )(place, adjacency, x0, x1, x2, x3, w_own, w_other, *pay)
+    )(place, adjacency, x0, x1, x2, x3, w_own, w_other, *pay, mark)
 
     def weight_grad(parity, d):
         return vmem_call(
@@ -389,9 +411,14 @@
     away = weight_grad(1, d)
     d, away = lax.optimization_barrier((d, away))
     sent = swap(away, "fsdp", 1)
-    d_got = [d[0]] + [swap(d[j], "seq", j) for j in (1, 2, 3)]
+    d_got = {j: swap(d[j], "seq", j) for j in (3, 2, 1)}
+    d_got = [d[0], d_got[1], d_got[2], d_got[3]]
+    d, u_part = lax.optimization_barrier((d, u_part))
     kept = weight_grad(0, d)
     total = kept + sent
+    u_own = jnp.stack([u_rows, *u_part, swap(u_part[0], "fsdp", 4)])
+    d_got[2], u_own = lax.optimization_barrier((d_got[2], u_own))
+    u_other = swap(u_own, "fsdp", 1)
     got = [swap(total[i], "fsdp", 2 * i) for i in (1, 2, 3)]
     factor = 1.0 / math.sqrt(4 * rows * lax.axis_size("fsdp"))
     summed = (((total[0] + got[0]) + (got[1] + got[2])) * factor).astype(BF16)
@@ -401,17 +428,20 @@
         token_grad_kernel,
         [shape(rows, width // 2)] * 2,
         smem=1,
-        total=COST << 30,
-    )(place, *d_got, u_own, u_other)
+        total=2 << 30,
+    )(place, *d_got, w_own, w_other, u_own, u_other)
     half = swap(send, "seq", 2)
 
-    attended = vmem_call(attended_join_kernel, shape(rows, 4 * wide), smem=1)(place, *d_got)
-    grad_in = vmem_call(token_join_kernel, shape(rows, width), smem=1)(place, own, half)
-    grad_wq, grad_wk, grad_wv = vmem_call(
+    attended = vmem_call(
+        attended_join_kernel, shape(rows, 4 * wide)
+    )(place, *d_got)
+    weights = vmem_call(
         weight_join_kernel,
         [shape(depth, 4 * wide), shape(depth, 4 * narrow), shape(depth, 4 * narrow)],
         smem=1,
     )(place, *w_final)
+    grad_wq, grad_wk, grad_wv = weights
+    grad_in = vmem_call(token_join_kernel, shape(rows, width), smem=1)(place, own, half)
     return attended[None], grad_in[None], grad_wq, grad_wk, grad_wv
 
 

time: 120 us -> 115 us (0.958)
  Pallas kernels: 19.8 us -> 15.8 us
  waiting for transfers between devices: 61.6 us -> 58.5 us
  starting transfers between devices: 33.5 us -> 34.7 us
    pallas_call x8, Pallas kernels: 19.8 us -> 15.8 us  [call(): pl.pallas_call(kernel, out_shape=out_shape, in_specs=in_specs, out_specs=...]
    ppermute x25, waiting for transfers between devices: 61.6 us -> 58.5 us  [swap(): return lax.ppermute(x, axis, [(i, i ^ j) for i in range(n)])]
  transfers between devices with their start and end apart: 25 -> 25, of which waited for: 11 -> 11; matrix products, arithmetic and copies ran while one was open for 1% -> 1% of each run, Pallas kernels for 15% -> 13%
where the time goes in v3:
time: 115 us; the launch traced here: 114 us
  waiting for transfers between devices  58.5 us (51%)
  starting transfers between devices  34.7 us (30%)
  Pallas kernels  15.8 us (14%)
  local copies, waits for them, and re-layouts  3.52 us (3%)
    ppermute x25, waiting for transfers between devices, swap(): return lax.ppermute(x, axis, [(i, i ^ j) for i in range(n)])  58.5 us
    ppermute x25, starting transfers between devices, swap(): return lax.ppermute(x, axis, [(i, i ^ j) for i in range(n)])  34.7 us
    pallas_call x8, Pallas kernels, call(): pl.pallas_call(kernel, out_shape=out_shape, in_specs=in_specs, out_specs=...  15.8 us
    unnamed x12, local copies, waits for them, and re-layouts  3.38 us
  transfers between devices with their start and end apart: 25, of which 11 were waited for; matrix products, arithmetic and copies ran while one was open for 1% of the time, Pallas kernels for 13%

profile of v3, /device:TPU:0, one launch (start us, length us, event | category | flops | bytes accessed | tf_op | source)
XLA Modules:
  0.0 114.2 jit_solution(8120538268399554290)
XLA Ops:
  0.6 4.1 %collective-permute-start.3 = (bf16[128,2048]{1,0:T(8,128)(2,1)}, bf16[128,2048]{1,0:T(8,128)(2,1)S(1)}, u32[]{:S(2)}, u32[]{:S(2)}) collective-permute-start(bf16[128,2048]{1,0:T(8,128)(2,1)} %bitcast.51), channel_id=1, source_target_pairs={{0,2},{1,3},{2,0},{3,1},{4,6},{5,7},{6,4},{7,5},{8,10},{9,11},{10,... | collective-permute-start | bytes 1572872 | tf_op jit(solution)/shard_map/ppermute | solution.py:104
  4.8 0.9 copy-done.1
  5.8 0.9 copy-done.2
  6.7 0.8 copy-done.3
  7.4 0.8 copy-done.4
  8.2 1.1 shard_map.101
  9.3 1.6 %collective-permute-start = (bf16[64,2048]{1,0:T(8,128)(2,1)S(1)}, bf16[64,2048]{1,0:T(8,128)(2,1)S(1)}, u32[]{:S(2)}, u32[]{:S(2)}) collective-permute-start(bf16[64,2048]{1,0:T(8,128)(2,1)S(1)} %get-tuple-element.40), channel_id=1, source_target_pairs={{0,1},{1,0},{2,3},{3,2},{4,5},{5,4},{6,7},{7,6},{8,9},{9,8},{10,11... | collective-permute-start | bytes 786440 | tf_op jit(solution)/shard_map/ppermute | solution.py:104
  10.9 0.3 collective-permute-start.1
  11.2 2.5 %collective-permute-start.2 = (bf16[64,896]{1,0:T(8,128)(2,1)S(1)}, bf16[64,896]{1,0:T(8,128)(2,1)S(1)}, u32[]{:S(2)}, u32[]{:S(2)}) collective-permute-start(bf16[64,896]{1,0:T(8,128)(2,1)S(1)} %get-tuple-element.42), channel_id=1, source_target_pairs={{0,3},{1,2},{2,1},{3,0},{4,7},{5,6},{6,5},{7,4},{8,11},{9,10},{10,... | collective-permute-start | bytes 344072 | tf_op jit(solution)/shard_map/ppermute | solution.py:104
  13.7 0.7 collective-permute-start.7
  14.4 22.0 %collective-permute-done.1.refs_8_ = bf16[64,896]{1,0:T(8,128)(2,1)S(1)} collective-permute-done((bf16[64,896]{1,0:T(8,128)(2,1)S(1)}, bf16[64,896]{1,0:T(8,128)(2,1)S(1)}, u32[]{:S(2)}, u32[]{:S(2)}) %collective-permute-start.1) | collective-permute-done | bytes 114720 | tf_op jit(solution)/shard_map/ppermute | solution.py:104
  36.5 1.9 %collective-permute-start.5 = (bf16[4,64,384]{2,1,0:T(8,128)(2,1)S(1)}, bf16[4,64,384]{2,1,0:T(8,128)(2,1)S(1)}, u32[]{:S(2)}, u32[]{:S(2)}) collective-permute-start(bf16[4,64,384]{2,1,0:T(8,128)(2,1)S(1)} %get-tuple-element.83), channel_id=1, source_target_pairs={{0,16},{4,20},{8,24},{12,28},{16,0},{20,4},{24,8},{28,12},{1,17},{... | collective-permute-start | bytes 589832 | tf_op jit(solution)/shard_map/ppermute | solution.py:104
  38.4 1.4 %collective-permute-start.6 = (bf16[4,64,384]{2,1,0:T(8,128)(2,1)S(1)}, bf16[4,64,384]{2,1,0:T(8,128)(2,1)S(1)}, u32[]{:S(2)}, u32[]{:S(2)}) collective-permute-start(bf16[4,64,384]{2,1,0:T(8,128)(2,1)S(1)} %get-tuple-element.83), channel_id=1, source_target_pairs={{0,24},{4,28},{8,16},{12,20},{16,8},{20,12},{24,0},{28,4},{1,25},{... | collective-permute-start | bytes 589832 | tf_op jit(solution)/shard_map/ppermute | solution.py:104
  39.8 0.2 collective-permute-start.4
  40.0 2.3 %collective-permute-start.8 = (bf16[128,2048]{1,0:T(8,128)(2,1)S(1)}, bf16[128,2048]{1,0:T(8,128)(2,1)S(1)}, u32[]{:S(2)}, u32[]{:S(2)}) collective-permute-start(bf16[128,2048]{1,0:T(8,128)(2,1)S(1)} %collective-permute-done.3.refs_2_.x2), channel_id=1, source_target_pairs={{0,1},{1,0},{2,3},{3,2},{4,5},{5,4},{6,7},{7,6},{8,9},{9,8},{10,11... | collective-permute-start | bytes 1572872 | tf_op jit(solution)/shard_map/ppermute | solution.py:104
  42.4 3.6 %collective-permute-done.5 = bf16[4,64,384]{2,1,0:T(8,128)(2,1)S(1)} collective-permute-done((bf16[4,64,384]{2,1,0:T(8,128)(2,1)S(1)}, bf16[4,64,384]{2,1,0:T(8,128)(2,1)S(1)}, u32[]{:S(2)}, u32[]{:S(2)}) %collective-permute-start.5) | collective-permute-done | bytes 196640 | tf_op jit(solution)/shard_map/ppermute | solution.py:104
  46.0 0.3 collective-permute-start.12
  46.3 2.5 %collective-permute-start.13 = (bf16[2,64,1152]{2,1,0:T(8,128)(2,1)S(1)}, bf16[2,64,1152]{2,1,0:T(8,128)(2,1)S(1)}, u32[]{:S(2)}, u32[]{:S(2)}) collective-permute-start(bf16[2,64,1152]{2,1,0:T(8,128)(2,1)S(1)} %get-tuple-element.77), channel_id=1, source_target_pairs={{0,16},{4,20},{8,24},{12,28},{16,0},{20,4},{24,8},{28,12},{1,17},{... | collective-permute-start | bytes 884744 | tf_op jit(solution)/shard_map/ppermute | solution.py:104
  48.8 1.0 collective-permute-done.4
  49.8 0.1 pad_maximum_fusion.1.refs_4_.refs_0_
  50.1 4.5 %collective-permute-done.8.refs_0_.refs_3_.x3 = bf16[128,2048]{1,0:T(8,128)(2,1)S(1)} collective-permute-done((bf16[128,2048]{1,0:T(8,128)(2,1)S(1)}, bf16[128,2048]{1,0:T(8,128)(2,1)S(1)}, u32[]{:S(2)}, u32[]{:S(2)}) %collective-permute-start.8) | collective-permute-done | bytes 524320 | tf_op jit(solution)/shard_map/ppermute | solution.py:104
  54.6 6.7 %shard_map.103 = (bf16[256,512]{1,0:T(8,128)(2,1)S(1)}, bf16[256,512]{1,0:T(8,128)(2,1)S(1)}, bf16[256,512]{1,0:T(8,128)(2,1)S(1)}, bf16[256,512]{1,0:T(8,128)(2,1)S(1)}) custom-call(s32[2]{0:T(128)S(1)} %pad_add_fusion.place_ref, s32[8,8]{1,0:T(8,128)S(1)} %copy-done.5, bf16[128,2048]{1,0:T(8,128)(2,1)S(1)} %bitcast.53, ...), custom_call_target="tpu_custom_call" | custom-call | flops 21474836480 | bytes 4194304 | tf_op jit(solution)/shard_map/pallas_call | solution.py:128
  61.2 1.3 %shard_map.104 = f32[4,4,64,384]{3,2,1,0:T(8,128)S(1)} custom-call(s32[2]{0:T(128)S(1)} %pad_add_fusion.place_ref, bf16[128,2048]{1,0:T(8,128)(2,1)S(1)} %bitcast.54, bf16[128,2048]{1,0:T(8,128)(2,1)S(1)} %collective-permute-done.7.refs_1_.x1, bf16[128,2048]{1,0:T(8,128)(2,1)S(1)} %collective-permute-done.3.refs_2_.x2, ...), custom_call_target="tpu_custom_call" | custom-call | flops 1073741824 | bytes 4194304 | tf_op jit(solution)/shard_map/pallas_call | solution.py:128
  62.7 1.6 %collective-permute-start.14 = (bf16[2,64,1152]{2,1,0:T(8,128)(2,1)S(1)}, bf16[2,64,1152]{2,1,0:T(8,128)(2,1)S(1)}, u32[]{:S(2)}, u32[]{:S(2)}) collective-permute-start(bf16[2,64,1152]{2,1,0:T(8,128)(2,1)S(1)} %collective-permute-done.12), channel_id=1, source_target_pairs={{0,16},{4,20},{8,24},{12,28},{16,0},{20,4},{24,8},{28,12},{1,17},{... | collective-permute-start | bytes 884744 | tf_op jit(solution)/shard_map/ppermute | solution.py:104
  64.3 2.7 %collective-permute-start.11 = (bf16[256,512]{1,0:T(8,128)(2,1)S(1)}, bf16[256,512]{1,0:T(8,128)(2,1)S(1)}, u32[]{:S(2)}, u32[]{:S(2)}) collective-permute-start(bf16[256,512]{1,0:T(8,128)(2,1)S(1)} %get-tuple-element.58), channel_id=1, source_target_pairs={{0,2},{1,3},{2,0},{3,1},{4,6},{5,7},{6,4},{7,5},{8,10},{9,11},{10,... | collective-permute-start | bytes 786440 | tf_op jit(solution)/shard_map/ppermute | solution.py:104
  67.0 5.1 %collective-permute-done.14 = bf16[2,64,1152]{2,1,0:T(8,128)(2,1)S(1)} collective-permute-done((bf16[2,64,1152]{2,1,0:T(8,128)(2,1)S(1)}, bf16[2,64,1152]{2,1,0:T(8,128)(2,1)S(1)}, u32[]{:S(2)}, u32[]{:S(2)}) %collective-permute-start.14) | collective-permute-done | bytes 294944 | tf_op jit(solution)/shard_map/ppermute | solution.py:104
  72.1 0.2 pad_maximum_fusion.refs_2_
  72.3 7.0 %collective-permute-done.11.d2 = bf16[256,512]{1,0:T(8,128)(2,1)S(1)} collective-permute-done((bf16[256,512]{1,0:T(8,128)(2,1)S(1)}, bf16[256,512]{1,0:T(8,128)(2,1)S(1)}, u32[]{:S(2)}, u32[]{:S(2)}) %collective-permute-start.11) | collective-permute-done | bytes 262176 | tf_op jit(solution)/shard_map/ppermute | solution.py:104
  79.2 2.4 %collective-permute-start.15 = (bf16[256,512]{1,0:T(8,128)(2,1)S(1)}, bf16[256,512]{1,0:T(8,128)(2,1)S(1)}, u32[]{:S(2)}, u32[]{:S(2)}) collective-permute-start(bf16[256,512]{1,0:T(8,128)(2,1)S(1)} %get-tuple-element.60), channel_id=1, source_target_pairs={{0,3},{1,2},{2,1},{3,0},{4,7},{5,6},{6,5},{7,4},{8,11},{9,10},{10,... | collective-permute-start | bytes 786440 | tf_op jit(solution)/shard_map/ppermute | solution.py:104
  81.6 1.3 %shard_map.108 = f32[4,4,64,384]{3,2,1,0:T(8,128)S(1)} custom-call(s32[2]{0:T(128)S(1)} %pad_add_fusion.place_ref, bf16[128,2048]{1,0:T(8,128)(2,1)S(1)} %bitcast.55, bf16[128,2048]{1,0:T(8,128)(2,1)S(1)} %collective-permute-done.7.refs_1_.x1, bf16[128,2048]{1,0:T(8,128)(2,1)S(1)} %collective-permute-done.3.refs_2_.x2, ...), custom_call_target="tpu_custom_call" | custom-call | flops 1073741824 | bytes 4194304 | tf_op jit(solution)/shard_map/pallas_call | solution.py:128
  82.9 0.2 add.12
  83.2 1.6 %collective-permute-start.19 = (f32[4,64,384]{2,1,0:T(8,128)S(1)}, f32[4,64,384]{2,1,0:T(8,128)S(1)}, u32[]{:S(2)}, u32[]{:S(2)}) collective-permute-start(f32[4,64,384]{2,1,0:T(8,128)S(1)} %get-tuple-element.75), channel_id=1, source_target_pairs={{0,8},{4,12},{8,0},{12,4},{16,24},{20,28},{24,16},{28,20},{1,9},{5... | collective-permute-start | bytes 1179656 | tf_op jit(solution)/shard_map/ppermute | solution.py:104
  84.8 0.5 collective-permute-start.20
  85.3 2.6 %collective-permute-done.10.d1 = bf16[256,512]{1,0:T(8,128)(2,1)S(1)} collective-permute-done((bf16[256,512]{1,0:T(8,128)(2,1)S(1)}, bf16[256,512]{1,0:T(8,128)(2,1)S(1)}, u32[]{:S(2)}, u32[]{:S(2)}) %collective-permute-start.10) | collective-permute-done | bytes 262176 | tf_op jit(solution)/shard_map/ppermute | solution.py:104
  87.9 1.4 %collective-permute-start.21 = (f32[4,64,384]{2,1,0:T(8,128)S(1)}, f32[4,64,384]{2,1,0:T(8,128)S(1)}, u32[]{:S(2)}, u32[]{:S(2)}) collective-permute-start(f32[4,64,384]{2,1,0:T(8,128)S(1)} %get-tuple-element.73), channel_id=1, source_target_pairs={{0,24},{4,28},{8,16},{12,20},{16,8},{20,12},{24,0},{28,4},{1,25},{... | collective-permute-start | bytes 1179656 | tf_op jit(solution)/shard_map/ppermute | solution.py:104
  89.4 4.9 %collective-permute-done.15.d3 = bf16[256,512]{1,0:T(8,128)(2,1)S(1)} collective-permute-done((bf16[256,512]{1,0:T(8,128)(2,1)S(1)}, bf16[256,512]{1,0:T(8,128)(2,1)S(1)}, u32[]{:S(2)}, u32[]{:S(2)}) %collective-permute-start.15) | collective-permute-done | bytes 262176 | tf_op jit(solution)/shard_map/ppermute | solution.py:104
  94.3 1.9 %shard_map.106 = (bf16[128,1024]{1,0:T(8,128)(2,1)S(1)}, bf16[128,1024]{1,0:T(8,128)(2,1)S(1)}) custom-call(s32[2]{0:T(128)S(1)} %pad_add_fusion.place_ref, bf16[256,512]{1,0:T(8,128)(2,1)S(1)} %get-tuple-element.67.d0_ref.d0, bf16[256,512]{1,0:T(8,128)(2,1)S(1)} %collective-permute-done.10.d1, bf16[256,512]{1,0:T(8,128)(2,1)S(1)} %collective-permute-done.11.d2, ...), custom_call_target="tpu_custom_call" | custom-call | flops 2147483648 | bytes 4194304 | tf_op jit(solution)/shard_map/pallas_call | solution.py:128
  96.2 2.0 %collective-permute-start.17 = (bf16[128,1024]{1,0:T(8,128)(2,1)S(1)}, bf16[128,1024]{1,0:T(8,128)(2,1)S(1)}, u32[]{:S(2)}, u32[]{:S(2)}) collective-permute-start(bf16[128,1024]{1,0:T(8,128)(2,1)S(1)} %get-tuple-element.66), channel_id=1, source_target_pairs={{0,2},{1,3},{2,0},{3,1},{4,6},{5,7},{6,4},{7,5},{8,10},{9,11},{10,... | collective-permute-start | bytes 786440 | tf_op jit(solution)/shard_map/ppermute | solution.py:104
  98.2 6.0 %collective-permute-done.20 = f32[4,64,384]{2,1,0:T(8,128)S(1)} collective-permute-done((f32[4,64,384]{2,1,0:T(8,128)S(1)}, f32[4,64,384]{2,1,0:T(8,128)S(1)}, u32[]{:S(2)}, u32[]{:S(2)}) %collective-permute-start.20) | collective-permute-done | bytes 393248 | tf_op jit(solution)/shard_map/ppermute | solution.py:104
  104.2 0.1 fusion.3
  104.3 0.9 collective-permute-start.22
  105.2 1.2 %collective-permute-start.23 = (bf16[64,384]{1,0:T(8,128)(2,1)S(1)}, bf16[64,384]{1,0:T(8,128)(2,1)S(1)}, u32[]{:S(2)}, u32[]{:S(2)}) collective-permute-start(bf16[64,384]{1,0:T(8,128)(2,1)S(1)} %get-tuple-element.79), channel_id=1, source_target_pairs={{0,2},{1,3},{2,0},{3,1},{4,6},{5,7},{6,4},{7,5},{8,10},{9,11},{10,... | collective-permute-start | bytes 147464 | tf_op jit(solution)/shard_map/ppermute | solution.py:104
  106.4 2.3 %collective-permute-start.24 = (bf16[64,384]{1,0:T(8,128)(2,1)S(1)}, bf16[64,384]{1,0:T(8,128)(2,1)S(1)}, u32[]{:S(2)}, u32[]{:S(2)}) collective-permute-start(bf16[64,384]{1,0:T(8,128)(2,1)S(1)} %get-tuple-element.78), channel_id=1, source_target_pairs={{0,3},{1,2},{2,1},{3,0},{4,7},{5,6},{6,5},{7,4},{8,11},{9,10},{10,... | collective-permute-start | bytes 147464 | tf_op jit(solution)/shard_map/ppermute | solution.py:104
  108.8 0.8 shard_map.105
  109.6 1.8 %collective-permute-done.17.got_ref = bf16[128,1024]{1,0:T(8,128)(2,1)S(1)} collective-permute-done((bf16[128,1024]{1,0:T(8,128)(2,1)S(1)}, bf16[128,1024]{1,0:T(8,128)(2,1)S(1)}, u32[]{:S(2)}, u32[]{:S(2)}) %collective-permute-start.17) | collective-permute-done | bytes 262176 | tf_op jit(solution)/shard_map/ppermute | solution.py:104
  111.4 1.5 %shard_map.107 = bf16[128,2048]{1,0:T(8,128)(2,1)} custom-call(s32[2]{0:T(128)S(1)} %pad_add_fusion.place_ref, bf16[128,1024]{1,0:T(8,128)(2,1)S(1)} %get-tuple-element.65.own_ref, bf16[128,1024]{1,0:T(8,128)(2,1)S(1)} %collective-permute-done.17.got_ref), custom_call_target="tpu_custom_call" | custom-call | bytes 4194304 | tf_op jit(solution)/shard_map/pallas_call | solution.py:128
  112.9 0.1 collective-permute-done.23.b2
  113.0 1.3 %shard_map.109 = (bf16[64,1024]{1,0:T(8,128)(2,1)}, bf16[64,256]{1,0:T(8,128)(2,1)}, bf16[64,256]{1,0:T(8,128)(2,1)}) custom-call(s32[2]{0:T(128)S(1)} %pad_add_fusion.place_ref, bf16[64,384]{1,0:T(8,128)(2,1)S(1)} %get-tuple-element.81.b0, bf16[64,384]{1,0:T(8,128)(2,1)S(1)} %collective-permute-done.22.b1, bf16[64,384]{1,0:T(8,128)(2,1)S(1)} %collective-permute-done.23.b2, ...), custom_call_target="tpu_custom_call" | custom-call | bytes 4194304 | tf_op jit(solution)/shard_map/pallas_call | solution.py:128
  (35 shorter events, 0.5 us)
Async XLA Ops:
  0.6 35.7 %collective-permute-start.3 = (bf16[128,2048]{1,0:T(8,128)(2,1)}, bf16[128,2048]{1,0:T(8,128)(2,1)S(1)}, u32[]{:S(2)}, u32[]{:S(2)}) collective-permute-start(bf16[128,2048]{1,0:T(8,128)(2,1)} %bitcast.51), channel_id=1, source_target_pairs={{0,2},{1,3},{2,0},{3,1},{4,6},{5,7},{6,4},{7,5},{8,10},{9,11},{10,... | collective-permute-start | bytes 1572872 | tf_op jit(solution)/shard_map/ppermute | solution.py:104
  4.8 0.9 copy-start.1
  5.8 0.9 copy-start.2
  6.7 0.8 copy-start.3
  7.4 0.8 copy-start.4
  9.3 27.1 %collective-permute-start = (bf16[64,2048]{1,0:T(8,128)(2,1)S(1)}, bf16[64,2048]{1,0:T(8,128)(2,1)S(1)}, u32[]{:S(2)}, u32[]{:S(2)}) collective-permute-start(bf16[64,2048]{1,0:T(8,128)(2,1)S(1)} %get-tuple-element.40), channel_id=1, source_target_pairs={{0,1},{1,0},{2,3},{3,2},{4,5},{5,4},{6,7},{7,6},{8,9},{9,8},{10,11... | collective-permute-start | bytes 786440 | tf_op jit(solution)/shard_map/ppermute | solution.py:104
  10.9 25.5 %collective-permute-start.1 = (bf16[64,896]{1,0:T(8,128)(2,1)S(1)}, bf16[64,896]{1,0:T(8,128)(2,1)S(1)}, u32[]{:S(2)}, u32[]{:S(2)}) collective-permute-start(bf16[64,896]{1,0:T(8,128)(2,1)S(1)} %get-tuple-element.41), channel_id=1, source_target_pairs={{0,2},{1,3},{2,0},{3,1},{4,6},{5,7},{6,4},{7,5},{8,10},{9,11},{10,... | collective-permute-start | bytes 344072 | tf_op jit(solution)/shard_map/ppermute | solution.py:104
  11.2 25.1 %collective-permute-start.2 = (bf16[64,896]{1,0:T(8,128)(2,1)S(1)}, bf16[64,896]{1,0:T(8,128)(2,1)S(1)}, u32[]{:S(2)}, u32[]{:S(2)}) collective-permute-start(bf16[64,896]{1,0:T(8,128)(2,1)S(1)} %get-tuple-element.42), channel_id=1, source_target_pairs={{0,3},{1,2},{2,1},{3,0},{4,7},{5,6},{6,5},{7,4},{8,11},{9,10},{10,... | collective-permute-start | bytes 344072 | tf_op jit(solution)/shard_map/ppermute | solution.py:104
  13.7 36.3 %collective-permute-start.7 = (bf16[128,2048]{1,0:T(8,128)(2,1)}, bf16[128,2048]{1,0:T(8,128)(2,1)S(1)}, u32[]{:S(2)}, u32[]{:S(2)}) collective-permute-start(bf16[128,2048]{1,0:T(8,128)(2,1)} %bitcast.52), channel_id=1, source_target_pairs={{0,1},{1,0},{2,3},{3,2},{4,5},{5,4},{6,7},{7,6},{8,9},{9,8},{10,11... | collective-permute-start | bytes 1572872 | tf_op jit(solution)/shard_map/ppermute | solution.py:104
  36.5 9.5 %collective-permute-start.5 = (bf16[4,64,384]{2,1,0:T(8,128)(2,1)S(1)}, bf16[4,64,384]{2,1,0:T(8,128)(2,1)S(1)}, u32[]{:S(2)}, u32[]{:S(2)}) collective-permute-start(bf16[4,64,384]{2,1,0:T(8,128)(2,1)S(1)} %get-tuple-element.83), channel_id=1, source_target_pairs={{0,16},{4,20},{8,24},{12,28},{16,0},{20,4},{24,8},{28,12},{1,17},{... | collective-permute-start | bytes 589832 | tf_op jit(solution)/shard_map/ppermute | solution.py:104
  38.4 7.9 %collective-permute-start.6 = (bf16[4,64,384]{2,1,0:T(8,128)(2,1)S(1)}, bf16[4,64,384]{2,1,0:T(8,128)(2,1)S(1)}, u32[]{:S(2)}, u32[]{:S(2)}) collective-permute-start(bf16[4,64,384]{2,1,0:T(8,128)(2,1)S(1)} %get-tuple-element.83), channel_id=1, source_target_pairs={{0,24},{4,28},{8,16},{12,20},{16,8},{20,12},{24,0},{28,4},{1,25},{... | collective-permute-start | bytes 589832 | tf_op jit(solution)/shard_map/ppermute | solution.py:104
  39.8 10.0 %collective-permute-start.4 = (bf16[4,64,384]{2,1,0:T(8,128)(2,1)S(1)}, bf16[4,64,384]{2,1,0:T(8,128)(2,1)S(1)}, u32[]{:S(2)}, u32[]{:S(2)}) collective-permute-start(bf16[4,64,384]{2,1,0:T(8,128)(2,1)S(1)} %get-tuple-element.83), channel_id=1, source_target_pairs={{0,8},{4,12},{8,0},{12,4},{16,24},{20,28},{24,16},{28,20},{1,9},{5... | collective-permute-start | bytes 589832 | tf_op jit(solution)/shard_map/ppermute | solution.py:104
  40.0 14.5 %collective-permute-start.8 = (bf16[128,2048]{1,0:T(8,128)(2,1)S(1)}, bf16[128,2048]{1,0:T(8,128)(2,1)S(1)}, u32[]{:S(2)}, u32[]{:S(2)}) collective-permute-start(bf16[128,2048]{1,0:T(8,128)(2,1)S(1)} %collective-permute-done.3.refs_2_.x2), channel_id=1, source_target_pairs={{0,1},{1,0},{2,3},{3,2},{4,5},{5,4},{6,7},{7,6},{8,9},{9,8},{10,11... | collective-permute-start | bytes 1572872 | tf_op jit(solution)/shard_map/ppermute | solution.py:104
  46.0 16.6 %collective-permute-start.12 = (bf16[2,64,1152]{2,1,0:T(8,128)(2,1)S(1)}, bf16[2,64,1152]{2,1,0:T(8,128)(2,1)S(1)}, u32[]{:S(2)}, u32[]{:S(2)}) collective-permute-start(bf16[2,64,1152]{2,1,0:T(8,128)(2,1)S(1)} %get-tuple-element.77), channel_id=1, source_target_pairs={{0,8},{4,12},{8,0},{12,4},{16,24},{20,28},{24,16},{28,20},{1,9},{5... | collective-permute-start | bytes 884744 | tf_op jit(solution)/shard_map/ppermute | solution.py:104
  46.3 16.4 %collective-permute-start.13 = (bf16[2,64,1152]{2,1,0:T(8,128)(2,1)S(1)}, bf16[2,64,1152]{2,1,0:T(8,128)(2,1)S(1)}, u32[]{:S(2)}, u32[]{:S(2)}) collective-permute-start(bf16[2,64,1152]{2,1,0:T(8,128)(2,1)S(1)} %get-tuple-element.77), channel_id=1, source_target_pairs={{0,16},{4,20},{8,24},{12,28},{16,0},{20,4},{24,8},{28,12},{1,17},{... | collective-permute-start | bytes 884744 | tf_op jit(solution)/shard_map/ppermute | solution.py:104
  50.0 4.6 %copy-start = (bf16[1,128,2048]{2,1,0:T(8,128)(2,1)S(1)}, bf16[1,128,2048]{2,1,0:T(8,128)(2,1)}, u32[]{:S(2)}) copy-start(bf16[1,128,2048]{2,1,0:T(8,128)(2,1)} %param.6) | copy-start | bytes 1572868
  50.0 4.6 %copy-start.5 = (s32[8,8]{1,0:T(8,128)S(1)}, s32[8,8]{1,0:T(8,128)}, u32[]{:S(2)}) copy-start(s32[8,8]{1,0:T(8,128)} %adjacency_ref.1) | copy-start | bytes 772
  50.0 4.5 %collective-permute-start.9 = (bf16[4,4,64,384]{3,2,1,0:T(8,128)(2,1)S(1)}, bf16[4,4,64,384]{3,2,1,0:T(8,128)(2,1)S(1)}, u32[]{:S(2)}, u32[]{:S(2)}) collective-permute-start(bf16[4,4,64,384]{3,2,1,0:T(8,128)(2,1)S(1)} %pad_maximum_fusion.1.refs_4_.refs_0_), channel_id=1, source_target_pairs={{0,4},{4,0},{8,12},{12,8},{16,20},{20,16},{24,28},{28,24},{1,5},{5... | collective-permute-start | bytes 2359304 | tf_op jit(solution)/shard_map/ppermute | solution.py:104
  62.6 20.3 %collective-permute-start.18 = (f32[4,4,64,384]{3,2,1,0:T(8,128)S(1)}, f32[4,4,64,384]{3,2,1,0:T(8,128)S(1)}, u32[]{:S(2)}, u32[]{:S(2)}) collective-permute-start(f32[4,4,64,384]{3,2,1,0:T(8,128)S(1)} %shard_map.104), channel_id=1, source_target_pairs={{0,4},{4,0},{8,12},{12,8},{16,20},{20,16},{24,28},{28,24},{1,5},{5... | collective-permute-start | bytes 4718600 | tf_op jit(solution)/shard_map/ppermute | solution.py:104
  62.7 9.4 %collective-permute-start.14 = (bf16[2,64,1152]{2,1,0:T(8,128)(2,1)S(1)}, bf16[2,64,1152]{2,1,0:T(8,128)(2,1)S(1)}, u32[]{:S(2)}, u32[]{:S(2)}) collective-permute-start(bf16[2,64,1152]{2,1,0:T(8,128)(2,1)S(1)} %collective-permute-done.12), channel_id=1, source_target_pairs={{0,16},{4,20},{8,24},{12,28},{16,0},{20,4},{24,8},{28,12},{1,17},{... | collective-permute-start | bytes 884744 | tf_op jit(solution)/shard_map/ppermute | solution.py:104
  64.3 14.9 %collective-permute-start.11 = (bf16[256,512]{1,0:T(8,128)(2,1)S(1)}, bf16[256,512]{1,0:T(8,128)(2,1)S(1)}, u32[]{:S(2)}, u32[]{:S(2)}) collective-permute-start(bf16[256,512]{1,0:T(8,128)(2,1)S(1)} %get-tuple-element.58), channel_id=1, source_target_pairs={{0,2},{1,3},{2,0},{3,1},{4,6},{5,7},{6,4},{7,5},{8,10},{9,11},{10,... | collective-permute-start | bytes 786440 | tf_op jit(solution)/shard_map/ppermute | solution.py:104
  79.2 15.1 %collective-permute-start.16 = (bf16[4,2,64,1152]{3,2,1,0:T(8,128)(2,1)S(1)}, bf16[4,2,64,1152]{3,2,1,0:T(8,128)(2,1)S(1)}, u32[]{:S(2)}, u32[]{:S(2)}) collective-permute-start(bf16[4,2,64,1152]{3,2,1,0:T(8,128)(2,1)S(1)} %pad_maximum_fusion.refs_2_), channel_id=1, source_target_pairs={{0,4},{4,0},{8,12},{12,8},{16,20},{20,16},{24,28},{28,24},{1,5},{5... | collective-permute-start | bytes 3538952 | tf_op jit(solution)/shard_map/ppermute | solution.py:104
  79.2 8.7 %collective-permute-start.10 = (bf16[256,512]{1,0:T(8,128)(2,1)S(1)}, bf16[256,512]{1,0:T(8,128)(2,1)S(1)}, u32[]{:S(2)}, u32[]{:S(2)}) collective-permute-start(bf16[256,512]{1,0:T(8,128)(2,1)S(1)} %get-tuple-element.68.d1_ref), channel_id=1, source_target_pairs={{0,1},{1,0},{2,3},{3,2},{4,5},{5,4},{6,7},{7,6},{8,9},{9,8},{10,11... | collective-permute-start | bytes 786440 | tf_op jit(solution)/shard_map/ppermute | solution.py:104
  79.2 15.1 %collective-permute-start.15 = (bf16[256,512]{1,0:T(8,128)(2,1)S(1)}, bf16[256,512]{1,0:T(8,128)(2,1)S(1)}, u32[]{:S(2)}, u32[]{:S(2)}) collective-permute-start(bf16[256,512]{1,0:T(8,128)(2,1)S(1)} %get-tuple-element.60), channel_id=1, source_target_pairs={{0,3},{1,2},{2,1},{3,0},{4,7},{5,6},{6,5},{7,4},{8,11},{9,10},{10,... | collective-permute-start | bytes 786440 | tf_op jit(solution)/shard_map/ppermute | solution.py:104
  83.2 14.9 %collective-permute-start.19 = (f32[4,64,384]{2,1,0:T(8,128)S(1)}, f32[4,64,384]{2,1,0:T(8,128)S(1)}, u32[]{:S(2)}, u32[]{:S(2)}) collective-permute-start(f32[4,64,384]{2,1,0:T(8,128)S(1)} %get-tuple-element.75), channel_id=1, source_target_pairs={{0,8},{4,12},{8,0},{12,4},{16,24},{20,28},{24,16},{28,20},{1,9},{5... | collective-permute-start | bytes 1179656 | tf_op jit(solution)/shard_map/ppermute | solution.py:104
  84.8 19.4 %collective-permute-start.20 = (f32[4,64,384]{2,1,0:T(8,128)S(1)}, f32[4,64,384]{2,1,0:T(8,128)S(1)}, u32[]{:S(2)}, u32[]{:S(2)}) collective-permute-start(f32[4,64,384]{2,1,0:T(8,128)S(1)} %get-tuple-element.74), channel_id=1, source_target_pairs={{0,16},{4,20},{8,24},{12,28},{16,0},{20,4},{24,8},{28,12},{1,17},{... | collective-permute-start | bytes 1179656 | tf_op jit(solution)/shard_map/ppermute | solution.py:104
  87.9 16.2 %collective-permute-start.21 = (f32[4,64,384]{2,1,0:T(8,128)S(1)}, f32[4,64,384]{2,1,0:T(8,128)S(1)}, u32[]{:S(2)}, u32[]{:S(2)}) collective-permute-start(f32[4,64,384]{2,1,0:T(8,128)S(1)} %get-tuple-element.73), channel_id=1, source_target_pairs={{0,24},{4,28},{8,16},{12,20},{16,8},{20,12},{24,0},{28,4},{1,25},{... | collective-permute-start | bytes 1179656 | tf_op jit(solution)/shard_map/ppermute | solution.py:104
  96.2 15.2 %collective-permute-start.17 = (bf16[128,1024]{1,0:T(8,128)(2,1)S(1)}, bf16[128,1024]{1,0:T(8,128)(2,1)S(1)}, u32[]{:S(2)}, u32[]{:S(2)}) collective-permute-start(bf16[128,1024]{1,0:T(8,128)(2,1)S(1)} %get-tuple-element.66), channel_id=1, source_target_pairs={{0,2},{1,3},{2,0},{3,1},{4,6},{5,7},{6,4},{7,5},{8,10},{9,11},{10,... | collective-permute-start | bytes 786440 | tf_op jit(solution)/shard_map/ppermute | solution.py:104
  104.3 8.5 %collective-permute-start.22 = (bf16[64,384]{1,0:T(8,128)(2,1)S(1)}, bf16[64,384]{1,0:T(8,128)(2,1)S(1)}, u32[]{:S(2)}, u32[]{:S(2)}) collective-permute-start(bf16[64,384]{1,0:T(8,128)(2,1)S(1)} %get-tuple-element.80), channel_id=1, source_target_pairs={{0,1},{1,0},{2,3},{3,2},{4,5},{5,4},{6,7},{7,6},{8,9},{9,8},{10,11... | collective-permute-start | bytes 147464 | tf_op jit(solution)/shard_map/ppermute | solution.py:104
  105.2 7.7 %collective-permute-start.23 = (bf16[64,384]{1,0:T(8,128)(2,1)S(1)}, bf16[64,384]{1,0:T(8,128)(2,1)S(1)}, u32[]{:S(2)}, u32[]{:S(2)}) collective-permute-start(bf16[64,384]{1,0:T(8,128)(2,1)S(1)} %get-tuple-element.79), channel_id=1, source_target_pairs={{0,2},{1,3},{2,0},{3,1},{4,6},{5,7},{6,4},{7,5},{8,10},{9,11},{10,... | collective-permute-start | bytes 147464 | tf_op jit(solution)/shard_map/ppermute | solution.py:104
  106.4 6.5 %collective-permute-start.24 = (bf16[64,384]{1,0:T(8,128)(2,1)S(1)}, bf16[64,384]{1,0:T(8,128)(2,1)S(1)}, u32[]{:S(2)}, u32[]{:S(2)}) collective-permute-start(bf16[64,384]{1,0:T(8,128)(2,1)S(1)} %get-tuple-element.78), channel_id=1, source_target_pairs={{0,3},{1,2},{2,1},{3,0},{4,7},{5,6},{6,5},{7,4},{8,11},{9,10},{10,... | collective-permute-start | bytes 147464 | tf_op jit(solution)/shard_map/ppermute | solution.py:104

commit v4 on v3

--- a/solution.py
+++ b/solution.py
@@ -119,7 +119,7 @@
     )(*others)
 
 
-def vmem_call(kernel, out_shape, scratch_shapes=(), smem=0, total=0, place=pltpu.VMEM):
+def vmem_call(kernel, out_shape, scratch_shapes=(), smem=0, total=0, place=pltpu.VMEM, limit=VMEM_LIMIT):
     def call(*args):
         in_specs = [
             pl.BlockSpec(memory_space=pltpu.SMEM if i < smem else place)
@@ -131,7 +131,7 @@
             in_specs=in_specs,
             out_specs=jax.tree.map(lambda _: pl.BlockSpec(memory_space=pltpu.VMEM), out_shape),
             scratch_shapes=scratch_shapes,
-            compiler_params=pltpu.CompilerParams(vmem_limit_bytes=VMEM_LIMIT),
+            compiler_params=pltpu.CompilerParams(vmem_limit_bytes=limit),
             cost_estimate=pl.CostEstimate(flops=total, bytes_accessed=4 << 20, transcendentals=0),
         )(*args)
 
@@ -192,8 +192,8 @@
 def attend_kernel(place_ref, adjacency_ref, *refs):
     f, s = place_ref[0], place_ref[1]
     x_refs, own_ref, other_ref, pay_refs = refs[0:4], refs[4], refs[5], refs[6:10]
-    d_refs = refs[11:15]
-    w_scr, q_scr, gt_scr = refs[15:18]
+    d_refs = refs[11:14]
+    w_scr, q_scr, gt_scr = refs[-3:]
     rows = x_refs[0].shape[0]
     length = 4 * rows
     depth, joined = own_ref.shape[2:]
@@ -268,10 +268,14 @@
         att = out_t[:, j * rows : (j + 1) * rows].T.astype(BF16)
         dq = dq_t[:, j * rows : (j + 1) * rows].T.astype(BF16)
         block = jnp.concatenate([dq, dkv[j * rows : (j + 1) * rows]], axis=1)
-        d_refs[j][:rows, :joined] = block
-        d_refs[j ^ 2][rows:, :joined] = block
-        d_refs[j][:rows, joined:] = att[:, : wide // 2]
-        d_refs[j][rows:, joined:] = att[:, wide // 2 :]
+        if j < 3:
+            d_refs[j][:rows, :joined] = block
+        if j != 1:
+            d_refs[j ^ 2][rows:, :joined] = block
+        spot = d_refs[j] if j < 3 else d_refs[1]
+        left = joined if j < 3 else joined + wide // 2
+        spot[:rows, left : left + wide // 2] = att[:, : wide // 2]
+        spot[rows:, left : left + wide // 2] = att[:, wide // 2 :]
 
 
 def weight_grad_kernel(parity, place_ref, x0, x1, x2, x3, d0_ref, d1_ref, out_ref):
@@ -294,6 +298,7 @@
     depth, joined = group_refs[0].shape[2:]
     last = (((1,), (1,)), ((), ()))
     d = [r[:, :joined] for r in (d0, d1, d2, d3)]
+    d[3] = jnp.concatenate([d[3][rows:], d[3][:rows]], axis=0)
     sides = []
     for l in range(2):
         first = jnp.concatenate([group_refs[i % 2][i // 2, l] for i in range(8)], axis=0)
@@ -329,7 +334,8 @@
     rows = out_ref.shape[0]
     part = out_ref.shape[1] // 8
     for j, ref in enumerate((d0, d1, d2, d3)):
-        both = jnp.concatenate([ref[:rows, -part:], ref[rows:, -part:]], axis=1)
+        here = slice(3 * part, 4 * part)
+        both = jnp.concatenate([ref[:rows, here], ref[rows:, here]], axis=1)
         out_ref[:, pl.ds(pl.multiple_of((s ^ j) * 2 * part, 2 * part), 2 * part)] = both
 
 
@@ -346,6 +352,11 @@
     two = [jnp.where(high, one[i ^ 2], one[i]) for i in range(4)]
     k_ref[...] = jnp.concatenate([b[:, :narrow] for b in two], axis=1)
     v_ref[...] = jnp.concatenate([b[:, narrow:] for b in two], axis=1)
+
+
+def join_kernel(place_ref, b0, b1, b2, b3, own, got, q_ref, k_ref, v_ref, out_ref):
+    token_join_kernel(place_ref, own, got, out_ref)
+    weight_join_kernel(place_ref, b0, b1, b2, b3, q_ref, k_ref, v_ref)
 
 
 def head_body(tokens, adjacency, w_query, w_key, value_weight, grad_attn):
@@ -390,14 +401,14 @@
 
     d = vmem_call(
         attend_kernel,
-        [shape(2 * rows, joined + wide // 2)] * 4,
+        [shape(2 * rows, joined + extra * (wide // 2)) for extra in (1, 2, 1)],
         scratch_shapes=[
             pltpu.VMEM((width, joined), BF16),
             pltpu.VMEM((4 * rows, wide), BF16),
             pltpu.VMEM((4 * rows, wide), BF16),
         ],
         smem=2,
-        total=20 << 30,
+        total=8 << 30,
     )(place, adjacency, x0, x1, x2, x3, w_own, w_other, *pay, mark)
 
     def weight_grad(parity, d):
@@ -405,19 +416,21 @@
             functools.partial(weight_grad_kernel, parity),
             shape(4, 4, depth, joined, dtype=F32),
             smem=1,
-            total=1 << 30,
+            total=8 << 30,
         )(place, x0, x1, x2, x3, d[0], d[1])
 
     away = weight_grad(1, d)
     d, away = lax.optimization_barrier((d, away))
     sent = swap(away, "fsdp", 1)
-    d_got = {j: swap(d[j], "seq", j) for j in (3, 2, 1)}
-    d_got = [d[0], d_got[1], d_got[2], d_got[3]]
+    d_two = swap(d[2], "seq", 2)
+    d_got = [d[0], swap(d[1], "seq", 1), d_two]
+    onward = [d_got[1][:, :joined], d_got[1][:, joined + wide // 2 :]]
+    onward = jnp.concatenate(onward, axis=1)
+    d_got.append(swap(onward, "seq", 2))
     d, u_part = lax.optimization_barrier((d, u_part))
     kept = weight_grad(0, d)
     total = kept + sent
     u_own = jnp.stack([u_rows, *u_part, swap(u_part[0], "fsdp", 4)])
-    d_got[2], u_own = lax.optimization_barrier((d_got[2], u_own))
     u_other = swap(u_own, "fsdp", 1)
     got = [swap(total[i], "fsdp", 2 * i) for i in (1, 2, 3)]
     factor = 1.0 / math.sqrt(4 * rows * lax.axis_size("fsdp"))
@@ -433,15 +446,14 @@
     half = swap(send, "seq", 2)
 
     attended = vmem_call(
-        attended_join_kernel, shape(rows, 4 * wide)
+        attended_join_kernel, shape(rows, 4 * wide), smem=1
     )(place, *d_got)
-    weights = vmem_call(
-        weight_join_kernel,
-        [shape(depth, 4 * wide), shape(depth, 4 * narrow), shape(depth, 4 * narrow)],
+    grad_wq, grad_wk, grad_wv, grad_in = vmem_call(
+        join_kernel,
+        [shape(depth, 4 * wide), shape(depth, 4 * narrow), shape(depth, 4 * narrow)]
+        + [shape(rows, width)],
         smem=1,
-    )(place, *w_final)
-    grad_wq, grad_wk, grad_wv = weights
-    grad_in = vmem_call(token_join_kernel, shape(rows, width), smem=1)(place, own, half)
+    )(place, *w_final, own, half)
     return attended[None], grad_in[None], grad_wq, grad_wk, grad_wv
 
 

time: 115 us -> 114 us (level)
  waiting for transfers between devices: 58.5 us -> 62.9 us
  starting transfers between devices: 34.7 us -> 30.6 us
    ppermute x25, waiting for transfers between devices: 58.5 us -> 62.9 us  [swap(): return lax.ppermute(x, axis, [(i, i ^ j) for i in range(n)])]
    ppermute x25, starting transfers between devices: 34.7 us -> 30.6 us  [swap(): return lax.ppermute(x, axis, [(i, i ^ j) for i in range(n)])]
    pallas_call x8 -> x7, Pallas kernels: 15.8 us -> 15 us  [call(): pl.pallas_call(kernel, out_shape=out_shape, in_specs=in_specs, out_specs=...]
  transfers between devices with their start and end apart: 25 -> 25, of which waited for: 11 -> 11; matrix products, arithmetic and copies ran while one was open for 1% -> 1% of each run, Pallas kernels for 13% -> 12%
where the time goes in v4:
time: 114 us
  waiting for transfers between devices  62.9 us (55%)
  starting transfers between devices  30.6 us (27%)
  Pallas kernels  15 us (13%)
  local copies, waits for them, and re-layouts  3.55 us (3%)
    ppermute x25, waiting for transfers between devices, swap(): return lax.ppermute(x, axis, [(i, i ^ j) for i in range(n)])  62.9 us
    ppermute x25, starting transfers between devices, swap(): return lax.ppermute(x, axis, [(i, i ^ j) for i in range(n)])  30.6 us
    pallas_call x7, Pallas kernels, call(): pl.pallas_call(kernel, out_shape=out_shape, in_specs=in_specs, out_specs=...  15 us
    unnamed x12, local copies, waits for them, and re-layouts  3.38 us
  transfers between devices with their start and end apart: 25, of which 11 were waited for; matrix products, arithmetic and copies ran while one was open for 1% of the time, Pallas kernels for 12%

profile of v4, /device:TPU:0, one launch (start us, length us, event | category | flops | bytes accessed | tf_op | source)
XLA Modules:
  0.0 113.8 jit_solution(4096947706074732459)
XLA Ops:
  0.6 4.1 %collective-permute-start.3 = (bf16[128,2048]{1,0:T(8,128)(2,1)}, bf16[128,2048]{1,0:T(8,128)(2,1)S(1)}, u32[]{:S(2)}, u32[]{:S(2)}) collective-permute-start(bf16[128,2048]{1,0:T(8,128)(2,1)} %bitcast.53), channel_id=1, source_target_pairs={{0,2},{1,3},{2,0},{3,1},{4,6},{5,7},{6,4},{7,5},{8,10},{9,11},{10,... | collective-permute-start | bytes 1572872 | tf_op jit(solution)/shard_map/ppermute | solution.py:104
  4.7 0.1 pad_add_fusion.place_ref
  4.8 0.9 copy-done
  5.8 0.9 copy-done.1
  6.7 0.8 copy-done.2
  7.4 0.8 copy-done.3
  8.2 1.1 shard_map.101
  9.3 1.6 %collective-permute-start = (bf16[64,2048]{1,0:T(8,128)(2,1)S(1)}, bf16[64,2048]{1,0:T(8,128)(2,1)S(1)}, u32[]{:S(2)}, u32[]{:S(2)}) collective-permute-start(bf16[64,2048]{1,0:T(8,128)(2,1)S(1)} %get-tuple-element.37), channel_id=1, source_target_pairs={{0,1},{1,0},{2,3},{3,2},{4,5},{5,4},{6,7},{7,6},{8,9},{9,8},{10,11... | collective-permute-start | bytes 786440 | tf_op jit(solution)/shard_map/ppermute | solution.py:104
  10.9 0.3 collective-permute-start.1
  11.2 2.5 %collective-permute-start.2 = (bf16[64,896]{1,0:T(8,128)(2,1)S(1)}, bf16[64,896]{1,0:T(8,128)(2,1)S(1)}, u32[]{:S(2)}, u32[]{:S(2)}) collective-permute-start(bf16[64,896]{1,0:T(8,128)(2,1)S(1)} %get-tuple-element.39), channel_id=1, source_target_pairs={{0,3},{1,2},{2,1},{3,0},{4,7},{5,6},{6,5},{7,4},{8,11},{9,10},{10,... | collective-permute-start | bytes 344072 | tf_op jit(solution)/shard_map/ppermute | solution.py:104
  13.7 0.7 collective-permute-start.7
  14.4 22.0 %collective-permute-done.1.refs_8_ = bf16[64,896]{1,0:T(8,128)(2,1)S(1)} collective-permute-done((bf16[64,896]{1,0:T(8,128)(2,1)S(1)}, bf16[64,896]{1,0:T(8,128)(2,1)S(1)}, u32[]{:S(2)}, u32[]{:S(2)}) %collective-permute-start.1) | collective-permute-done | bytes 114720 | tf_op jit(solution)/shard_map/ppermute | solution.py:104
  36.5 2.9 %collective-permute-start.6 = (bf16[4,64,384]{2,1,0:T(8,128)(2,1)S(1)}, bf16[4,64,384]{2,1,0:T(8,128)(2,1)S(1)}, u32[]{:S(2)}, u32[]{:S(2)}) collective-permute-start(bf16[4,64,384]{2,1,0:T(8,128)(2,1)S(1)} %get-tuple-element.77), channel_id=1, source_target_pairs={{0,24},{4,28},{8,16},{12,20},{16,8},{20,12},{24,0},{28,4},{1,25},{... | collective-permute-start | bytes 589832 | tf_op jit(solution)/shard_map/ppermute | solution.py:104
  39.3 0.5 collective-permute-start.5
  39.8 0.2 collective-permute-start.4
  40.0 2.3 %collective-permute-start.8 = (bf16[128,2048]{1,0:T(8,128)(2,1)S(1)}, bf16[128,2048]{1,0:T(8,128)(2,1)S(1)}, u32[]{:S(2)}, u32[]{:S(2)}) collective-permute-start(bf16[128,2048]{1,0:T(8,128)(2,1)S(1)} %collective-permute-done.3.refs_2_.x2), channel_id=1, source_target_pairs={{0,1},{1,0},{2,3},{3,2},{4,5},{5,4},{6,7},{7,6},{8,9},{9,8},{10,11... | collective-permute-start | bytes 1572872 | tf_op jit(solution)/shard_map/ppermute | solution.py:104
  42.4 2.5 %collective-permute-done.6 = bf16[4,64,384]{2,1,0:T(8,128)(2,1)S(1)} collective-permute-done((bf16[4,64,384]{2,1,0:T(8,128)(2,1)S(1)}, bf16[4,64,384]{2,1,0:T(8,128)(2,1)S(1)}, u32[]{:S(2)}, u32[]{:S(2)}) %collective-permute-start.6) | collective-permute-done | bytes 196640 | tf_op jit(solution)/shard_map/ppermute | solution.py:104
  44.9 1.2 %collective-permute-start.13 = (bf16[2,64,1152]{2,1,0:T(8,128)(2,1)S(1)}, bf16[2,64,1152]{2,1,0:T(8,128)(2,1)S(1)}, u32[]{:S(2)}, u32[]{:S(2)}) collective-permute-start(bf16[2,64,1152]{2,1,0:T(8,128)(2,1)S(1)} %get-tuple-element.71), channel_id=1, source_target_pairs={{0,8},{4,12},{8,0},{12,4},{16,24},{20,28},{24,16},{28,20},{1,9},{5... | collective-permute-start | bytes 884744 | tf_op jit(solution)/shard_map/ppermute | solution.py:104
  46.2 0.7 collective-permute-done.5
  46.9 1.3 %collective-permute-start.14 = (bf16[2,64,1152]{2,1,0:T(8,128)(2,1)S(1)}, bf16[2,64,1152]{2,1,0:T(8,128)(2,1)S(1)}, u32[]{:S(2)}, u32[]{:S(2)}) collective-permute-start(bf16[2,64,1152]{2,1,0:T(8,128)(2,1)S(1)} %get-tuple-element.71), channel_id=1, source_target_pairs={{0,16},{4,20},{8,24},{12,28},{16,0},{20,4},{24,8},{28,12},{1,17},{... | collective-permute-start | bytes 884744 | tf_op jit(solution)/shard_map/ppermute | solution.py:104
  48.2 1.2 %collective-permute-done.4 = bf16[4,64,384]{2,1,0:T(8,128)(2,1)S(1)} collective-permute-done((bf16[4,64,384]{2,1,0:T(8,128)(2,1)S(1)}, bf16[4,64,384]{2,1,0:T(8,128)(2,1)S(1)}, u32[]{:S(2)}, u32[]{:S(2)}) %collective-permute-start.4) | collective-permute-done | bytes 196640 | tf_op jit(solution)/shard_map/ppermute | solution.py:104
  49.4 0.1 pad_maximum_fusion.1.refs_4_.refs_0_
  49.7 4.9 %collective-permute-done.8.refs_0_.refs_3_.x3 = bf16[128,2048]{1,0:T(8,128)(2,1)S(1)} collective-permute-done((bf16[128,2048]{1,0:T(8,128)(2,1)S(1)}, bf16[128,2048]{1,0:T(8,128)(2,1)S(1)}, u32[]{:S(2)}, u32[]{:S(2)}) %collective-permute-start.8) | collective-permute-done | bytes 524320 | tf_op jit(solution)/shard_map/ppermute | solution.py:104
  54.6 6.7 %shard_map.103 = (bf16[256,512]{1,0:T(8,128)(2,1)S(1)}, bf16[256,640]{1,0:T(8,128)(2,1)S(1)}, bf16[256,512]{1,0:T(8,128)(2,1)S(1)}) custom-call(s32[2]{0:T(128)S(1)} %pad_add_fusion.place_ref, s32[8,8]{1,0:T(8,128)S(1)} %copy-done.5, bf16[128,2048]{1,0:T(8,128)(2,1)S(1)} %bitcast.55, bf16[128,2048]{1,0:T(8,128)(2,1)S(1)} %collective-permute-done.7.refs_1_.x1, ...), custom_call_target="tpu_custom_call" | custom-call | flops 8589934592 | bytes 4194304 | tf_op jit(solution)/shard_map/pallas_call | solution.py:128
  61.2 1.3 %shard_map.104 = f32[4,4,64,384]{3,2,1,0:T(8,128)S(1)} custom-call(s32[2]{0:T(128)S(1)} %pad_add_fusion.place_ref, bf16[128,2048]{1,0:T(8,128)(2,1)S(1)} %bitcast.56, bf16[128,2048]{1,0:T(8,128)(2,1)S(1)} %collective-permute-done.7.refs_1_.x1, bf16[128,2048]{1,0:T(8,128)(2,1)S(1)} %collective-permute-done.3.refs_2_.x2, ...), custom_call_target="tpu_custom_call" | custom-call | flops 8589934592 | bytes 4194304 | tf_op jit(solution)/shard_map/pallas_call | solution.py:128
  62.7 1.6 %collective-permute-start.22 = (bf16[2,64,1152]{2,1,0:T(8,128)(2,1)S(1)}, bf16[2,64,1152]{2,1,0:T(8,128)(2,1)S(1)}, u32[]{:S(2)}, u32[]{:S(2)}) collective-permute-start(bf16[2,64,1152]{2,1,0:T(8,128)(2,1)S(1)} %collective-permute-done.13), channel_id=1, source_target_pairs={{0,16},{4,20},{8,24},{12,28},{16,0},{20,4},{24,8},{28,12},{1,17},{... | collective-permute-start | bytes 884744 | tf_op jit(solution)/shard_map/ppermute | solution.py:104
  64.3 0.8 collective-permute-start.10
  65.1 2.2 %collective-permute-start.11 = (bf16[256,512]{1,0:T(8,128)(2,1)S(1)}, bf16[256,512]{1,0:T(8,128)(2,1)S(1)}, u32[]{:S(2)}, u32[]{:S(2)}) collective-permute-start(bf16[256,512]{1,0:T(8,128)(2,1)S(1)} %get-tuple-element.54), channel_id=1, source_target_pairs={{0,2},{1,3},{2,0},{3,1},{4,6},{5,7},{6,4},{7,5},{8,10},{9,11},{10,... | collective-permute-start | bytes 786440 | tf_op jit(solution)/shard_map/ppermute | solution.py:104
  67.3 4.8 %collective-permute-done.22 = bf16[2,64,1152]{2,1,0:T(8,128)(2,1)S(1)} collective-permute-done((bf16[2,64,1152]{2,1,0:T(8,128)(2,1)S(1)}, bf16[2,64,1152]{2,1,0:T(8,128)(2,1)S(1)}, u32[]{:S(2)}, u32[]{:S(2)}) %collective-permute-start.22) | collective-permute-done | bytes 294944 | tf_op jit(solution)/shard_map/ppermute | solution.py:104
  72.1 0.2 pad_maximum_fusion.refs_2_
  72.3 1.3 %shard_map.106 = f32[4,4,64,384]{3,2,1,0:T(8,128)S(1)} custom-call(s32[2]{0:T(128)S(1)} %pad_add_fusion.place_ref, bf16[128,2048]{1,0:T(8,128)(2,1)S(1)} %bitcast.57, bf16[128,2048]{1,0:T(8,128)(2,1)S(1)} %collective-permute-done.7.refs_1_.x1, bf16[128,2048]{1,0:T(8,128)(2,1)S(1)} %collective-permute-done.3.refs_2_.x2, ...), custom_call_target="tpu_custom_call" | custom-call | flops 8589934592 | bytes 4194304 | tf_op jit(solution)/shard_map/pallas_call | solution.py:128
  73.6 6.0 %collective-permute-done.10.d1 = bf16[256,640]{1,0:T(8,128)(2,1)S(1)} collective-permute-done((bf16[256,640]{1,0:T(8,128)(2,1)S(1)}, bf16[256,640]{1,0:T(8,128)(2,1)S(1)}, u32[]{:S(2)}, u32[]{:S(2)}) %collective-permute-start.10) | collective-permute-done | bytes 327712 | tf_op jit(solution)/shard_map/ppermute | solution.py:104
  79.8 0.2 add.12
  80.1 0.1 slice_bitcast_fusion
  80.2 1.5 %collective-permute-start.16 = (f32[4,64,384]{2,1,0:T(8,128)S(1)}, f32[4,64,384]{2,1,0:T(8,128)S(1)}, u32[]{:S(2)}, u32[]{:S(2)}) collective-permute-start(f32[4,64,384]{2,1,0:T(8,128)S(1)} %get-tuple-element.69), channel_id=1, source_target_pairs={{0,8},{4,12},{8,0},{12,4},{16,24},{20,28},{24,16},{28,20},{1,9},{5... | collective-permute-start | bytes 1179656 | tf_op jit(solution)/shard_map/ppermute | solution.py:104
  81.7 0.5 collective-permute-start.17
  82.2 1.5 %collective-permute-start.18 = (f32[4,64,384]{2,1,0:T(8,128)S(1)}, f32[4,64,384]{2,1,0:T(8,128)S(1)}, u32[]{:S(2)}, u32[]{:S(2)}) collective-permute-start(f32[4,64,384]{2,1,0:T(8,128)S(1)} %get-tuple-element.67), channel_id=1, source_target_pairs={{0,24},{4,28},{8,16},{12,20},{16,8},{20,12},{24,0},{28,4},{1,25},{... | collective-permute-start | bytes 1179656 | tf_op jit(solution)/shard_map/ppermute | solution.py:104
  83.7 9.3 %collective-permute-done.12.d3 = bf16[256,512]{1,0:T(8,128)(2,1)S(1)} collective-permute-done((bf16[256,512]{1,0:T(8,128)(2,1)S(1)}, bf16[256,512]{1,0:T(8,128)(2,1)S(1)}, u32[]{:S(2)}, u32[]{:S(2)}) %collective-permute-start.12) | collective-permute-done | bytes 262176 | tf_op jit(solution)/shard_map/ppermute | solution.py:104
  93.0 1.9 %shard_map.107 = (bf16[128,1024]{1,0:T(8,128)(2,1)S(1)}, bf16[128,1024]{1,0:T(8,128)(2,1)S(1)}) custom-call(s32[2]{0:T(128)S(1)} %pad_add_fusion.place_ref, bf16[256,512]{1,0:T(8,128)(2,1)S(1)} %get-tuple-element.56.d0_ref.d0, bf16[256,640]{1,0:T(8,128)(2,1)S(1)} %collective-permute-done.10.d1, bf16[256,512]{1,0:T(8,128)(2,1)S(1)} %collective-permute-done.11.d2, ...), custom_call_target="tpu_custom_call" | custom-call | flops 2147483648 | bytes 4194304 | tf_op jit(solution)/shard_map/pallas_call | solution.py:128
  95.0 5.2 %collective-permute-done.17 = f32[4,64,384]{2,1,0:T(8,128)S(1)} collective-permute-done((f32[4,64,384]{2,1,0:T(8,128)S(1)}, f32[4,64,384]{2,1,0:T(8,128)S(1)}, u32[]{:S(2)}, u32[]{:S(2)}) %collective-permute-start.17) | collective-permute-done | bytes 393248 | tf_op jit(solution)/shard_map/ppermute | solution.py:104
  100.2 0.1 fusion.3
  100.4 2.0 %collective-permute-start.19 = (bf16[64,384]{1,0:T(8,128)(2,1)S(1)}, bf16[64,384]{1,0:T(8,128)(2,1)S(1)}, u32[]{:S(2)}, u32[]{:S(2)}) collective-permute-start(bf16[64,384]{1,0:T(8,128)(2,1)S(1)} %get-tuple-element.74), channel_id=1, source_target_pairs={{0,1},{1,0},{2,3},{3,2},{4,5},{5,4},{6,7},{7,6},{8,9},{9,8},{10,11... | collective-permute-start | bytes 147464 | tf_op jit(solution)/shard_map/ppermute | solution.py:104
  102.3 0.8 collective-permute-start.20
  103.1 1.7 %collective-permute-start.21 = (bf16[64,384]{1,0:T(8,128)(2,1)S(1)}, bf16[64,384]{1,0:T(8,128)(2,1)S(1)}, u32[]{:S(2)}, u32[]{:S(2)}) collective-permute-start(bf16[64,384]{1,0:T(8,128)(2,1)S(1)} %get-tuple-element.72), channel_id=1, source_target_pairs={{0,3},{1,2},{2,1},{3,0},{4,7},{5,6},{6,5},{7,4},{8,11},{9,10},{10,... | collective-permute-start | bytes 147464 | tf_op jit(solution)/shard_map/ppermute | solution.py:104
  104.8 1.3 %shard_map.105 = bf16[128,1024]{1,0:T(8,128)(2,1)} custom-call(s32[2]{0:T(128)S(1)} %pad_add_fusion.place_ref, bf16[256,512]{1,0:T(8,128)(2,1)S(1)} %get-tuple-element.56.d0_ref.d0, bf16[256,640]{1,0:T(8,128)(2,1)S(1)} %collective-permute-done.10.d1, bf16[256,512]{1,0:T(8,128)(2,1)S(1)} %collective-permute-done.11.d2, ...), custom_call_target="tpu_custom_call" | custom-call | bytes 4194304 | tf_op jit(solution)/shard_map/pallas_call | solution.py:128
  106.1 5.2 %collective-permute-done.24.got = bf16[128,1024]{1,0:T(8,128)(2,1)S(1)} collective-permute-done((bf16[128,1024]{1,0:T(8,128)(2,1)S(1)}, bf16[128,1024]{1,0:T(8,128)(2,1)S(1)}, u32[]{:S(2)}, u32[]{:S(2)}) %collective-permute-start.24) | collective-permute-done | bytes 262176 | tf_op jit(solution)/shard_map/ppermute | solution.py:104
  111.3 1.0 collective-permute-done.20.b2
  112.4 1.5 %shard_map.108 = (bf16[64,1024]{1,0:T(8,128)(2,1)}, bf16[64,256]{1,0:T(8,128)(2,1)}, bf16[64,256]{1,0:T(8,128)(2,1)}, bf16[128,2048]{1,0:T(8,128)(2,1)}) custom-call(s32[2]{0:T(128)S(1)} %pad_add_fusion.place_ref, bf16[64,384]{1,0:T(8,128)(2,1)S(1)} %get-tuple-element.75.b0, bf16[64,384]{1,0:T(8,128)(2,1)S(1)} %collective-permute-done.19.b1, ...), custom_call_target="tpu_custom_call" | custom-call | bytes 4194304 | tf_op jit(solution)/shard_map/pallas_call | solution.py:128
  (37 shorter events, 0.6 us)
Async XLA Ops:
  0.6 35.7 %collective-permute-start.3 = (bf16[128,2048]{1,0:T(8,128)(2,1)}, bf16[128,2048]{1,0:T(8,128)(2,1)S(1)}, u32[]{:S(2)}, u32[]{:S(2)}) collective-permute-start(bf16[128,2048]{1,0:T(8,128)(2,1)} %bitcast.53), channel_id=1, source_target_pairs={{0,2},{1,3},{2,0},{3,1},{4,6},{5,7},{6,4},{7,5},{8,10},{9,11},{10,... | collective-permute-start | bytes 1572872 | tf_op jit(solution)/shard_map/ppermute | solution.py:104
  4.8 0.9 copy-start
  5.8 0.9 copy-start.1
  6.7 0.8 copy-start.2
  7.4 0.8 copy-start.3
  9.3 27.1 %collective-permute-start = (bf16[64,2048]{1,0:T(8,128)(2,1)S(1)}, bf16[64,2048]{1,0:T(8,128)(2,1)S(1)}, u32[]{:S(2)}, u32[]{:S(2)}) collective-permute-start(bf16[64,2048]{1,0:T(8,128)(2,1)S(1)} %get-tuple-element.37), channel_id=1, source_target_pairs={{0,1},{1,0},{2,3},{3,2},{4,5},{5,4},{6,7},{7,6},{8,9},{9,8},{10,11... | collective-permute-start | bytes 786440 | tf_op jit(solution)/shard_map/ppermute | solution.py:104
  10.9 25.5 %collective-permute-start.1 = (bf16[64,896]{1,0:T(8,128)(2,1)S(1)}, bf16[64,896]{1,0:T(8,128)(2,1)S(1)}, u32[]{:S(2)}, u32[]{:S(2)}) collective-permute-start(bf16[64,896]{1,0:T(8,128)(2,1)S(1)} %get-tuple-element.38), channel_id=1, source_target_pairs={{0,2},{1,3},{2,0},{3,1},{4,6},{5,7},{6,4},{7,5},{8,10},{9,11},{10,... | collective-permute-start | bytes 344072 | tf_op jit(solution)/shard_map/ppermute | solution.py:104
  11.2 25.1 %collective-permute-start.2 = (bf16[64,896]{1,0:T(8,128)(2,1)S(1)}, bf16[64,896]{1,0:T(8,128)(2,1)S(1)}, u32[]{:S(2)}, u32[]{:S(2)}) collective-permute-start(bf16[64,896]{1,0:T(8,128)(2,1)S(1)} %get-tuple-element.39), channel_id=1, source_target_pairs={{0,3},{1,2},{2,1},{3,0},{4,7},{5,6},{6,5},{7,4},{8,11},{9,10},{10,... | collective-permute-start | bytes 344072 | tf_op jit(solution)/shard_map/ppermute | solution.py:104
  13.7 35.9 %collective-permute-start.7 = (bf16[128,2048]{1,0:T(8,128)(2,1)}, bf16[128,2048]{1,0:T(8,128)(2,1)S(1)}, u32[]{:S(2)}, u32[]{:S(2)}) collective-permute-start(bf16[128,2048]{1,0:T(8,128)(2,1)} %bitcast.54), channel_id=1, source_target_pairs={{0,1},{1,0},{2,3},{3,2},{4,5},{5,4},{6,7},{7,6},{8,9},{9,8},{10,11... | collective-permute-start | bytes 1572872 | tf_op jit(solution)/shard_map/ppermute | solution.py:104
  36.5 8.5 %collective-permute-start.6 = (bf16[4,64,384]{2,1,0:T(8,128)(2,1)S(1)}, bf16[4,64,384]{2,1,0:T(8,128)(2,1)S(1)}, u32[]{:S(2)}, u32[]{:S(2)}) collective-permute-start(bf16[4,64,384]{2,1,0:T(8,128)(2,1)S(1)} %get-tuple-element.77), channel_id=1, source_target_pairs={{0,24},{4,28},{8,16},{12,20},{16,8},{20,12},{24,0},{28,4},{1,25},{... | collective-permute-start | bytes 589832 | tf_op jit(solution)/shard_map/ppermute | solution.py:104
  39.3 7.6 %collective-permute-start.5 = (bf16[4,64,384]{2,1,0:T(8,128)(2,1)S(1)}, bf16[4,64,384]{2,1,0:T(8,128)(2,1)S(1)}, u32[]{:S(2)}, u32[]{:S(2)}) collective-permute-start(bf16[4,64,384]{2,1,0:T(8,128)(2,1)S(1)} %get-tuple-element.77), channel_id=1, source_target_pairs={{0,16},{4,20},{8,24},{12,28},{16,0},{20,4},{24,8},{28,12},{1,17},{... | collective-permute-start | bytes 589832 | tf_op jit(solution)/shard_map/ppermute | solution.py:104
  39.8 9.6 %collective-permute-start.4 = (bf16[4,64,384]{2,1,0:T(8,128)(2,1)S(1)}, bf16[4,64,384]{2,1,0:T(8,128)(2,1)S(1)}, u32[]{:S(2)}, u32[]{:S(2)}) collective-permute-start(bf16[4,64,384]{2,1,0:T(8,128)(2,1)S(1)} %get-tuple-element.77), channel_id=1, source_target_pairs={{0,8},{4,12},{8,0},{12,4},{16,24},{20,28},{24,16},{28,20},{1,9},{5... | collective-permute-start | bytes 589832 | tf_op jit(solution)/shard_map/ppermute | solution.py:104
  40.0 14.5 %collective-permute-start.8 = (bf16[128,2048]{1,0:T(8,128)(2,1)S(1)}, bf16[128,2048]{1,0:T(8,128)(2,1)S(1)}, u32[]{:S(2)}, u32[]{:S(2)}) collective-permute-start(bf16[128,2048]{1,0:T(8,128)(2,1)S(1)} %collective-permute-done.3.refs_2_.x2), channel_id=1, source_target_pairs={{0,1},{1,0},{2,3},{3,2},{4,5},{5,4},{6,7},{7,6},{8,9},{9,8},{10,11... | collective-permute-start | bytes 1572872 | tf_op jit(solution)/shard_map/ppermute | solution.py:104
  44.9 17.7 %collective-permute-start.13 = (bf16[2,64,1152]{2,1,0:T(8,128)(2,1)S(1)}, bf16[2,64,1152]{2,1,0:T(8,128)(2,1)S(1)}, u32[]{:S(2)}, u32[]{:S(2)}) collective-permute-start(bf16[2,64,1152]{2,1,0:T(8,128)(2,1)S(1)} %get-tuple-element.71), channel_id=1, source_target_pairs={{0,8},{4,12},{8,0},{12,4},{16,24},{20,28},{24,16},{28,20},{1,9},{5... | collective-permute-start | bytes 884744 | tf_op jit(solution)/shard_map/ppermute | solution.py:104
  46.9 15.8 %collective-permute-start.14 = (bf16[2,64,1152]{2,1,0:T(8,128)(2,1)S(1)}, bf16[2,64,1152]{2,1,0:T(8,128)(2,1)S(1)}, u32[]{:S(2)}, u32[]{:S(2)}) collective-permute-start(bf16[2,64,1152]{2,1,0:T(8,128)(2,1)S(1)} %get-tuple-element.71), channel_id=1, source_target_pairs={{0,16},{4,20},{8,24},{12,28},{16,0},{20,4},{24,8},{28,12},{1,17},{... | collective-permute-start | bytes 884744 | tf_op jit(solution)/shard_map/ppermute | solution.py:104
  49.6 5.0 %copy-start.4 = (bf16[1,128,2048]{2,1,0:T(8,128)(2,1)S(1)}, bf16[1,128,2048]{2,1,0:T(8,128)(2,1)}, u32[]{:S(2)}) copy-start(bf16[1,128,2048]{2,1,0:T(8,128)(2,1)} %param.6) | copy-start | bytes 1572868
  49.6 5.0 %copy-start.5 = (s32[8,8]{1,0:T(8,128)S(1)}, s32[8,8]{1,0:T(8,128)}, u32[]{:S(2)}) copy-start(s32[8,8]{1,0:T(8,128)} %adjacency_ref.1) | copy-start | bytes 772
  49.6 5.0 %collective-permute-start.9 = (bf16[4,4,64,384]{3,2,1,0:T(8,128)(2,1)S(1)}, bf16[4,4,64,384]{3,2,1,0:T(8,128)(2,1)S(1)}, u32[]{:S(2)}, u32[]{:S(2)}) collective-permute-start(bf16[4,4,64,384]{3,2,1,0:T(8,128)(2,1)S(1)} %pad_maximum_fusion.1.refs_4_.refs_0_), channel_id=1, source_target_pairs={{0,4},{4,0},{8,12},{12,8},{16,20},{20,16},{24,28},{28,24},{1,5},{5... | collective-permute-start | bytes 2359304 | tf_op jit(solution)/shard_map/ppermute | solution.py:104
  62.6 17.3 %collective-permute-start.15 = (f32[4,4,64,384]{3,2,1,0:T(8,128)S(1)}, f32[4,4,64,384]{3,2,1,0:T(8,128)S(1)}, u32[]{:S(2)}, u32[]{:S(2)}) collective-permute-start(f32[4,4,64,384]{3,2,1,0:T(8,128)S(1)} %shard_map.104), channel_id=1, source_target_pairs={{0,4},{4,0},{8,12},{12,8},{16,20},{20,16},{24,28},{28,24},{1,5},{5... | collective-permute-start | bytes 4718600 | tf_op jit(solution)/shard_map/ppermute | solution.py:104
  62.7 9.4 %collective-permute-start.22 = (bf16[2,64,1152]{2,1,0:T(8,128)(2,1)S(1)}, bf16[2,64,1152]{2,1,0:T(8,128)(2,1)S(1)}, u32[]{:S(2)}, u32[]{:S(2)}) collective-permute-start(bf16[2,64,1152]{2,1,0:T(8,128)(2,1)S(1)} %collective-permute-done.13), channel_id=1, source_target_pairs={{0,16},{4,20},{8,24},{12,28},{16,0},{20,4},{24,8},{28,12},{1,17},{... | collective-permute-start | bytes 884744 | tf_op jit(solution)/shard_map/ppermute | solution.py:104
  64.3 15.4 %collective-permute-start.10 = (bf16[256,640]{1,0:T(8,128)(2,1)S(1)}, bf16[256,640]{1,0:T(8,128)(2,1)S(1)}, u32[]{:S(2)}, u32[]{:S(2)}) collective-permute-start(bf16[256,640]{1,0:T(8,128)(2,1)S(1)} %get-tuple-element.57.d1_ref), channel_id=1, source_target_pairs={{0,1},{1,0},{2,3},{3,2},{4,5},{5,4},{6,7},{7,6},{8,9},{9,8},{10,11... | collective-permute-start | bytes 983048 | tf_op jit(solution)/shard_map/ppermute | solution.py:104
  65.1 17.2 %collective-permute-start.11 = (bf16[256,512]{1,0:T(8,128)(2,1)S(1)}, bf16[256,512]{1,0:T(8,128)(2,1)S(1)}, u32[]{:S(2)}, u32[]{:S(2)}) collective-permute-start(bf16[256,512]{1,0:T(8,128)(2,1)S(1)} %get-tuple-element.54), channel_id=1, source_target_pairs={{0,2},{1,3},{2,0},{3,1},{4,6},{5,7},{6,4},{7,5},{8,10},{9,11},{10,... | collective-permute-start | bytes 786440 | tf_op jit(solution)/shard_map/ppermute | solution.py:104
  72.3 20.8 %collective-permute-start.23 = (bf16[4,2,64,1152]{3,2,1,0:T(8,128)(2,1)S(1)}, bf16[4,2,64,1152]{3,2,1,0:T(8,128)(2,1)S(1)}, u32[]{:S(2)}, u32[]{:S(2)}) collective-permute-start(bf16[4,2,64,1152]{3,2,1,0:T(8,128)(2,1)S(1)} %pad_maximum_fusion.refs_2_), channel_id=1, source_target_pairs={{0,4},{4,0},{8,12},{12,8},{16,20},{20,16},{24,28},{28,24},{1,5},{5... | collective-permute-start | bytes 3538952 | tf_op jit(solution)/shard_map/ppermute | solution.py:104
  79.7 13.3 %collective-permute-start.12 = (bf16[256,512]{1,0:T(8,128)(2,1)S(1)}, bf16[256,512]{1,0:T(8,128)(2,1)S(1)}, u32[]{:S(2)}, u32[]{:S(2)}) collective-permute-start(bf16[256,512]{1,0:T(8,128)(2,1)S(1)} %pad_maximum_fusion.3), channel_id=1, source_target_pairs={{0,2},{1,3},{2,0},{3,1},{4,6},{5,7},{6,4},{7,5},{8,10},{9,11},{10,... | collective-permute-start | bytes 786440 | tf_op jit(solution)/shard_map/ppermute | solution.py:104
  80.2 14.8 %collective-permute-start.16 = (f32[4,64,384]{2,1,0:T(8,128)S(1)}, f32[4,64,384]{2,1,0:T(8,128)S(1)}, u32[]{:S(2)}, u32[]{:S(2)}) collective-permute-start(f32[4,64,384]{2,1,0:T(8,128)S(1)} %get-tuple-element.69), channel_id=1, source_target_pairs={{0,8},{4,12},{8,0},{12,4},{16,24},{20,28},{24,16},{28,20},{1,9},{5... | collective-permute-start | bytes 1179656 | tf_op jit(solution)/shard_map/ppermute | solution.py:104
  81.7 18.5 %collective-permute-start.17 = (f32[4,64,384]{2,1,0:T(8,128)S(1)}, f32[4,64,384]{2,1,0:T(8,128)S(1)}, u32[]{:S(2)}, u32[]{:S(2)}) collective-permute-start(f32[4,64,384]{2,1,0:T(8,128)S(1)} %get-tuple-element.68), channel_id=1, source_target_pairs={{0,16},{4,20},{8,24},{12,28},{16,0},{20,4},{24,8},{28,12},{1,17},{... | collective-permute-start | bytes 1179656 | tf_op jit(solution)/shard_map/ppermute | solution.py:104
  82.2 18.0 %collective-permute-start.18 = (f32[4,64,384]{2,1,0:T(8,128)S(1)}, f32[4,64,384]{2,1,0:T(8,128)S(1)}, u32[]{:S(2)}, u32[]{:S(2)}) collective-permute-start(f32[4,64,384]{2,1,0:T(8,128)S(1)} %get-tuple-element.67), channel_id=1, source_target_pairs={{0,24},{4,28},{8,16},{12,20},{16,8},{20,12},{24,0},{28,4},{1,25},{... | collective-permute-start | bytes 1179656 | tf_op jit(solution)/shard_map/ppermute | solution.py:104
  94.9 16.4 %collective-permute-start.24 = (bf16[128,1024]{1,0:T(8,128)(2,1)S(1)}, bf16[128,1024]{1,0:T(8,128)(2,1)S(1)}, u32[]{:S(2)}, u32[]{:S(2)}) collective-permute-start(bf16[128,1024]{1,0:T(8,128)(2,1)S(1)} %get-tuple-element.62), channel_id=1, source_target_pairs={{0,2},{1,3},{2,0},{3,1},{4,6},{5,7},{6,4},{7,5},{8,10},{9,11},{10,... | collective-permute-start | bytes 786440 | tf_op jit(solution)/shard_map/ppermute | solution.py:104
  100.4 11.0 %collective-permute-start.19 = (bf16[64,384]{1,0:T(8,128)(2,1)S(1)}, bf16[64,384]{1,0:T(8,128)(2,1)S(1)}, u32[]{:S(2)}, u32[]{:S(2)}) collective-permute-start(bf16[64,384]{1,0:T(8,128)(2,1)S(1)} %get-tuple-element.74), channel_id=1, source_target_pairs={{0,1},{1,0},{2,3},{3,2},{4,5},{5,4},{6,7},{7,6},{8,9},{9,8},{10,11... | collective-permute-start | bytes 147464 | tf_op jit(solution)/shard_map/ppermute | solution.py:104
  102.3 10.0 %collective-permute-start.20 = (bf16[64,384]{1,0:T(8,128)(2,1)S(1)}, bf16[64,384]{1,0:T(8,128)(2,1)S(1)}, u32[]{:S(2)}, u32[]{:S(2)}) collective-permute-start(bf16[64,384]{1,0:T(8,128)(2,1)S(1)} %get-tuple-element.73), channel_id=1, source_target_pairs={{0,2},{1,3},{2,0},{3,1},{4,6},{5,7},{6,4},{7,5},{8,10},{9,11},{10,... | collective-permute-start | bytes 147464 | tf_op jit(solution)/shard_map/ppermute | solution.py:104
  103.1 9.2 %collective-permute-start.21 = (bf16[64,384]{1,0:T(8,128)(2,1)S(1)}, bf16[64,384]{1,0:T(8,128)(2,1)S(1)}, u32[]{:S(2)}, u32[]{:S(2)}) collective-permute-start(bf16[64,384]{1,0:T(8,128)(2,1)S(1)} %get-tuple-element.72), channel_id=1, source_target_pairs={{0,3},{1,2},{2,1},{3,0},{4,7},{5,6},{6,5},{7,4},{8,11},{9,10},{10,... | collective-permute-start | bytes 147464 | tf_op jit(solution)/shard_map/ppermute | solution.py:104

commit v5 on v4

--- a/solution.py
+++ b/solution.py
@@ -293,7 +293,7 @@
 
 def token_grad_kernel(place_ref, d0, d1, d2, d3, *refs):
     f, s = place_ref[0], place_ref[1]
-    group_refs, rest_refs, own_ref, send_ref = refs[:2], refs[2:4], refs[4], refs[5]
+    group_refs, rest_refs, own_ref, send_ref = refs[:2], refs[2:4], refs[5], refs[6]
     rows = own_ref.shape[0]
     depth, joined = group_refs[0].shape[2:]
     last = (((1,), (1,)), ((), ()))
@@ -339,7 +339,7 @@
         out_ref[:, pl.ds(pl.multiple_of((s ^ j) * 2 * part, 2 * part), 2 * part)] = both
 
 
-def weight_join_kernel(place_ref, b0, b1, b2, b3, q_ref, k_ref, v_ref):
+def weight_join_kernel(place_ref, b0, b1, b2, b3, _, q_ref, k_ref, v_ref):
     s = place_ref[1]
     wide = q_ref.shape[1] // 4
     narrow = k_ref.shape[1] // 4
@@ -354,9 +354,9 @@
     v_ref[...] = jnp.concatenate([b[:, narrow:] for b in two], axis=1)
 
 
-def join_kernel(place_ref, b0, b1, b2, b3, own, got, q_ref, k_ref, v_ref, out_ref):
+def join_kernel(place_ref, b0, b1, b2, b3, mark, own, got, q_ref, k_ref, v_ref, out_ref):
     token_join_kernel(place_ref, own, got, out_ref)
-    weight_join_kernel(place_ref, b0, b1, b2, b3, q_ref, k_ref, v_ref)
+    weight_join_kernel(place_ref, b0, b1, b2, b3, mark, q_ref, k_ref, v_ref)
 
 
 def head_body(tokens, adjacency, w_query, w_key, value_weight, grad_attn):
@@ -420,19 +420,20 @@
         )(place, x0, x1, x2, x3, d[0], d[1])
 
     away = weight_grad(1, d)
-    d, away = lax.optimization_barrier((d, away))
+    d, away, u_part = lax.optimization_barrier((d, away, u_part))
     sent = swap(away, "fsdp", 1)
     d_two = swap(d[2], "seq", 2)
     d_got = [d[0], swap(d[1], "seq", 1), d_two]
     onward = [d_got[1][:, :joined], d_got[1][:, joined + wide // 2 :]]
     onward = jnp.concatenate(onward, axis=1)
     d_got.append(swap(onward, "seq", 2))
-    d, u_part = lax.optimization_barrier((d, u_part))
     kept = weight_grad(0, d)
     total = kept + sent
     u_own = jnp.stack([u_rows, *u_part, swap(u_part[0], "fsdp", 4)])
+    u_own, late = lax.optimization_barrier((u_own, total[0, 0, :8, :128]))
     u_other = swap(u_own, "fsdp", 1)
     got = [swap(total[i], "fsdp", 2 * i) for i in (1, 2, 3)]
+    got, mark = lax.optimization_barrier((got, note(8, *got)))
     factor = 1.0 / math.sqrt(4 * rows * lax.axis_size("fsdp"))
     summed = (((total[0] + got[0]) + (got[1] + got[2])) * factor).astype(BF16)
     w_final = [summed[0]] + [swap(summed[j], "seq", j) for j in (1, 2, 3)]
@@ -441,8 +442,8 @@
         token_grad_kernel,
         [shape(rows, width // 2)] * 2,
         smem=1,
-        total=2 << 30,
-    )(place, *d_got, w_own, w_other, u_own, u_other)
+        total=6 << 30,
+    )(place, *d_got, w_own, w_other, u_own, u_other, late)
     half = swap(send, "seq", 2)
 
     attended = vmem_call(
@@ -453,7 +454,7 @@
         [shape(depth, 4 * wide), shape(depth, 4 * narrow), shape(depth, 4 * narrow)]
         + [shape(rows, width)],
         smem=1,
-    )(place, *w_final, own, half)
+    )(place, *w_final, mark, own, half)
     return attended[None], grad_in[None], grad_wq, grad_wk, grad_wv
 
 

time: 114 us -> 114 us (level)
  starting transfers between devices: 30.6 us -> 33.1 us
  waiting for transfers between devices: 62.9 us -> 60.4 us
    ppermute x25, waiting for transfers between devices: 62.9 us -> 60.4 us  [swap(): return lax.ppermute(x, axis, [(i, i ^ j) for i in range(n)])]
    ppermute x25, starting transfers between devices: 30.6 us -> 33.1 us  [swap(): return lax.ppermute(x, axis, [(i, i ^ j) for i in range(n)])]
  transfers between devices with their start and end apart: 25 -> 25, of which waited for: 11 -> 11; matrix products, arithmetic and copies ran while one was open for 1% -> 1% of each run, Pallas kernels for 12% -> 10%
where the time goes in v5:
time: 114 us
  waiting for transfers between devices  60.4 us (53%)
  starting transfers between devices  33.1 us (29%)
  Pallas kernels  15 us (13%)
  local copies, waits for them, and re-layouts  3.55 us (3%)
    ppermute x25, waiting for transfers between devices, swap(): return lax.ppermute(x, axis, [(i, i ^ j) for i in range(n)])  60.4 us
    ppermute x25, starting transfers between devices, swap(): return lax.ppermute(x, axis, [(i, i ^ j) for i in range(n)])  33.1 us
    pallas_call x7, Pallas kernels, call(): pl.pallas_call(kernel, out_shape=out_shape, in_specs=in_specs, out_specs=...  15 us
    unnamed x12, local copies, waits for them, and re-layouts  3.38 us
  transfers between devices with their start and end apart: 25, of which 11 were waited for; matrix products, arithmetic and copies ran while one was open for 1% of the time, Pallas kernels for 10%

profile of v5, /device:TPU:0, one launch (start us, length us, event | category | flops | bytes accessed | tf_op | source)
XLA Modules:
  0.0 113.8 jit_solution(5541078054256145313)
XLA Ops:
  0.6 4.1 %collective-permute-start.3 = (bf16[128,2048]{1,0:T(8,128)(2,1)}, bf16[128,2048]{1,0:T(8,128)(2,1)S(1)}, u32[]{:S(2)}, u32[]{:S(2)}) collective-permute-start(bf16[128,2048]{1,0:T(8,128)(2,1)} %bitcast.55), channel_id=1, source_target_pairs={{0,2},{1,3},{2,0},{3,1},{4,6},{5,7},{6,4},{7,5},{8,10},{9,11},{10,... | collective-permute-start | bytes 1572872 | tf_op jit(solution)/shard_map/ppermute | solution.py:104
  4.8 0.9 copy-done
  5.8 0.9 copy-done.1
  6.7 0.8 copy-done.2
  7.4 0.8 copy-done.3
  8.2 1.1 shard_map.101
  9.3 1.6 %collective-permute-start = (bf16[64,2048]{1,0:T(8,128)(2,1)S(1)}, bf16[64,2048]{1,0:T(8,128)(2,1)S(1)}, u32[]{:S(2)}, u32[]{:S(2)}) collective-permute-start(bf16[64,2048]{1,0:T(8,128)(2,1)S(1)} %get-tuple-element.41), channel_id=1, source_target_pairs={{0,1},{1,0},{2,3},{3,2},{4,5},{5,4},{6,7},{7,6},{8,9},{9,8},{10,11... | collective-permute-start | bytes 786440 | tf_op jit(solution)/shard_map/ppermute | solution.py:104
  10.9 0.3 collective-permute-start.1
  11.2 2.5 %collective-permute-start.2 = (bf16[64,896]{1,0:T(8,128)(2,1)S(1)}, bf16[64,896]{1,0:T(8,128)(2,1)S(1)}, u32[]{:S(2)}, u32[]{:S(2)}) collective-permute-start(bf16[64,896]{1,0:T(8,128)(2,1)S(1)} %get-tuple-element.43), channel_id=1, source_target_pairs={{0,3},{1,2},{2,1},{3,0},{4,7},{5,6},{6,5},{7,4},{8,11},{9,10},{10,... | collective-permute-start | bytes 344072 | tf_op jit(solution)/shard_map/ppermute | solution.py:104
  13.7 0.7 collective-permute-start.7
  14.4 22.0 %collective-permute-done.1.refs_8_ = bf16[64,896]{1,0:T(8,128)(2,1)S(1)} collective-permute-done((bf16[64,896]{1,0:T(8,128)(2,1)S(1)}, bf16[64,896]{1,0:T(8,128)(2,1)S(1)}, u32[]{:S(2)}, u32[]{:S(2)}) %collective-permute-start.1) | collective-permute-done | bytes 114720 | tf_op jit(solution)/shard_map/ppermute | solution.py:104
  36.5 1.9 %collective-permute-start.5 = (bf16[4,64,384]{2,1,0:T(8,128)(2,1)S(1)}, bf16[4,64,384]{2,1,0:T(8,128)(2,1)S(1)}, u32[]{:S(2)}, u32[]{:S(2)}) collective-permute-start(bf16[4,64,384]{2,1,0:T(8,128)(2,1)S(1)} %get-tuple-element.85), channel_id=1, source_target_pairs={{0,16},{4,20},{8,24},{12,28},{16,0},{20,4},{24,8},{28,12},{1,17},{... | collective-permute-start | bytes 589832 | tf_op jit(solution)/shard_map/ppermute | solution.py:104
  38.4 1.4 %collective-permute-start.6 = (bf16[4,64,384]{2,1,0:T(8,128)(2,1)S(1)}, bf16[4,64,384]{2,1,0:T(8,128)(2,1)S(1)}, u32[]{:S(2)}, u32[]{:S(2)}) collective-permute-start(bf16[4,64,384]{2,1,0:T(8,128)(2,1)S(1)} %get-tuple-element.85), channel_id=1, source_target_pairs={{0,24},{4,28},{8,16},{12,20},{16,8},{20,12},{24,0},{28,4},{1,25},{... | collective-permute-start | bytes 589832 | tf_op jit(solution)/shard_map/ppermute | solution.py:104
  39.8 0.2 collective-permute-start.4
  40.0 2.3 %collective-permute-start.8 = (bf16[128,2048]{1,0:T(8,128)(2,1)S(1)}, bf16[128,2048]{1,0:T(8,128)(2,1)S(1)}, u32[]{:S(2)}, u32[]{:S(2)}) collective-permute-start(bf16[128,2048]{1,0:T(8,128)(2,1)S(1)} %collective-permute-done.3.refs_2_.x2), channel_id=1, source_target_pairs={{0,1},{1,0},{2,3},{3,2},{4,5},{5,4},{6,7},{7,6},{8,9},{9,8},{10,11... | collective-permute-start | bytes 1572872 | tf_op jit(solution)/shard_map/ppermute | solution.py:104
  42.4 3.6 %collective-permute-done.5 = bf16[4,64,384]{2,1,0:T(8,128)(2,1)S(1)} collective-permute-done((bf16[4,64,384]{2,1,0:T(8,128)(2,1)S(1)}, bf16[4,64,384]{2,1,0:T(8,128)(2,1)S(1)}, u32[]{:S(2)}, u32[]{:S(2)}) %collective-permute-start.5) | collective-permute-done | bytes 196640 | tf_op jit(solution)/shard_map/ppermute | solution.py:104
  46.0 0.3 collective-permute-start.10
  46.3 2.5 %collective-permute-start.11 = (bf16[2,64,1152]{2,1,0:T(8,128)(2,1)S(1)}, bf16[2,64,1152]{2,1,0:T(8,128)(2,1)S(1)}, u32[]{:S(2)}, u32[]{:S(2)}) collective-permute-start(bf16[2,64,1152]{2,1,0:T(8,128)(2,1)S(1)} %get-tuple-element.79), channel_id=1, source_target_pairs={{0,16},{4,20},{8,24},{12,28},{16,0},{20,4},{24,8},{28,12},{1,17},{... | collective-permute-start | bytes 884744 | tf_op jit(solution)/shard_map/ppermute | solution.py:104
  48.8 1.0 collective-permute-done.4
  49.8 0.1 pad_maximum_fusion.1.refs_4_.refs_0_
  50.1 4.5 %collective-permute-done.8.refs_0_.refs_3_.x3 = bf16[128,2048]{1,0:T(8,128)(2,1)S(1)} collective-permute-done((bf16[128,2048]{1,0:T(8,128)(2,1)S(1)}, bf16[128,2048]{1,0:T(8,128)(2,1)S(1)}, u32[]{:S(2)}, u32[]{:S(2)}) %collective-permute-start.8) | collective-permute-done | bytes 524320 | tf_op jit(solution)/shard_map/ppermute | solution.py:104
  54.6 6.7 %shard_map.103 = (bf16[256,512]{1,0:T(8,128)(2,1)S(1)}, bf16[256,640]{1,0:T(8,128)(2,1)S(1)}, bf16[256,512]{1,0:T(8,128)(2,1)S(1)}) custom-call(s32[2]{0:T(128)S(1)} %pad_add_fusion.place_ref, s32[8,8]{1,0:T(8,128)S(1)} %copy-done.5, bf16[128,2048]{1,0:T(8,128)(2,1)S(1)} %bitcast.57, bf16[128,2048]{1,0:T(8,128)(2,1)S(1)} %collective-permute-done.7.refs_1_.x1, ...), custom_call_target="tpu_custom_call" | custom-call | flops 8589934592 | bytes 4194304 | tf_op jit(solution)/shard_map/pallas_call | solution.py:128
  61.2 1.3 %shard_map.104 = f32[4,4,64,384]{3,2,1,0:T(8,128)S(1)} custom-call(s32[2]{0:T(128)S(1)} %pad_add_fusion.place_ref, bf16[128,2048]{1,0:T(8,128)(2,1)S(1)} %bitcast.58, bf16[128,2048]{1,0:T(8,128)(2,1)S(1)} %collective-permute-done.7.refs_1_.x1, bf16[128,2048]{1,0:T(8,128)(2,1)S(1)} %collective-permute-done.3.refs_2_.x2, ...), custom_call_target="tpu_custom_call" | custom-call | flops 8589934592 | bytes 4194304 | tf_op jit(solution)/shard_map/pallas_call | solution.py:128
  62.7 1.6 %collective-permute-start.22 = (bf16[2,64,1152]{2,1,0:T(8,128)(2,1)S(1)}, bf16[2,64,1152]{2,1,0:T(8,128)(2,1)S(1)}, u32[]{:S(2)}, u32[]{:S(2)}) collective-permute-start(bf16[2,64,1152]{2,1,0:T(8,128)(2,1)S(1)} %collective-permute-done.10), channel_id=1, source_target_pairs={{0,16},{4,20},{8,24},{12,28},{16,0},{20,4},{24,8},{28,12},{1,17},{... | collective-permute-start | bytes 884744 | tf_op jit(solution)/shard_map/ppermute | solution.py:104
  64.3 0.8 collective-permute-start.12
  65.1 1.3 %shard_map.106 = f32[4,4,64,384]{3,2,1,0:T(8,128)S(1)} custom-call(s32[2]{0:T(128)S(1)} %pad_add_fusion.place_ref, bf16[128,2048]{1,0:T(8,128)(2,1)S(1)} %bitcast.59, bf16[128,2048]{1,0:T(8,128)(2,1)S(1)} %collective-permute-done.7.refs_1_.x1, bf16[128,2048]{1,0:T(8,128)(2,1)S(1)} %collective-permute-done.3.refs_2_.x2, ...), custom_call_target="tpu_custom_call" | custom-call | flops 8589934592 | bytes 4194304 | tf_op jit(solution)/shard_map/pallas_call | solution.py:128
  66.4 2.3 %collective-permute-start.13 = (bf16[256,512]{1,0:T(8,128)(2,1)S(1)}, bf16[256,512]{1,0:T(8,128)(2,1)S(1)}, u32[]{:S(2)}, u32[]{:S(2)}) collective-permute-start(bf16[256,512]{1,0:T(8,128)(2,1)S(1)} %get-tuple-element.59), channel_id=1, source_target_pairs={{0,2},{1,3},{2,0},{3,1},{4,6},{5,7},{6,4},{7,5},{8,10},{9,11},{10,... | collective-permute-start | bytes 786440 | tf_op jit(solution)/shard_map/ppermute | solution.py:104
  68.6 0.2 add.12
  68.9 0.1 slice_bitcast_fusion
  69.0 1.5 %collective-permute-start.16 = (f32[4,64,384]{2,1,0:T(8,128)S(1)}, f32[4,64,384]{2,1,0:T(8,128)S(1)}, u32[]{:S(2)}, u32[]{:S(2)}) collective-permute-start(f32[4,64,384]{2,1,0:T(8,128)S(1)} %get-tuple-element.77), channel_id=1, source_target_pairs={{0,8},{4,12},{8,0},{12,4},{16,24},{20,28},{24,16},{28,20},{1,9},{5... | collective-permute-start | bytes 1179656 | tf_op jit(solution)/shard_map/ppermute | solution.py:104
  70.5 0.5 collective-permute-start.17
  71.0 1.1 collective-permute-done.22
  72.1 2.9 %collective-permute-start.18 = (f32[4,64,384]{2,1,0:T(8,128)S(1)}, f32[4,64,384]{2,1,0:T(8,128)S(1)}, u32[]{:S(2)}, u32[]{:S(2)}) collective-permute-start(f32[4,64,384]{2,1,0:T(8,128)S(1)} %get-tuple-element.75), channel_id=1, source_target_pairs={{0,24},{4,28},{8,16},{12,20},{16,8},{20,12},{24,0},{28,4},{1,25},{... | collective-permute-start | bytes 1179656 | tf_op jit(solution)/shard_map/ppermute | solution.py:104
  75.0 0.2 pad_maximum_fusion.refs_2_
  75.2 4.5 %collective-permute-done.12.d1 = bf16[256,640]{1,0:T(8,128)(2,1)S(1)} collective-permute-done((bf16[256,640]{1,0:T(8,128)(2,1)S(1)}, bf16[256,640]{1,0:T(8,128)(2,1)S(1)}, u32[]{:S(2)}, u32[]{:S(2)}) %collective-permute-start.12) | collective-permute-done | bytes 327712 | tf_op jit(solution)/shard_map/ppermute | solution.py:104
  79.8 1.2 %collective-permute-done.16.refs_0_ = f32[4,64,384]{2,1,0:T(8,128)S(1)} collective-permute-done((f32[4,64,384]{2,1,0:T(8,128)S(1)}, f32[4,64,384]{2,1,0:T(8,128)S(1)}, u32[]{:S(2)}, u32[]{:S(2)}) %collective-permute-start.16) | collective-permute-done | bytes 393248 | tf_op jit(solution)/shard_map/ppermute | solution.py:104
  81.1 0.7 collective-permute-start.14
  81.8 7.5 %collective-permute-done.17.refs_1_ = f32[4,64,384]{2,1,0:T(8,128)S(1)} collective-permute-done((f32[4,64,384]{2,1,0:T(8,128)S(1)}, f32[4,64,384]{2,1,0:T(8,128)S(1)}, u32[]{:S(2)}, u32[]{:S(2)}) %collective-permute-start.17) | collective-permute-done | bytes 393248 | tf_op jit(solution)/shard_map/ppermute | solution.py:104
  89.3 0.1 fusion.3
  89.4 4.8 %collective-permute-done.14.d3 = bf16[256,512]{1,0:T(8,128)(2,1)S(1)} collective-permute-done((bf16[256,512]{1,0:T(8,128)(2,1)S(1)}, bf16[256,512]{1,0:T(8,128)(2,1)S(1)}, u32[]{:S(2)}, u32[]{:S(2)}) %collective-permute-start.14) | collective-permute-done | bytes 262176 | tf_op jit(solution)/shard_map/ppermute | solution.py:104
  94.2 1.9 %shard_map.108 = (bf16[128,1024]{1,0:T(8,128)(2,1)S(1)}, bf16[128,1024]{1,0:T(8,128)(2,1)S(1)}) custom-call(s32[2]{0:T(128)S(1)} %pad_add_fusion.place_ref, bf16[256,512]{1,0:T(8,128)(2,1)S(1)} %get-tuple-element.57.d0_ref.d0, bf16[256,640]{1,0:T(8,128)(2,1)S(1)} %collective-permute-done.12.d1, bf16[256,512]{1,0:T(8,128)(2,1)S(1)} %collective-permute-done.13.d2, ...), custom_call_target="tpu_custom_call" | custom-call | flops 6442450944 | bytes 4194304 | tf_op jit(solution)/shard_map/pallas_call | solution.py:128
  96.3 2.1 %collective-permute-start.19 = (bf16[64,384]{1,0:T(8,128)(2,1)S(1)}, bf16[64,384]{1,0:T(8,128)(2,1)S(1)}, u32[]{:S(2)}, u32[]{:S(2)}) collective-permute-start(bf16[64,384]{1,0:T(8,128)(2,1)S(1)} %get-tuple-element.82), channel_id=1, source_target_pairs={{0,1},{1,0},{2,3},{3,2},{4,5},{5,4},{6,7},{7,6},{8,9},{9,8},{10,11... | collective-permute-start | bytes 147464 | tf_op jit(solution)/shard_map/ppermute | solution.py:104
  98.3 1.0 collective-permute-start.20
  99.3 1.5 %collective-permute-start.21 = (bf16[64,384]{1,0:T(8,128)(2,1)S(1)}, bf16[64,384]{1,0:T(8,128)(2,1)S(1)}, u32[]{:S(2)}, u32[]{:S(2)}) collective-permute-start(bf16[64,384]{1,0:T(8,128)(2,1)S(1)} %get-tuple-element.80), channel_id=1, source_target_pairs={{0,3},{1,2},{2,1},{3,0},{4,7},{5,6},{6,5},{7,4},{8,11},{9,10},{10,... | collective-permute-start | bytes 147464 | tf_op jit(solution)/shard_map/ppermute | solution.py:104
  100.8 1.3 %shard_map.105 = bf16[128,1024]{1,0:T(8,128)(2,1)} custom-call(s32[2]{0:T(128)S(1)} %pad_add_fusion.place_ref, bf16[256,512]{1,0:T(8,128)(2,1)S(1)} %get-tuple-element.57.d0_ref.d0, bf16[256,640]{1,0:T(8,128)(2,1)S(1)} %collective-permute-done.12.d1, bf16[256,512]{1,0:T(8,128)(2,1)S(1)} %collective-permute-done.13.d2, ...), custom_call_target="tpu_custom_call" | custom-call | bytes 4194304 | tf_op jit(solution)/shard_map/pallas_call | solution.py:128
  102.0 1.9 %collective-permute-done.19.b1 = bf16[64,384]{1,0:T(8,128)(2,1)S(1)} collective-permute-done((bf16[64,384]{1,0:T(8,128)(2,1)S(1)}, bf16[64,384]{1,0:T(8,128)(2,1)S(1)}, u32[]{:S(2)}, u32[]{:S(2)}) %collective-permute-start.19) | collective-permute-done | bytes 49184 | tf_op jit(solution)/shard_map/ppermute | solution.py:104
  104.0 8.4 %collective-permute-done.20.b2 = bf16[64,384]{1,0:T(8,128)(2,1)S(1)} collective-permute-done((bf16[64,384]{1,0:T(8,128)(2,1)S(1)}, bf16[64,384]{1,0:T(8,128)(2,1)S(1)}, u32[]{:S(2)}, u32[]{:S(2)}) %collective-permute-start.20) | collective-permute-done | bytes 49184 | tf_op jit(solution)/shard_map/ppermute | solution.py:104
  112.3 1.5 %shard_map.109 = (bf16[64,1024]{1,0:T(8,128)(2,1)}, bf16[64,256]{1,0:T(8,128)(2,1)}, bf16[64,256]{1,0:T(8,128)(2,1)}, bf16[128,2048]{1,0:T(8,128)(2,1)}) custom-call(s32[2]{0:T(128)S(1)} %pad_add_fusion.place_ref, bf16[64,384]{1,0:T(8,128)(2,1)S(1)} %get-tuple-element.83.b0, bf16[64,384]{1,0:T(8,128)(2,1)S(1)} %collective-permute-done.19.b1, ...), custom_call_target="tpu_custom_call" | custom-call | bytes 4194304 | tf_op jit(solution)/shard_map/pallas_call | solution.py:128
  (39 shorter events, 0.6 us)
Async XLA Ops:
  0.6 35.7 %collective-permute-start.3 = (bf16[128,2048]{1,0:T(8,128)(2,1)}, bf16[128,2048]{1,0:T(8,128)(2,1)S(1)}, u32[]{:S(2)}, u32[]{:S(2)}) collective-permute-start(bf16[128,2048]{1,0:T(8,128)(2,1)} %bitcast.55), channel_id=1, source_target_pairs={{0,2},{1,3},{2,0},{3,1},{4,6},{5,7},{6,4},{7,5},{8,10},{9,11},{10,... | collective-permute-start | bytes 1572872 | tf_op jit(solution)/shard_map/ppermute | solution.py:104
  4.8 0.9 copy-start
  5.8 0.9 copy-start.1
  6.7 0.8 copy-start.2
  7.4 0.8 copy-start.3
  9.3 27.1 %collective-permute-start = (bf16[64,2048]{1,0:T(8,128)(2,1)S(1)}, bf16[64,2048]{1,0:T(8,128)(2,1)S(1)}, u32[]{:S(2)}, u32[]{:S(2)}) collective-permute-start(bf16[64,2048]{1,0:T(8,128)(2,1)S(1)} %get-tuple-element.41), channel_id=1, source_target_pairs={{0,1},{1,0},{2,3},{3,2},{4,5},{5,4},{6,7},{7,6},{8,9},{9,8},{10,11... | collective-permute-start | bytes 786440 | tf_op jit(solution)/shard_map/ppermute | solution.py:104
  10.9 25.5 %collective-permute-start.1 = (bf16[64,896]{1,0:T(8,128)(2,1)S(1)}, bf16[64,896]{1,0:T(8,128)(2,1)S(1)}, u32[]{:S(2)}, u32[]{:S(2)}) collective-permute-start(bf16[64,896]{1,0:T(8,128)(2,1)S(1)} %get-tuple-element.42), channel_id=1, source_target_pairs={{0,2},{1,3},{2,0},{3,1},{4,6},{5,7},{6,4},{7,5},{8,10},{9,11},{10,... | collective-permute-start | bytes 344072 | tf_op jit(solution)/shard_map/ppermute | solution.py:104
  11.2 25.1 %collective-permute-start.2 = (bf16[64,896]{1,0:T(8,128)(2,1)S(1)}, bf16[64,896]{1,0:T(8,128)(2,1)S(1)}, u32[]{:S(2)}, u32[]{:S(2)}) collective-permute-start(bf16[64,896]{1,0:T(8,128)(2,1)S(1)} %get-tuple-element.43), channel_id=1, source_target_pairs={{0,3},{1,2},{2,1},{3,0},{4,7},{5,6},{6,5},{7,4},{8,11},{9,10},{10,... | collective-permute-start | bytes 344072 | tf_op jit(solution)/shard_map/ppermute | solution.py:104
  13.7 36.3 %collective-permute-start.7 = (bf16[128,2048]{1,0:T(8,128)(2,1)}, bf16[128,2048]{1,0:T(8,128)(2,1)S(1)}, u32[]{:S(2)}, u32[]{:S(2)}) collective-permute-start(bf16[128,2048]{1,0:T(8,128)(2,1)} %bitcast.56), channel_id=1, source_target_pairs={{0,1},{1,0},{2,3},{3,2},{4,5},{5,4},{6,7},{7,6},{8,9},{9,8},{10,11... | collective-permute-start | bytes 1572872 | tf_op jit(solution)/shard_map/ppermute | solution.py:104
  36.5 9.5 %collective-permute-start.5 = (bf16[4,64,384]{2,1,0:T(8,128)(2,1)S(1)}, bf16[4,64,384]{2,1,0:T(8,128)(2,1)S(1)}, u32[]{:S(2)}, u32[]{:S(2)}) collective-permute-start(bf16[4,64,384]{2,1,0:T(8,128)(2,1)S(1)} %get-tuple-element.85), channel_id=1, source_target_pairs={{0,16},{4,20},{8,24},{12,28},{16,0},{20,4},{24,8},{28,12},{1,17},{... | collective-permute-start | bytes 589832 | tf_op jit(solution)/shard_map/ppermute | solution.py:104
  38.4 7.9 %collective-permute-start.6 = (bf16[4,64,384]{2,1,0:T(8,128)(2,1)S(1)}, bf16[4,64,384]{2,1,0:T(8,128)(2,1)S(1)}, u32[]{:S(2)}, u32[]{:S(2)}) collective-permute-start(bf16[4,64,384]{2,1,0:T(8,128)(2,1)S(1)} %get-tuple-element.85), channel_id=1, source_target_pairs={{0,24},{4,28},{8,16},{12,20},{16,8},{20,12},{24,0},{28,4},{1,25},{... | collective-permute-start | bytes 589832 | tf_op jit(solution)/shard_map/ppermute | solution.py:104
  39.8 10.0 %collective-permute-start.4 = (bf16[4,64,384]{2,1,0:T(8,128)(2,1)S(1)}, bf16[4,64,384]{2,1,0:T(8,128)(2,1)S(1)}, u32[]{:S(2)}, u32[]{:S(2)}) collective-permute-start(bf16[4,64,384]{2,1,0:T(8,128)(2,1)S(1)} %get-tuple-element.85), channel_id=1, source_target_pairs={{0,8},{4,12},{8,0},{12,4},{16,24},{20,28},{24,16},{28,20},{1,9},{5... | collective-permute-start | bytes 589832 | tf_op jit(solution)/shard_map/ppermute | solution.py:104
  40.0 14.5 %collective-permute-start.8 = (bf16[128,2048]{1,0:T(8,128)(2,1)S(1)}, bf16[128,2048]{1,0:T(8,128)(2,1)S(1)}, u32[]{:S(2)}, u32[]{:S(2)}) collective-permute-start(bf16[128,2048]{1,0:T(8,128)(2,1)S(1)} %collective-permute-done.3.refs_2_.x2), channel_id=1, source_target_pairs={{0,1},{1,0},{2,3},{3,2},{4,5},{5,4},{6,7},{7,6},{8,9},{9,8},{10,11... | collective-permute-start | bytes 1572872 | tf_op jit(solution)/shard_map/ppermute | solution.py:104
  46.0 16.6 %collective-permute-start.10 = (bf16[2,64,1152]{2,1,0:T(8,128)(2,1)S(1)}, bf16[2,64,1152]{2,1,0:T(8,128)(2,1)S(1)}, u32[]{:S(2)}, u32[]{:S(2)}) collective-permute-start(bf16[2,64,1152]{2,1,0:T(8,128)(2,1)S(1)} %get-tuple-element.79), channel_id=1, source_target_pairs={{0,8},{4,12},{8,0},{12,4},{16,24},{20,28},{24,16},{28,20},{1,9},{5... | collective-permute-start | bytes 884744 | tf_op jit(solution)/shard_map/ppermute | solution.py:104
  46.3 16.3 %collective-permute-start.11 = (bf16[2,64,1152]{2,1,0:T(8,128)(2,1)S(1)}, bf16[2,64,1152]{2,1,0:T(8,128)(2,1)S(1)}, u32[]{:S(2)}, u32[]{:S(2)}) collective-permute-start(bf16[2,64,1152]{2,1,0:T(8,128)(2,1)S(1)} %get-tuple-element.79), channel_id=1, source_target_pairs={{0,16},{4,20},{8,24},{12,28},{16,0},{20,4},{24,8},{28,12},{1,17},{... | collective-permute-start | bytes 884744 | tf_op jit(solution)/shard_map/ppermute | solution.py:104
  50.0 4.6 %copy-start.4 = (bf16[1,128,2048]{2,1,0:T(8,128)(2,1)S(1)}, bf16[1,128,2048]{2,1,0:T(8,128)(2,1)}, u32[]{:S(2)}) copy-start(bf16[1,128,2048]{2,1,0:T(8,128)(2,1)} %param.6) | copy-start | bytes 1572868
  50.0 4.6 %copy-start.5 = (s32[8,8]{1,0:T(8,128)S(1)}, s32[8,8]{1,0:T(8,128)}, u32[]{:S(2)}) copy-start(s32[8,8]{1,0:T(8,128)} %adjacency_ref.1) | copy-start | bytes 772
  50.0 4.5 %collective-permute-start.9 = (bf16[4,4,64,384]{3,2,1,0:T(8,128)(2,1)S(1)}, bf16[4,4,64,384]{3,2,1,0:T(8,128)(2,1)S(1)}, u32[]{:S(2)}, u32[]{:S(2)}) collective-permute-start(bf16[4,4,64,384]{3,2,1,0:T(8,128)(2,1)S(1)} %pad_maximum_fusion.1.refs_4_.refs_0_), channel_id=1, source_target_pairs={{0,4},{4,0},{8,12},{12,8},{16,20},{20,16},{24,28},{28,24},{1,5},{5... | collective-permute-start | bytes 2359304 | tf_op jit(solution)/shard_map/ppermute | solution.py:104
  62.6 6.1 %collective-permute-start.15 = (f32[4,4,64,384]{3,2,1,0:T(8,128)S(1)}, f32[4,4,64,384]{3,2,1,0:T(8,128)S(1)}, u32[]{:S(2)}, u32[]{:S(2)}) collective-permute-start(f32[4,4,64,384]{3,2,1,0:T(8,128)S(1)} %shard_map.104), channel_id=1, source_target_pairs={{0,4},{4,0},{8,12},{12,8},{16,20},{20,16},{24,28},{28,24},{1,5},{5... | collective-permute-start | bytes 4718600 | tf_op jit(solution)/shard_map/ppermute | solution.py:104
  62.7 9.4 %collective-permute-start.22 = (bf16[2,64,1152]{2,1,0:T(8,128)(2,1)S(1)}, bf16[2,64,1152]{2,1,0:T(8,128)(2,1)S(1)}, u32[]{:S(2)}, u32[]{:S(2)}) collective-permute-start(bf16[2,64,1152]{2,1,0:T(8,128)(2,1)S(1)} %collective-permute-done.10), channel_id=1, source_target_pairs={{0,16},{4,20},{8,24},{12,28},{16,0},{20,4},{24,8},{28,12},{1,17},{... | collective-permute-start | bytes 884744 | tf_op jit(solution)/shard_map/ppermute | solution.py:104
  64.3 15.4 %collective-permute-start.12 = (bf16[256,640]{1,0:T(8,128)(2,1)S(1)}, bf16[256,640]{1,0:T(8,128)(2,1)S(1)}, u32[]{:S(2)}, u32[]{:S(2)}) collective-permute-start(bf16[256,640]{1,0:T(8,128)(2,1)S(1)} %get-tuple-element.58.d1_ref), channel_id=1, source_target_pairs={{0,1},{1,0},{2,3},{3,2},{4,5},{5,4},{6,7},{7,6},{8,9},{9,8},{10,11... | collective-permute-start | bytes 983048 | tf_op jit(solution)/shard_map/ppermute | solution.py:104
  66.4 23.0 %collective-permute-start.13 = (bf16[256,512]{1,0:T(8,128)(2,1)S(1)}, bf16[256,512]{1,0:T(8,128)(2,1)S(1)}, u32[]{:S(2)}, u32[]{:S(2)}) collective-permute-start(bf16[256,512]{1,0:T(8,128)(2,1)S(1)} %get-tuple-element.59), channel_id=1, source_target_pairs={{0,2},{1,3},{2,0},{3,1},{4,6},{5,7},{6,4},{7,5},{8,10},{9,11},{10,... | collective-permute-start | bytes 786440 | tf_op jit(solution)/shard_map/ppermute | solution.py:104
  69.0 12.1 %collective-permute-start.16 = (f32[4,64,384]{2,1,0:T(8,128)S(1)}, f32[4,64,384]{2,1,0:T(8,128)S(1)}, u32[]{:S(2)}, u32[]{:S(2)}) collective-permute-start(f32[4,64,384]{2,1,0:T(8,128)S(1)} %get-tuple-element.77), channel_id=1, source_target_pairs={{0,8},{4,12},{8,0},{12,4},{16,24},{20,28},{24,16},{28,20},{1,9},{5... | collective-permute-start | bytes 1179656 | tf_op jit(solution)/shard_map/ppermute | solution.py:104
  70.5 18.8 %collective-permute-start.17 = (f32[4,64,384]{2,1,0:T(8,128)S(1)}, f32[4,64,384]{2,1,0:T(8,128)S(1)}, u32[]{:S(2)}, u32[]{:S(2)}) collective-permute-start(f32[4,64,384]{2,1,0:T(8,128)S(1)} %get-tuple-element.76), channel_id=1, source_target_pairs={{0,16},{4,20},{8,24},{12,28},{16,0},{20,4},{24,8},{28,12},{1,17},{... | collective-permute-start | bytes 1179656 | tf_op jit(solution)/shard_map/ppermute | solution.py:104
  72.1 17.2 %collective-permute-start.18 = (f32[4,64,384]{2,1,0:T(8,128)S(1)}, f32[4,64,384]{2,1,0:T(8,128)S(1)}, u32[]{:S(2)}, u32[]{:S(2)}) collective-permute-start(f32[4,64,384]{2,1,0:T(8,128)S(1)} %get-tuple-element.75), channel_id=1, source_target_pairs={{0,24},{4,28},{8,16},{12,20},{16,8},{20,12},{24,0},{28,4},{1,25},{... | collective-permute-start | bytes 1179656 | tf_op jit(solution)/shard_map/ppermute | solution.py:104
  79.7 14.5 %collective-permute-start.23 = (bf16[4,2,64,1152]{3,2,1,0:T(8,128)(2,1)S(1)}, bf16[4,2,64,1152]{3,2,1,0:T(8,128)(2,1)S(1)}, u32[]{:S(2)}, u32[]{:S(2)}) collective-permute-start(bf16[4,2,64,1152]{3,2,1,0:T(8,128)(2,1)S(1)} %pad_maximum_fusion.refs_2_), channel_id=1, source_target_pairs={{0,4},{4,0},{8,12},{12,8},{16,20},{20,16},{24,28},{28,24},{1,5},{5... | collective-permute-start | bytes 3538952 | tf_op jit(solution)/shard_map/ppermute | solution.py:104
  81.1 13.2 %collective-permute-start.14 = (bf16[256,512]{1,0:T(8,128)(2,1)S(1)}, bf16[256,512]{1,0:T(8,128)(2,1)S(1)}, u32[]{:S(2)}, u32[]{:S(2)}) collective-permute-start(bf16[256,512]{1,0:T(8,128)(2,1)S(1)} %pad_maximum_fusion.3), channel_id=1, source_target_pairs={{0,2},{1,3},{2,0},{3,1},{4,6},{5,7},{6,4},{7,5},{8,10},{9,11},{10,... | collective-permute-start | bytes 786440 | tf_op jit(solution)/shard_map/ppermute | solution.py:104
  96.1 16.2 %collective-permute-start.24 = (bf16[128,1024]{1,0:T(8,128)(2,1)S(1)}, bf16[128,1024]{1,0:T(8,128)(2,1)S(1)}, u32[]{:S(2)}, u32[]{:S(2)}) collective-permute-start(bf16[128,1024]{1,0:T(8,128)(2,1)S(1)} %get-tuple-element.70), channel_id=1, source_target_pairs={{0,2},{1,3},{2,0},{3,1},{4,6},{5,7},{6,4},{7,5},{8,10},{9,11},{10,... | collective-permute-start | bytes 786440 | tf_op jit(solution)/shard_map/ppermute | solution.py:104
  96.3 7.7 %collective-permute-start.19 = (bf16[64,384]{1,0:T(8,128)(2,1)S(1)}, bf16[64,384]{1,0:T(8,128)(2,1)S(1)}, u32[]{:S(2)}, u32[]{:S(2)}) collective-permute-start(bf16[64,384]{1,0:T(8,128)(2,1)S(1)} %get-tuple-element.82), channel_id=1, source_target_pairs={{0,1},{1,0},{2,3},{3,2},{4,5},{5,4},{6,7},{7,6},{8,9},{9,8},{10,11... | collective-permute-start | bytes 147464 | tf_op jit(solution)/shard_map/ppermute | solution.py:104
  98.3 14.0 %collective-permute-start.20 = (bf16[64,384]{1,0:T(8,128)(2,1)S(1)}, bf16[64,384]{1,0:T(8,128)(2,1)S(1)}, u32[]{:S(2)}, u32[]{:S(2)}) collective-permute-start(bf16[64,384]{1,0:T(8,128)(2,1)S(1)} %get-tuple-element.81), channel_id=1, source_target_pairs={{0,2},{1,3},{2,0},{3,1},{4,6},{5,7},{6,4},{7,5},{8,10},{9,11},{10,... | collective-permute-start | bytes 147464 | tf_op jit(solution)/shard_map/ppermute | solution.py:104
  99.3 13.0 %collective-permute-start.21 = (bf16[64,384]{1,0:T(8,128)(2,1)S(1)}, bf16[64,384]{1,0:T(8,128)(2,1)S(1)}, u32[]{:S(2)}, u32[]{:S(2)}) collective-permute-start(bf16[64,384]{1,0:T(8,128)(2,1)S(1)} %get-tuple-element.80), channel_id=1, source_target_pairs={{0,3},{1,2},{2,1},{3,0},{4,7},{5,6},{6,5},{7,4},{8,11},{9,10},{10,... | collective-permute-start | bytes 147464 | tf_op jit(solution)/shard_map/ppermute | solution.py:104
